TPU v7x, 32 devices: a whole 2x2x4 slice. The times are simulated.
32 devices in a mesh: section: 2 (over y), dp: 4 (over x, core), tensor: 4 (over z).
Axes of the slice: x: 2, y: 2, z: 4, core: 2. Of those that a mesh axis runs over, the one named last changes fastest.
Arguments:
- inputs: bfloat16 [2, 4, 512, 1536], P(None, 'dp'), may hold values from -6 to 6
- cotangent: bfloat16 [2, 4, 512, 1536], P(None, 'dp'), may hold values from -6 to 6
- lengths: int32 [2, 4], P(None, 'dp'), may hold values from 1 to 512, 1280 in all within a row
- norm_attn: float32 [2, 1536], P('section'), may hold values from 0.1 to 1.9
- w_query: bfloat16 [2, 1536, 1536], P('section', None, 'tensor'), may hold values from -0.15625 to 0.15625
- w_key: bfloat16 [2, 1536, 768], P('section', None, 'tensor'), may hold values from -0.15625 to 0.15625
- w_value: bfloat16 [2, 1536, 768], P('section', None, 'tensor'), may hold values from -0.15625 to 0.15625
- w_out: bfloat16 [2, 1536, 1536], P('section', 'tensor'), may hold values from -0.625 to 0.625
- norm_ffn: float32 [2, 1536], P('section'), may hold values from 0.1 to 1.9
- w_gate: bfloat16 [2, 1536, 4096], P('section', None, 'tensor'), may hold values from -0.15625 to 0.15625
- w_up: bfloat16 [2, 1536, 4096], P('section', None, 'tensor'), may hold values from -0.15625 to 0.15625
- w_down: bfloat16 [2, 4096, 1536], P('section', 'tensor'), may hold values from -0.09375 to 0.09375
Outputs:
- activations: bfloat16 [2, 2, 4, 512, 1536], P('section', None, 'dp')
- input_grads: bfloat16 [2, 2, 4, 512, 1536], P('section', None, 'dp')
- grad_norm_attn: float32 [2, 1536], P('section', 'dp')
- grad_query: float32 [2, 1536, 1536], P('section', 'dp', 'tensor')
- grad_key: float32 [2, 1536, 768], P('section', 'dp', 'tensor')
- grad_value: float32 [2, 1536, 768], P('section', 'dp', 'tensor')
- grad_out: float32 [2, 1536, 1536], P('section', 'tensor', 'dp')
- grad_norm_ffn: float32 [2, 1536], P('section', 'dp')
- grad_gate: float32 [2, 1536, 4096], P('section', 'dp', 'tensor')
- grad_up: float32 [2, 1536, 4096], P('section', 'dp', 'tensor')
- grad_down: float32 [2, 4096, 1536], P('section', 'tensor', 'dp')
Inputs may be any that keep to these rules, and one draw needn't show every extreme that they name: In each micro-batch the lengths sum to 1280 and the longest is exactly 512.
All inputs are finite; a program needn't handle non-finite values.
Results may differ from a plain program's by a relative error of at most 0.035.
Values may be sent and summed in bfloat16 or wider, within the bound.
A program may use at most 192 MiB of HBM per device.

v0:
```python
import jax
import jax.numpy as jnp
from jax import lax
from jax.sharding import PartitionSpec as P

HD = 96


epsilon = 1e-05
rope_base = 100000.0
negative = -1e30


def from_behind(value, axis, steps):
    count = lax.axis_size(axis)
    leading, last = (max(0, -steps), min(count, count - steps))
    return lax.ppermute(value, axis, [(source, source + steps) for source in range(leading, last)])


def tables(seq_len, head_width):
    half_width = head_width // 2
    inverse = rope_base ** (-(jnp.arange(half_width, dtype=jnp.float32) * 2.0 / head_width))
    angle = jnp.arange(seq_len, dtype=jnp.float32)[:, None] * inverse[None, :]
    cosine = jnp.concatenate([jnp.cos(angle), jnp.cos(angle)], axis=-1)
    sine = jnp.concatenate([jnp.sin(angle), jnp.sin(angle)], axis=-1)
    return (cosine[:, None, :], sine[:, None, :])


def rotate(value_in, cosine, sine):
    half_width = value_in.shape[-1] // 2
    turned = jnp.concatenate([-value_in[..., half_width:], value_in[..., :half_width]], axis=-1)
    return value_in * cosine + turned * sine


def unrotate(grad_in, cosine, sine):
    half_width = grad_in.shape[-1] // 2
    scaled = grad_in * sine
    turned = jnp.concatenate([scaled[..., half_width:], -scaled[..., :half_width]], axis=-1)
    return grad_in * cosine + turned


def with_transpose(left, right):
    return lax.dot_general(
        left, right, (((1,), (1,)), ((), ())), preferred_element_type=jnp.float32
    )


def rows_contract(left, right):
    return lax.dot_general(
        left, right, (((0,), (0,)), ((), ())), preferred_element_type=jnp.float32
    )


def attend(queries, key_rows, value_rows):
    seq_len, heads, head_width = queries.shape
    block_rows = min(512, seq_len)
    block_count = seq_len // block_rows
    groups = key_rows.shape[1]
    repeat = heads // groups
    score_scale = head_width ** (-0.5)
    query_blocks = queries.reshape(block_count, block_rows, groups, repeat, head_width)
    key_pos = jnp.arange(seq_len)

    def one_block(inputs):
        query_blk, first_row = inputs
        scores = (
            jnp.einsum("qgrd,kgd->grqk", query_blk, key_rows, preferred_element_type=jnp.float32)
            * score_scale
        )
        row_pos = first_row + jnp.arange(block_rows)
        scores = jnp.where(key_pos[None, :] <= row_pos[:, None], scores, negative)
        row_max = jnp.max(scores, axis=-1, keepdims=True)
        expo = jnp.exp(scores - row_max)
        row_total = jnp.sum(expo, axis=-1, keepdims=True)
        attn_prob = (expo / row_total).astype(jnp.bfloat16)
        output = jnp.einsum(
            "grqk,kgd->qgrd", attn_prob, value_rows, preferred_element_type=jnp.float32
        )
        return (output.astype(jnp.bfloat16), (row_max + jnp.log(row_total))[..., 0])

    output, logsum = lax.map(one_block, (query_blocks, jnp.arange(block_count) * block_rows))
    return (output.reshape(seq_len, heads * head_width), logsum)


def attend_back(queries, key_rows, value_rows, logsum, d_mixed):
    seq_len, heads, head_width = queries.shape
    block_rows = min(512, seq_len)
    block_count = seq_len // block_rows
    groups = key_rows.shape[1]
    repeat = heads // groups
    score_scale = head_width ** (-0.5)
    query_blocks = queries.reshape(block_count, block_rows, groups, repeat, head_width)
    grad_blocks = d_mixed.reshape(block_count, block_rows, groups, repeat, head_width)
    key_pos = jnp.arange(seq_len)

    def one_block(carry, inputs):
        d_keys, d_values = carry
        query_blk, grad_blk, logsum_blk, first_row = inputs
        scores = (
            jnp.einsum("qgrd,kgd->grqk", query_blk, key_rows, preferred_element_type=jnp.float32)
            * score_scale
        )
        row_pos = first_row + jnp.arange(block_rows)
        scores = jnp.where(key_pos[None, :] <= row_pos[:, None], scores, negative)
        attn_prob = jnp.exp(scores - logsum_blk[..., None])
        d_prob = jnp.einsum(
            "qgrd,kgd->grqk", grad_blk, value_rows, preferred_element_type=jnp.float32
        )
        row_dot = jnp.sum(attn_prob * d_prob, axis=-1, keepdims=True)
        d_scores = (attn_prob * (d_prob - row_dot)).astype(jnp.bfloat16)
        d_query_blk = (
            jnp.einsum("grqk,kgd->qgrd", d_scores, key_rows, preferred_element_type=jnp.float32)
            * score_scale
        )
        d_keys = (
            d_keys
            + jnp.einsum("grqk,qgrd->kgd", d_scores, query_blk, preferred_element_type=jnp.float32)
            * score_scale
        )
        d_values = d_values + jnp.einsum(
            "grqk,qgrd->kgd",
            attn_prob.astype(jnp.bfloat16),
            grad_blk,
            preferred_element_type=jnp.float32,
        )
        return ((d_keys, d_values), d_query_blk)

    zero_keys = jnp.zeros(key_rows.shape, jnp.float32)
    (d_keys, d_values), d_query = lax.scan(
        one_block,
        (zero_keys, zero_keys),
        (query_blocks, grad_blocks, logsum, jnp.arange(block_count) * block_rows),
    )
    return (d_query.reshape(seq_len, heads, head_width), d_keys, d_values)


def forward(stream, live_rows, weights):
    norm_one, query_w, key_w, value_w, out_w, norm_two, gate_w, up_w, down_w = weights
    hidden_in = stream.astype(jnp.float32)
    seq_len = hidden_in.shape[0]
    cosine, sine = tables(seq_len, HD)
    scale_one = lax.rsqrt(jnp.mean(hidden_in * hidden_in, axis=-1, keepdims=True) + epsilon)
    unit_one = hidden_in * scale_one
    normed_one = (unit_one * norm_one).astype(jnp.bfloat16)
    query_pre = jnp.dot(normed_one, query_w, preferred_element_type=jnp.float32)
    key_pre = jnp.dot(normed_one, key_w, preferred_element_type=jnp.float32)
    value_pre = jnp.dot(normed_one, value_w, preferred_element_type=jnp.float32)
    queries = rotate(query_pre.reshape(seq_len, -1, HD), cosine, sine).astype(jnp.bfloat16)
    key_rows = rotate(key_pre.reshape(seq_len, -1, HD), cosine, sine).astype(jnp.bfloat16)
    value_rows = value_pre.reshape(seq_len, -1, HD).astype(jnp.bfloat16)
    mixed, logsum = attend(queries, key_rows, value_rows)
    attn_part = jnp.dot(mixed, out_w, preferred_element_type=jnp.float32)
    resid = hidden_in + live_rows * lax.psum(attn_part.astype(jnp.bfloat16), "tensor").astype(
        jnp.float32
    )
    scale_two = lax.rsqrt(jnp.mean(resid * resid, axis=-1, keepdims=True) + epsilon)
    unit_two = resid * scale_two
    normed_two = (unit_two * norm_two).astype(jnp.bfloat16)
    gate_pre = jnp.dot(normed_two, gate_w, preferred_element_type=jnp.float32)
    up_pre = jnp.dot(normed_two, up_w, preferred_element_type=jnp.float32)
    activated = (gate_pre * jax.nn.sigmoid(gate_pre) * up_pre).astype(jnp.bfloat16)
    ffn_part = jnp.dot(activated, down_w, preferred_element_type=jnp.float32)
    result = (
        resid + live_rows * lax.psum(ffn_part.astype(jnp.bfloat16), "tensor").astype(jnp.float32)
    ).astype(jnp.bfloat16)
    kept_vals = (
        scale_one,
        unit_one,
        normed_one,
        queries,
        key_rows,
        value_rows,
        logsum,
        mixed,
        scale_two,
        unit_two,
        normed_two,
        gate_pre,
        up_pre,
        activated,
        live_rows,
    )
    return (result, kept_vals)


def backward(incoming, kept_vals, weights):
    norm_one, query_w, key_w, value_w, out_w, norm_two, gate_w, up_w, down_w = weights
    (
        scale_one,
        unit_one,
        normed_one,
        queries,
        key_rows,
        value_rows,
        logsum,
        mixed,
        scale_two,
        unit_two,
        normed_two,
        gate_pre,
        up_pre,
        activated,
        live_rows,
    ) = kept_vals
    seq_len = queries.shape[0]
    cosine, sine = tables(seq_len, HD)
    grad_in = incoming.astype(jnp.float32)
    d_ffn = (grad_in * live_rows).astype(jnp.bfloat16)
    d_act = with_transpose(d_ffn, down_w)
    sigma = jax.nn.sigmoid(gate_pre)
    d_up = (d_act * gate_pre * sigma).astype(jnp.bfloat16)
    d_gate = (d_act * up_pre * sigma * (1.0 + gate_pre * (1.0 - sigma))).astype(jnp.bfloat16)
    grad_down = rows_contract(activated, d_ffn)
    grad_gate = rows_contract(normed_two, d_gate)
    grad_up = rows_contract(normed_two, d_up)
    partial_two = with_transpose(d_gate, gate_w) + with_transpose(d_up, up_w)
    d_normed_two = lax.psum(partial_two.astype(jnp.bfloat16), "tensor").astype(jnp.float32)
    grad_norm_two = jnp.sum(d_normed_two * unit_two, axis=0)
    inner_two = d_normed_two * norm_two
    d_resid = grad_in + scale_two * (
        inner_two - unit_two * jnp.mean(inner_two * unit_two, axis=-1, keepdims=True)
    )
    d_attn = (d_resid * live_rows).astype(jnp.bfloat16)
    d_mixed = with_transpose(d_attn, out_w).astype(jnp.bfloat16)
    grad_out_w = rows_contract(mixed, d_attn)
    d_query, d_keys, d_values = attend_back(queries, key_rows, value_rows, logsum, d_mixed)
    d_query_pre = unrotate(d_query, cosine, sine).reshape(seq_len, -1).astype(jnp.bfloat16)
    d_key_pre = unrotate(d_keys, cosine, sine).reshape(seq_len, -1).astype(jnp.bfloat16)
    d_value_pre = d_values.reshape(seq_len, -1).astype(jnp.bfloat16)
    grad_query = rows_contract(normed_one, d_query_pre)
    grad_key = rows_contract(normed_one, d_key_pre)
    grad_value = rows_contract(normed_one, d_value_pre)
    partial_one = (
        with_transpose(d_query_pre, query_w)
        + with_transpose(d_key_pre, key_w)
        + with_transpose(d_value_pre, value_w)
    )
    d_normed_one = lax.psum(partial_one.astype(jnp.bfloat16), "tensor").astype(jnp.float32)
    grad_norm_one = jnp.sum(d_normed_one * unit_one, axis=0)
    inner_one = d_normed_one * norm_one
    d_stream = d_resid + scale_one * (
        inner_one - unit_one * jnp.mean(inner_one * unit_one, axis=-1, keepdims=True)
    )
    d_stream = d_stream.astype(jnp.bfloat16)
    return (
        d_stream,
        (
            grad_norm_one,
            grad_query,
            grad_key,
            grad_value,
            grad_out_w,
            grad_norm_two,
            grad_gate,
            grad_up,
            grad_down,
        ),
    )


def on_device(
    inputs,
    cotangent,
    lengths,
    norm_attn,
    w_query,
    w_key,
    w_value,
    w_out,
    norm_ffn,
    w_gate,
    w_up,
    w_down,
):
    section_idx = lax.axis_index("section")
    first_section = section_idx == 0
    micro_count = inputs.shape[0]
    seq_len = inputs.shape[2]
    width_all = inputs.shape[3]
    weights = (
        norm_attn[0],
        w_query[0],
        w_key[0],
        w_value[0],
        w_out[0],
        norm_ffn[0],
        w_gate[0],
        w_up[0],
        w_down[0],
    )
    positions = jnp.arange(seq_len)
    empty_rows = jnp.zeros((seq_len, width_all), jnp.bfloat16)
    arriving = empty_rows
    results = []
    saved_ticks = []
    for tick_num in range(micro_count + 1):
        own_rows = inputs[tick_num, 0] if tick_num < micro_count else empty_rows
        stream = jnp.where(first_section, own_rows, arriving)
        length = jnp.where(
            first_section,
            lengths[min(tick_num, micro_count - 1), 0],
            lengths[max(tick_num - 1, 0), 0],
        )
        live_rows = (positions < length).astype(jnp.float32)[:, None]
        result, kept_vals = forward(stream, live_rows, weights)
        results.append(result)
        saved_ticks.append(kept_vals)
        if tick_num < micro_count:
            arriving = from_behind(result, "section", 1)
    back_arriving = empty_rows
    grads_in = []
    totals = None
    for tick_num in range(micro_count + 1):
        kept_vals = saved_ticks[micro_count - tick_num]
        own_rows = (
            cotangent[micro_count - 1 - tick_num, 0] if tick_num < micro_count else empty_rows
        )
        incoming = jnp.where(first_section, back_arriving, own_rows)
        d_stream, tick_grads = backward(incoming, kept_vals, weights)
        grads_in.append(d_stream)
        totals = (
            tick_grads
            if totals is None
            else tuple((left + right for left, right in zip(totals, tick_grads)))
        )
        if tick_num < micro_count:
            back_arriving = from_behind(d_stream, "section", -1)
    final = (
        lax.psum_scatter(
            totals[0].astype(jnp.bfloat16), "dp", scatter_dimension=0, tiled=True
        ).astype(jnp.float32),
        lax.psum_scatter(
            totals[1].astype(jnp.bfloat16), "dp", scatter_dimension=0, tiled=True
        ).astype(jnp.float32),
        lax.psum_scatter(
            totals[2].astype(jnp.bfloat16), "dp", scatter_dimension=0, tiled=True
        ).astype(jnp.float32),
        lax.psum_scatter(
            totals[3].astype(jnp.bfloat16), "dp", scatter_dimension=0, tiled=True
        ).astype(jnp.float32),
        lax.psum_scatter(
            totals[4].astype(jnp.bfloat16), "dp", scatter_dimension=1, tiled=True
        ).astype(jnp.float32),
        lax.psum_scatter(
            totals[5].astype(jnp.bfloat16), "dp", scatter_dimension=0, tiled=True
        ).astype(jnp.float32),
        lax.psum_scatter(
            totals[6].astype(jnp.bfloat16), "dp", scatter_dimension=0, tiled=True
        ).astype(jnp.float32),
        lax.psum_scatter(
            totals[7].astype(jnp.bfloat16), "dp", scatter_dimension=0, tiled=True
        ).astype(jnp.float32),
        lax.psum_scatter(
            totals[8].astype(jnp.bfloat16), "dp", scatter_dimension=1, tiled=True
        ).astype(jnp.float32),
    )
    acts_out = jnp.stack(
        [
            jnp.where(first_section, results[batch_num], results[batch_num + 1])
            for batch_num in range(micro_count)
        ]
    )
    back_out = jnp.stack(
        [
            jnp.where(
                first_section,
                grads_in[micro_count - batch_num],
                grads_in[micro_count - 1 - batch_num],
            )
            for batch_num in range(micro_count)
        ]
    )
    acts_out = acts_out[None, :, None]
    back_out = back_out[None, :, None]
    return (
        acts_out,
        back_out,
        final[0][None],
        final[1][None],
        final[2][None],
        final[3][None],
        final[4][None],
        final[5][None],
        final[6][None],
        final[7][None],
        final[8][None],
    )


def solution(mesh):
    placed = (
        P(None, "dp", None, None),
        P(None, "dp", None, None),
        P(None, "dp"),
        P("section", None),
        P("section", None, "tensor"),
        P("section", None, "tensor"),
        P("section", None, "tensor"),
        P("section", "tensor", None),
        P("section", None),
        P("section", None, "tensor"),
        P("section", None, "tensor"),
        P("section", "tensor", None),
    )
    return jax.shard_map(
        on_device,
        mesh=mesh,
        in_specs=placed,
        out_specs=(
            P("section", None, "dp", None, None),
            P("section", None, "dp", None, None),
            P("section", "dp"),
            P("section", "dp", "tensor"),
            P("section", "dp", "tensor"),
            P("section", "dp", "tensor"),
            P("section", "tensor", "dp"),
            P("section", "dp"),
            P("section", "dp", "tensor"),
            P("section", "dp", "tensor"),
            P("section", "tensor", "dp"),
        ),
        check_vma=False,
    )
```

profile of v0, /device:TPU:0, one launch (start us, length us, event | category | flops | bytes accessed | tf_op | source)
XLA Modules:
  0.0 1395.7 jit_solution(15916000526074836989)
XLA Ops:
  33.2 68.4 %all-reduce.16.cloned.1.call-done = bf16[512,1536]{1,0:T(8,128)(2,1)} async-done(((bf16[512,1536]{1,0:T(8,128)(2,1)}), bf16[512,1536]{1,0:T(8,128)(2,1)}) %all-reduce.16.cloned.1.call-update) | async-done | bytes 1572880 | tf_op jit(solution)/shard_map/psum | solution.py:153
  116.6 68.3 %all-reduce.18.cloned.1.call-done = bf16[512,1536]{1,0:T(8,128)(2,1)} async-done(((bf16[512,1536]{1,0:T(8,128)(2,1)}), bf16[512,1536]{1,0:T(8,128)(2,1)}) %all-reduce.18.cloned.1.call-update) | async-done | bytes 1572880 | tf_op jit(solution)/shard_map/psum | solution.py:164
  192.3 32.2 %collective-permute-done = bf16[512,1536]{1,0:T(8,128)(2,1)S(1)} collective-permute-done((bf16[512,1536]{1,0:T(8,128)(2,1)S(1)}, bf16[512,1536]{1,0:T(8,128)(2,1)S(1)}, u32[]{:S(2)}, u32[]{:S(2)}) %collective-permute-start) | collective-permute-done | bytes 1572896 | tf_op jit(solution)/shard_map/ppermute | solution.py:17
  237.1 68.7 %all-reduce.20.cloned.1.call-done = bf16[512,1536]{1,0:T(8,128)(2,1)} async-done(((bf16[512,1536]{1,0:T(8,128)(2,1)}), bf16[512,1536]{1,0:T(8,128)(2,1)}) %all-reduce.20.cloned.1.call-update) | async-done | bytes 1572880 | tf_op jit(solution)/shard_map/psum | solution.py:153
  319.6 67.8 %all-reduce.22.cloned.1.call-done = bf16[512,1536]{1,0:T(8,128)(2,1)} async-done(((bf16[512,1536]{1,0:T(8,128)(2,1)}), bf16[512,1536]{1,0:T(8,128)(2,1)}) %all-reduce.22.cloned.1.call-update) | async-done | bytes 1572880 | tf_op jit(solution)/shard_map/psum | solution.py:164
  387.4 5.3 select_bitcast_fusion.1
  395.7 32.4 %collective-permute-done.1 = bf16[512,1536]{1,0:T(8,128)(2,1)S(1)} collective-permute-done((bf16[512,1536]{1,0:T(8,128)(2,1)S(1)}, bf16[512,1536]{1,0:T(8,128)(2,1)S(1)}, u32[]{:S(2)}, u32[]{:S(2)}) %collective-permute-start.1) | collective-permute-done | bytes 1572896 | tf_op jit(solution)/shard_map/ppermute | solution.py:17
  440.5 5.5 fusion.79
  446.0 63.6 %all-reduce.24.cloned.1.call-done = bf16[512,1536]{1,0:T(8,128)(2,1)} async-done(((bf16[512,1536]{1,0:T(8,128)(2,1)}), bf16[512,1536]{1,0:T(8,128)(2,1)}) %all-reduce.24.cloned.1.call-update) | async-done | bytes 1572880 | tf_op jit(solution)/shard_map/psum | solution.py:153
  526.4 67.0 %all-reduce.26.cloned.1.call-done = bf16[512,1536]{1,0:T(8,128)(2,1)} async-done(((bf16[512,1536]{1,0:T(8,128)(2,1)}), bf16[512,1536]{1,0:T(8,128)(2,1)}) %all-reduce.26.cloned.1.call-update) | async-done | bytes 1572880 | tf_op jit(solution)/shard_map/psum | solution.py:217
  614.5 68.7 %all-reduce.28.cloned.1.call-done = bf16[512,1536]{1,0:T(8,128)(2,1)} async-done(((bf16[512,1536]{1,0:T(8,128)(2,1)}), bf16[512,1536]{1,0:T(8,128)(2,1)}) %all-reduce.28.cloned.1.call-update) | async-done | bytes 1572880 | tf_op jit(solution)/shard_map/psum | solution.py:238
  691.3 35.7 %collective-permute-done.2 = bf16[512,1536]{1,0:T(8,128)(2,1)S(1)} collective-permute-done((bf16[512,1536]{1,0:T(8,128)(2,1)S(1)}, bf16[512,1536]{1,0:T(8,128)(2,1)S(1)}, u32[]{:S(2)}, u32[]{:S(2)}) %collective-permute-start.2) | collective-permute-done | bytes 1572896 | tf_op jit(solution)/shard_map/ppermute | solution.py:17
  736.8 67.1 %all-reduce.30.cloned.1.call-done = bf16[512,1536]{1,0:T(8,128)(2,1)} async-done(((bf16[512,1536]{1,0:T(8,128)(2,1)}), bf16[512,1536]{1,0:T(8,128)(2,1)}) %all-reduce.30.cloned.1.call-update) | async-done | bytes 1572880 | tf_op jit(solution)/shard_map/psum | solution.py:217
  825.3 68.3 %all-reduce.32.cloned.1.call-done = bf16[512,1536]{1,0:T(8,128)(2,1)} async-done(((bf16[512,1536]{1,0:T(8,128)(2,1)}), bf16[512,1536]{1,0:T(8,128)(2,1)}) %all-reduce.32.cloned.1.call-update) | async-done | bytes 1572880 | tf_op jit(solution)/shard_map/psum | solution.py:238
  903.5 35.2 %collective-permute-done.3 = bf16[512,1536]{1,0:T(8,128)(2,1)S(1)} collective-permute-done((bf16[512,1536]{1,0:T(8,128)(2,1)S(1)}, bf16[512,1536]{1,0:T(8,128)(2,1)S(1)}, u32[]{:S(2)}, u32[]{:S(2)}) %collective-permute-start.3) | collective-permute-done | bytes 1572896 | tf_op jit(solution)/shard_map/ppermute | solution.py:17
  951.3 64.2 %all-reduce.34.cloned.1.call-done = bf16[512,1536]{1,0:T(8,128)(2,1)} async-done(((bf16[512,1536]{1,0:T(8,128)(2,1)}), bf16[512,1536]{1,0:T(8,128)(2,1)}) %all-reduce.34.cloned.1.call-update) | async-done | bytes 1572880 | tf_op jit(solution)/shard_map/psum | solution.py:217
  1067.6 5.4 fusion.115
  1118.6 22.2 %reduce-scatter.16.cloned.1.call-done = bf16[384,384]{1,0:T(8,128)(2,1)} async-done(((bf16[1536,384]{1,0:T(8,128)(2,1)}), bf16[384,384]{1,0:T(8,128)(2,1)}) %reduce-scatter.16.cloned.1.call-update) | async-done | bytes 294928 | tf_op jit(solution)/shard_map/reduce_scatter | solution.py:332
  1142.6 123.1 %all-reduce.36.cloned.1.call-done = (bf16[512,1536]{1,0:T(8,128)(2,1)}, bf16[512,1536]{1,0:T(8,128)(2,1)}) async-done(((bf16[512,1536]{1,0:T(8,128)(2,1)}, bf16[512,1536]{1,0:T(8,128)(2,1)}), (bf16[512,1536]{1,0:T(8,128)(2,1)}, bf16[512,1536]{1,0:T(8,128)(2,1)})) %all-reduce.36.cloned.1.call-update) | async-done | bytes 3145744 | tf_op jit(solution)/shard_map/psum | solution.py:164
  1268.7 7.0 all-reduce.3
  1277.0 5.7 fusion.149
  1286.6 18.5 %reduce-scatter.28.cloned.1.call-done = bf16[384,1024]{1,0:T(8,128)(2,1)} async-done(((bf16[1536,1024]{1,0:T(8,128)(2,1)}), bf16[384,1024]{1,0:T(8,128)(2,1)}) %reduce-scatter.28.cloned.1.call-update) | async-done | bytes 786448
  1309.7 35.9 %reduce-scatter.18.cloned.1.call-done = bf16[384,1024]{1,0:T(8,128)(2,1)} async-done(((bf16[1536,1024]{1,0:T(8,128)(2,1)}), bf16[384,1024]{1,0:T(8,128)(2,1)}) %reduce-scatter.18.cloned.1.call-update) | async-done | bytes 786448 | tf_op jit(solution)/shard_map/reduce_scatter | solution.py:347
  1348.1 37.9 %reduce-scatter.20.cloned.1.call-done = bf16[384,1024]{1,0:T(8,128)(2,1)} async-done(((bf16[1536,1024]{1,0:T(8,128)(2,1)}), bf16[384,1024]{1,0:T(8,128)(2,1)}) %reduce-scatter.20.cloned.1.call-update) | async-done | bytes 786448 | tf_op jit(solution)/shard_map/reduce_scatter | solution.py:350
  (648 shorter events, 302.1 us)
Async XLA Ops:
  7.2 94.4 %all-reduce.16.cloned.1.call-start = ((), (), s32[]{:S(2)}) async-start(), calls=%async_computation.7 | async-start | bytes 3145728 | tf_op jit(solution)/shard_map/psum | solution.py:153
  29.6 155.3 %all-reduce.18.cloned.1.call-start = ((), (), s32[]{:S(2)}) async-start(), calls=%async_computation.8 | async-start | bytes 3145728 | tf_op jit(solution)/shard_map/psum | solution.py:164
  116.6 189.2 %all-reduce.20.cloned.1.call-start = ((), (), s32[]{:S(2)}) async-start(), calls=%async_computation.9 | async-start | bytes 3145728 | tf_op jit(solution)/shard_map/psum | solution.py:153
  188.4 36.0 %collective-permute-start = (bf16[512,1536]{1,0:T(8,128)(2,1)S(1)}, bf16[512,1536]{1,0:T(8,128)(2,1)S(1)}, u32[]{:S(2)}, u32[]{:S(2)}) collective-permute-start(bf16[512,1536]{1,0:T(8,128)(2,1)S(1)} %add_convert_fusion.5), channel_id=1, source_target_pairs={{0,16},{1,17},{2,18},{3,19},{4,20},{5,21},{6,22},{7,23},{8,24},{9,... | collective-permute-start | bytes 4718600 | tf_op jit(solution)/shard_map/ppermute | solution.py:17
  235.2 152.2 %all-reduce.22.cloned.1.call-start = ((), (), s32[]{:S(2)}) async-start(), calls=%async_computation.10 | async-start | bytes 3145728 | tf_op jit(solution)/shard_map/psum | solution.py:164
  319.1 190.5 %all-reduce.24.cloned.1.call-start = ((), (), s32[]{:S(2)}) async-start(), calls=%async_computation.11 | async-start | bytes 3145728 | tf_op jit(solution)/shard_map/psum | solution.py:153
  392.7 35.4 %collective-permute-start.1 = (bf16[512,1536]{1,0:T(8,128)(2,1)S(1)}, bf16[512,1536]{1,0:T(8,128)(2,1)S(1)}, u32[]{:S(2)}, u32[]{:S(2)}) collective-permute-start(bf16[512,1536]{1,0:T(8,128)(2,1)S(1)} %get-tuple-element.216), channel_id=1, source_target_pairs={{0,16},{1,17},{2,18},{3,19},{4,20},{5,21},{6,22},{7,23},{8,24},{9,... | collective-permute-start | bytes 4718600 | tf_op jit(solution)/shard_map/ppermute | solution.py:17
  439.0 154.4 %all-reduce.26.cloned.1.call-start = ((), (), s32[]{:S(2)}) async-start(), calls=%async_computation.12 | async-start | bytes 3145728 | tf_op jit(solution)/shard_map/psum | solution.py:217
  524.7 158.6 %all-reduce.28.cloned.1.call-start = ((), (), s32[]{:S(2)}) async-start(), calls=%async_computation.13 | async-start | bytes 3145728 | tf_op jit(solution)/shard_map/psum | solution.py:238
  614.4 189.5 %all-reduce.30.cloned.1.call-start = ((), (), s32[]{:S(2)}) async-start(), calls=%async_computation.14 | async-start | bytes 3145728 | tf_op jit(solution)/shard_map/psum | solution.py:217
  689.7 37.3 %collective-permute-start.2 = (bf16[512,1536]{1,0:T(8,128)(2,1)S(1)}, bf16[512,1536]{1,0:T(8,128)(2,1)S(1)}, u32[]{:S(2)}, u32[]{:S(2)}) collective-permute-start(bf16[512,1536]{1,0:T(8,128)(2,1)S(1)} %fusion.52), channel_id=1, source_target_pairs={{16,0},{17,1},{18,2},{19,3},{20,4},{21,5},{22,6},{23,7},{24,8},{25... | collective-permute-start | bytes 4718600 | tf_op jit(solution)/shard_map/ppermute | solution.py:17
  735.3 158.3 %all-reduce.32.cloned.1.call-start = ((), (), s32[]{:S(2)}) async-start(), calls=%async_computation.15 | async-start | bytes 3145728 | tf_op jit(solution)/shard_map/psum | solution.py:238
  825.3 190.3 %all-reduce.34.cloned.1.call-start = ((), (), s32[]{:S(2)}) async-start(), calls=%async_computation.16 | async-start | bytes 3145728 | tf_op jit(solution)/shard_map/psum | solution.py:217
  901.8 36.9 %collective-permute-start.3 = (bf16[512,1536]{1,0:T(8,128)(2,1)S(1)}, bf16[512,1536]{1,0:T(8,128)(2,1)S(1)}, u32[]{:S(2)}, u32[]{:S(2)}) collective-permute-start(bf16[512,1536]{1,0:T(8,128)(2,1)S(1)} %get-tuple-element.214), channel_id=1, source_target_pairs={{16,0},{17,1},{18,2},{19,3},{20,4},{21,5},{22,6},{23,7},{24,8},{25... | collective-permute-start | bytes 4718600 | tf_op jit(solution)/shard_map/ppermute | solution.py:17
  946.9 166.1 %reduce-scatter.22.cloned.1.call-start = ((), (), s32[]{:S(2)}) async-start(), calls=%async_computation.20 | async-start | bytes 983040
  1036.1 78.0 %reduce-scatter.24.cloned.1.call-start = ((), (), s32[]{:S(2)}) async-start(), calls=%async_computation.21 | async-start | bytes 983040
  1047.0 69.6 %reduce-scatter.26.cloned.1.call-start = ((), (), s32[]{:S(2)}) async-start(), calls=%async_computation.22 | async-start | bytes 1474560
  1056.7 84.1 %reduce-scatter.16.cloned.1.call-start = ((), (), s32[]{:S(2)}) async-start(), calls=%async_computation.17 | async-start | bytes 1474560 | tf_op jit(solution)/shard_map/reduce_scatter | solution.py:332
  1067.5 198.2 %all-reduce.36.cloned.1.call-start = ((), (), s32[]{:S(2)}) async-start(), calls=%async_computation.24 | async-start | bytes 6291456 | tf_op jit(solution)/shard_map/psum | solution.py:164
  1077.0 228.1 %reduce-scatter.28.cloned.1.call-start = ((), (), s32[]{:S(2)}) async-start(), calls=%async_computation.23 | async-start | bytes 3932160
  1091.7 253.9 %reduce-scatter.18.cloned.1.call-start = ((), (), s32[]{:S(2)}) async-start(), calls=%async_computation.18 | async-start | bytes 3932160 | tf_op jit(solution)/shard_map/reduce_scatter | solution.py:347
  1101.2 284.8 %reduce-scatter.20.cloned.1.call-start = ((), (), s32[]{:S(2)}) async-start(), calls=%async_computation.19 | async-start | bytes 3932160 | tf_op jit(solution)/shard_map/reduce_scatter | solution.py:350
  1111.0 154.7 %copy-start.183 = (f32[512]{0:T(512)S(1)}, f32[512]{0:T(512)}, u32[]{:S(2)}) copy-start(f32[512]{0:T(512)} %copy-done.179) | copy-start | bytes 6148
  1115.1 153.6 %copy-start.163 = (f32[1536]{0:T(1024)S(1)}, f32[1536]{0:T(1024)}, u32[]{:S(2)}) copy-start(f32[1536]{0:T(1024)} %get-tuple-element.207) | copy-start | bytes 18436
  (208 other events, 1331.4 us)
Sparse Core Ops, SparseCore 0:
  29.7 71.7 all-reduce.15
  116.7 68.1 all-reduce.17
  235.3 70.4 all-reduce.19
  319.3 68.1 all-reduce.21
  439.2 70.4 all-reduce.23
  524.8 68.6 all-reduce.25
  614.5 68.6 all-reduce.27
  735.4 68.4 all-reduce.29
  825.4 68.1 all-reduce.31
  947.0 68.5 all-reduce.33
  1036.2 22.0 reduce-scatter.21
  1060.8 23.2 reduce-scatter.23
  1086.7 25.7 reduce-scatter.25
  1115.1 25.6 reduce-scatter.15
  1144.2 121.4 all-reduce.35
  1268.1 36.9 reduce-scatter.27
  1307.6 37.9 reduce-scatter.17
  1348.0 37.9 reduce-scatter.19
where the time goes:
time: 1400 us
  waiting for transfers between devices  1050 us (75%)
  matrix products  149 us (11%)
  other arithmetic  109 us (8%)
  local copies, waits for them, and re-layouts  52.6 us (4%)
  between operations  19.5 us (1%)
    psum x3, waiting for transfers between devices, forward(): lax.psum(ffn_part.astype(jnp.bfloat16), 'tensor').astype(jnp.float32)  259 us
    psum x3, waiting for transfers between devices, forward(): lax.psum(attn_part.astype(jnp.bfloat16), 'tensor').astype(jnp.float32)  201 us
    psum x3, waiting for transfers between devices, backward(): lax.psum(partial_two.astype(jnp.bfloat16), 'tensor').astype(jnp.float32)  198 us
    psum x2, waiting for transfers between devices, backward(): lax.psum(partial_one.astype(jnp.bfloat16), 'tensor').astype(jnp.float32)  137 us
    ppermute x4, waiting for transfers between devices, from_behind(): lax.ppermute(value, axis, [(source, source + steps) for source in range(l...  136 us
    unnamed x430, local copies, waits for them, and re-layouts  50.1 us
    dot_general x21, matrix products, rows_contract(): lax.dot_general(left, right, (((0,), (0,)), ((), ())), preferred_element_...  49.7 us
    reduce_scatter x1, waiting for transfers between devices, on_device(): lax.psum_scatter(totals[7].astype(jnp.bfloat16), 'dp', scatter_dimension=...  37.9 us
  transfers between devices with their start and end apart: 22, of which 19 were waited for; matrix products, arithmetic and copies ran while one was open for 8% of the time, Pallas kernels for 0%

commit v1 on v0

v1 whole, which is shorter than its diff:
```python
import functools

import jax
import jax.numpy as jnp
from jax import lax
from jax.experimental import pallas as pl
from jax.experimental.pallas import tpu as pltpu
from jax.sharding import PartitionSpec as P

HD = 96

epsilon = 1e-05
rope_base = 100000.0
negative = -1e30
MESH = pl.DeviceIdType.MESH
F32 = jnp.float32
BF16 = jnp.bfloat16


def line_kernel(half, pieces, lag_b, lag_c, normed, shift, *refs):
    if normed:
        part, base, xrow, gain, out, gsum = refs[:6]
        rest = refs[6:]
    else:
        part, base, out = refs[:3]
        rest = refs[3:]
    if shift:
        arrived, rest = rest[0], rest[1:]
    (rin, smid, rmid, s_up, r_up, s_mid, r_mid, s_b1, s_b2, r_b, s_c, r_c) = rest[:12]
    if shift:
        s_s, r_s = rest[12:]
    step_rows = half // pieces
    t = lax.axis_index("tensor")
    section = lax.axis_index("section")
    mid = jnp.logical_or(t == 1, t == 2)
    bar = pltpu.get_barrier_semaphore()

    @pl.when(t > 0)
    def _():
        pl.semaphore_signal(bar, inc=1, device_id={"tensor": jnp.maximum(t - 1, 0)}, device_id_type=MESH)

    @pl.when(t < 3)
    def _():
        pl.semaphore_signal(bar, inc=1, device_id={"tensor": jnp.minimum(t + 1, 3)}, device_id_type=MESH)

    if shift:
        pl.semaphore_signal(bar, inc=1, device_id={"section": 1 - section}, device_id_type=MESH)
    more = 1 if shift else 0

    @pl.when(mid)
    def _():
        pl.semaphore_wait(bar, 2 + more)

    @pl.when(jnp.logical_not(mid))
    def _():
        pl.semaphore_wait(bar, 1 + more)

    sends = section == (0 if shift > 0 else 1)

    def rows(start, p):
        return pl.ds(pl.multiple_of(start + p * step_rows, step_rows), step_rows)

    def remote(src, dst, s_sem, r_sem, where):
        return pltpu.make_async_remote_copy(
            src_ref=src, dst_ref=dst, send_sem=s_sem, recv_sem=r_sem, device_id=where, device_id_type=MESH
        )

    def moved(start, p):
        side = start // half
        return remote(
            out.at[rows(start, p)], arrived.at[rows(start, p)], s_s.at[side, p], r_s.at[side, p], {"section": 1 - section}
        )

    def pass_on(start, p):
        if shift:

            @pl.when(sends)
            def _():
                moved(start, p).start()

    def outcome(src, s_sem, r_sem, where, start, p):
        return remote(out.at[rows(start, p)], out.at[rows(start, p)], s_sem.at[p], r_sem.at[p], where)

    @pl.when(jnp.logical_not(mid))
    def _():
        nbr = {"tensor": jnp.where(t == 0, 1, 2)}
        far = jnp.where(t == 0, half, 0)
        near = half - far
        if normed:
            gsum[...] = jnp.zeros_like(gsum)

        def up(start, p, k):
            return remote(part.at[rows(start, p)], rin.at[rows(start, p)], s_up.at[k, p], r_up.at[k, p], nbr)

        def begin(p, c):
            up(far, p, 0).start()
            up(near, p, 1).start()
            return c

        lax.fori_loop(0, pieces, begin, 0)

        def finish(p, c):
            outcome(None, s_b2, r_b, nbr, near, p).wait_recv()
            pass_on(near, p)
            outcome(None, s_c, r_c, nbr, far, p).wait_recv()
            pass_on(far, p)
            up(far, p, 0).wait_send()
            up(near, p, 1).wait_send()
            return c

        lax.fori_loop(0, pieces, finish, 0)

    @pl.when(mid)
    def _():
        outer = {"tensor": jnp.where(t == 1, 0, 3)}
        other = {"tensor": 3 - t}
        near = (t - 1) * half
        far = half - near
        if normed:
            gsum[...] = jnp.zeros_like(gsum)

        def up(start, p, k):
            return remote(part.at[rows(start, p)], rin.at[rows(start, p)], s_up.at[k, p], r_up.at[k, p], outer)

        def cross(p):
            return remote(smid.at[rows(0, p)], rmid.at[rows(0, p)], s_mid.at[p], r_mid.at[p], other)

        def step(i, c):
            @pl.when(i < pieces)
            def _():
                up(far, i, 0).wait_recv()
                smid[rows(0, i)] = (part[rows(far, i)].astype(F32) + rin[rows(far, i)].astype(F32)).astype(BF16)
                cross(i).start()

            j = i - lag_b

            @pl.when(jnp.logical_and(j >= 0, j < pieces))
            def _():
                up(near, j, 1).wait_recv()
                cross(j).wait_recv()
                here = rows(near, j)
                total = part[here].astype(F32) + rin[here].astype(F32) + rmid[rows(0, j)].astype(F32)
                start_val = base[here].astype(F32)
                if normed:
                    x = xrow[here].astype(F32)
                    scale = lax.rsqrt(jnp.mean(x * x, axis=-1, keepdims=True) + epsilon)
                    unit = x * scale
                    gsum[...] += jnp.sum(total * unit, axis=0, keepdims=True)
                    inner = total * gain[...]
                    total = scale * (inner - unit * jnp.mean(inner * unit, axis=-1, keepdims=True))
                out[here] = (start_val + total).astype(BF16)
                outcome(None, s_b1, r_b, other, near, j).start()
                outcome(None, s_b2, r_b, outer, near, j).start()
                pass_on(near, j)

            k = i - lag_c

            @pl.when(k >= 0)
            def _():
                outcome(None, s_b1, r_b, other, far, k).wait_recv()
                outcome(None, s_c, r_c, outer, far, k).start()
                pass_on(far, k)

            return c

        lax.fori_loop(0, pieces + lag_c, step, 0)

        def finish(p, c):
            cross(p).wait_send()
            outcome(None, s_b1, r_b, other, near, p).wait_send()
            outcome(None, s_b2, r_b, outer, near, p).wait_send()
            outcome(None, s_c, r_c, outer, far, p).wait_send()
            return c

        lax.fori_loop(0, pieces, finish, 0)

    if shift:

        def close(p, c):
            @pl.when(sends)
            def _():
                moved(0, p).wait_send()
                moved(half, p).wait_send()

            @pl.when(jnp.logical_not(sends))
            def _():
                moved(0, p).wait_recv()
                moved(half, p).wait_recv()

            return c

        lax.fori_loop(0, pieces, close, 0)


def line_sum(part, base, cid, xrow=None, gain=None, shift=0, pieces=10):
    count, width = part.shape
    half = count // 2
    normed = xrow is not None
    whole = jax.ShapeDtypeStruct((count, width), BF16)
    outs = [whole]
    args = [part, base]
    if normed:
        outs.append(jax.ShapeDtypeStruct((1, width), F32))
        args += [xrow, gain[None]]
    if shift:
        outs.append(whole)
    dma = pltpu.SemaphoreType.DMA
    scratch = [
        pltpu.VMEM((count, width), BF16),
        pltpu.VMEM((half, width), BF16),
        pltpu.VMEM((half, width), BF16),
        dma((2, pieces)),
        dma((2, pieces)),
    ] + [dma((pieces,))] * 7
    if shift:
        scratch += [dma((2, pieces))] * 2
    vmem = pl.BlockSpec(memory_space=pltpu.VMEM)
    return pl.pallas_call(
        functools.partial(line_kernel, half, pieces, 2, 4, normed, shift),
        out_shape=outs,
        in_specs=[vmem] * len(args),
        out_specs=[vmem] * len(outs),
        scratch_shapes=scratch,
        compiler_params=pltpu.CompilerParams(
            collective_id=cid, has_side_effects=True, vmem_limit_bytes=32 * 2**20
        ),
        name="line_sum_%d" % cid,
    )(*args)


def rope_tables(pos):
    half_width = HD // 2
    inverse = rope_base ** (-(jnp.arange(half_width, dtype=F32) * 2.0 / HD))
    angle = pos.astype(F32)[:, None] * inverse[None, :]
    cosine = jnp.concatenate([jnp.cos(angle), jnp.cos(angle)], axis=-1)
    sine = jnp.concatenate([jnp.sin(angle), jnp.sin(angle)], axis=-1)
    return (cosine[:, None, :], sine[:, None, :])


def rotate(value_in, cosine, sine):
    half_width = value_in.shape[-1] // 2
    turned = jnp.concatenate([-value_in[..., half_width:], value_in[..., :half_width]], axis=-1)
    return value_in * cosine + turned * sine


def unrotate(grad_in, cosine, sine):
    half_width = grad_in.shape[-1] // 2
    scaled = grad_in * sine
    turned = jnp.concatenate([scaled[..., half_width:], -scaled[..., :half_width]], axis=-1)
    return grad_in * cosine + turned


def with_transpose(left, right):
    return lax.dot_general(left, right, (((1,), (1,)), ((), ())), preferred_element_type=F32)


def rows_contract(left, right):
    return lax.dot_general(left, right, (((0,), (0,)), ((), ())), preferred_element_type=F32)


def normalize(rows, gain):
    rows = rows.astype(F32)
    scale = lax.rsqrt(jnp.mean(rows * rows, axis=-1, keepdims=True) + epsilon)
    return (rows * scale * gain).astype(BF16)


def slots_of(lens, count):
    groups = lens.shape[0]
    kept = jnp.minimum(lens, count)
    free, extra = count - kept, lens - kept
    free_off = jnp.cumsum(free) - free
    extra_end = jnp.cumsum(extra)
    slot = jnp.arange(count)
    own = slot[None, :] < kept[:, None]
    index = free_off[:, None] + slot[None, :] - kept[:, None]
    source = jnp.sum(index[:, :, None] >= extra_end[None, None, :], axis=-1)
    begins = jnp.sum(jnp.where(index[:, :, None] >= extra_end[None, None, :], extra[None, None, :], 0), axis=-1)
    seq = jnp.where(own, jnp.arange(groups)[:, None], source)
    pos = jnp.where(own, slot[None, :], count + index - begins)
    return seq, pos, own


def forward(stream, spots, weights, first_id):
    norm_one, query_w, key_w, value_w, out_w, norm_two, gate_w, up_w, down_w = weights
    cosine, sine, allowed = spots
    count = stream.shape[0]
    normed_one = normalize(stream, norm_one)
    query_pre = jnp.dot(normed_one, query_w, preferred_element_type=F32)
    key_pre = jnp.dot(normed_one, key_w, preferred_element_type=F32)
    value_pre = jnp.dot(normed_one, value_w, preferred_element_type=F32)
    queries = rotate(query_pre.reshape(count, -1, HD), cosine, sine).astype(BF16)
    key_rows = rotate(key_pre.reshape(count, -1, HD), cosine, sine).astype(BF16)
    own_keys = jnp.concatenate([key_rows.reshape(count, -1), value_pre.astype(BF16)], axis=1)
    every = lax.all_gather(own_keys, "dp", axis=0, tiled=True)
    width = key_w.shape[1]
    keys_all = every[:, :width].reshape(every.shape[0], -1, HD)
    values_all = every[:, width:].reshape(every.shape[0], -1, HD)
    groups = keys_all.shape[1]
    q = queries.reshape(count, groups, -1, HD)
    scores = jnp.einsum("qgrd,kgd->grqk", q, keys_all, preferred_element_type=F32) * HD ** (-0.5)
    scores = jnp.where(allowed, scores, negative)
    row_max = jnp.max(scores, axis=-1, keepdims=True)
    expo = jnp.exp(scores - row_max)
    row_total = jnp.sum(expo, axis=-1, keepdims=True)
    prob = (expo / row_total).astype(BF16)
    mixed = jnp.einsum("grqk,kgd->qgrd", prob, values_all, preferred_element_type=F32)
    mixed = mixed.astype(BF16).reshape(count, -1)
    logsum = (row_max + jnp.log(row_total))[..., 0]
    attn_part = jnp.dot(mixed, out_w, preferred_element_type=F32)
    resid = line_sum(attn_part.astype(BF16), stream, first_id)[0]
    normed_two = normalize(resid, norm_two)
    gate_pre = jnp.dot(normed_two, gate_w, preferred_element_type=F32)
    up_pre = jnp.dot(normed_two, up_w, preferred_element_type=F32)
    activated = (gate_pre * jax.nn.sigmoid(gate_pre) * up_pre).astype(BF16)
    ffn_part = jnp.dot(activated, down_w, preferred_element_type=F32)
    result, arrived = line_sum(ffn_part.astype(BF16), resid, first_id + 1, shift=1)
    kept = (stream, normed_one, q, keys_all, values_all, logsum, mixed, resid, normed_two, gate_pre, up_pre, activated)
    return result, arrived, kept


def backward(incoming, kept, spots, weights, first_id):
    norm_one, query_w, key_w, value_w, out_w, norm_two, gate_w, up_w, down_w = weights
    stream, normed_one, q, keys_all, values_all, logsum, mixed, resid, normed_two, gate_pre, up_pre, activated = kept
    cosine, sine, allowed = spots
    count = stream.shape[0]
    d_act = with_transpose(incoming, down_w)
    sigma = jax.nn.sigmoid(gate_pre)
    d_up = (d_act * gate_pre * sigma).astype(BF16)
    d_gate = (d_act * up_pre * sigma * (1.0 + gate_pre * (1.0 - sigma))).astype(BF16)
    grad_down = rows_contract(activated, incoming)
    grad_gate = rows_contract(normed_two, d_gate)
    grad_up = rows_contract(normed_two, d_up)
    partial_two = with_transpose(d_gate, gate_w) + with_transpose(d_up, up_w)
    d_resid, grad_norm_two = line_sum(partial_two.astype(BF16), incoming, first_id, xrow=resid, gain=norm_two)
    d_mixed = with_transpose(d_resid, out_w).astype(BF16)
    grad_out = rows_contract(mixed, d_resid)
    dm = d_mixed.reshape(q.shape)
    score_scale = HD ** (-0.5)
    scores = jnp.einsum("qgrd,kgd->grqk", q, keys_all, preferred_element_type=F32) * score_scale
    prob = jnp.exp(jnp.where(allowed, scores, negative) - logsum[..., None])
    d_prob = jnp.einsum("qgrd,kgd->grqk", dm, values_all, preferred_element_type=F32)
    row_dot = jnp.sum(prob * d_prob, axis=-1, keepdims=True)
    d_scores = (prob * (d_prob - row_dot)).astype(BF16)
    d_query = jnp.einsum("grqk,kgd->qgrd", d_scores, keys_all, preferred_element_type=F32) * score_scale
    d_keys = jnp.einsum("grqk,qgrd->kgd", d_scores, q, preferred_element_type=F32) * score_scale
    d_values = jnp.einsum("grqk,qgrd->kgd", prob.astype(BF16), dm, preferred_element_type=F32)
    every = jnp.concatenate([d_keys.reshape(keys_all.shape[0], -1), d_values.reshape(keys_all.shape[0], -1)], axis=1)
    own = lax.psum_scatter(every.astype(BF16), "dp", scatter_dimension=0, tiled=True).astype(F32)
    width = key_w.shape[1]
    d_query_pre = unrotate(d_query.reshape(count, -1, HD), cosine, sine).reshape(count, -1).astype(BF16)
    d_key_pre = unrotate(own[:, :width].reshape(count, -1, HD), cosine, sine).reshape(count, -1).astype(BF16)
    d_value_pre = own[:, width:].astype(BF16)
    grad_query = rows_contract(normed_one, d_query_pre)
    grad_key = rows_contract(normed_one, d_key_pre)
    grad_value = rows_contract(normed_one, d_value_pre)
    partial_one = (
        with_transpose(d_query_pre, query_w)
        + with_transpose(d_key_pre, key_w)
        + with_transpose(d_value_pre, value_w)
    )
    d_stream, grad_norm_one, arrived = line_sum(
        partial_one.astype(BF16), d_resid, first_id + 1, xrow=stream, gain=norm_one, shift=-1
    )
    return (
        d_stream,
        arrived,
        (
            grad_norm_one[0],
            grad_query,
            grad_key,
            grad_value,
            grad_out,
            grad_norm_two[0],
            grad_gate,
            grad_up,
            grad_down,
        ),
    )


def on_device(
    inputs,
    cotangent,
    lengths,
    norm_attn,
    w_query,
    w_key,
    w_value,
    w_out,
    norm_ffn,
    w_gate,
    w_up,
    w_down,
):
    first = lax.axis_index("section") == 0
    me = lax.axis_index("dp")
    groups = lax.axis_size("dp")
    micro, seq_len, width = inputs.shape[0], inputs.shape[2], inputs.shape[3]
    count = seq_len * 5 // 8
    spare = seq_len - count
    weights = tuple(
        item[0] for item in (norm_attn, w_query, w_key, w_value, w_out, norm_ffn, w_gate, w_up, w_down)
    )
    lens = lax.all_gather(lengths[:, 0], "dp", axis=1)

    source = jnp.where(first, inputs[:, 0], cotangent[:, 0])
    packed, slots = [], []
    for b in range(micro):
        seq, pos, own = slots_of(lens[b], count)
        slots.append((seq, pos))
        extra = lax.all_gather(source[b, count:], "dp", axis=0, tiled=True)
        wanted = seq[me] * spare + pos[me] - count
        chosen = jnp.logical_and(jnp.arange(groups * spare)[None, :] == wanted[:, None], ~own[me][:, None])
        brought = jnp.dot(chosen.astype(BF16), extra, preferred_element_type=F32).astype(BF16)
        packed.append(jnp.where(own[me][:, None], source[b, :count], brought))

    def spots_of(b):
        seq, pos = slots[b]
        same = seq[me][:, None] == seq.reshape(-1)[None, :]
        allowed = jnp.logical_and(same, pos.reshape(-1)[None, :] <= pos[me][:, None])
        return rope_tables(pos[me]) + (allowed,)

    spots = [spots_of(b) for b in range(micro)]

    def spots_at(tick):
        early, late = spots[min(tick, micro - 1)], spots[max(tick - 1, 0)]
        return tuple(jnp.where(first, a, b) for a, b in zip(early, late))

    empty = jnp.zeros((count, width), BF16)
    arriving = empty
    results, saved = [], []
    for tick in range(micro + 1):
        stream = jnp.where(first, packed[tick] if tick < micro else empty, arriving)
        result, arriving, kept = forward(stream, spots_at(tick), weights, 0)
        results.append(result)
        saved.append(kept)
    arriving = empty
    grads_in, totals = [], None
    for tick in range(micro + 1):
        incoming = jnp.where(first, arriving, packed[micro - 1 - tick] if tick < micro else empty)
        d_stream, arriving, grads = backward(incoming, saved[micro - tick], spots_at(micro - tick), weights, 2)
        grads_in.append(d_stream)
        totals = grads if totals is None else tuple(a + b for a, b in zip(totals, grads))

    def scattered(value, dim):
        return lax.psum_scatter(value.astype(BF16), "dp", scatter_dimension=dim, tiled=True).astype(F32)

    gains = lax.psum(jnp.stack([totals[0], totals[5]]), ("tensor", "dp"))
    part = width // groups
    gains = lax.dynamic_slice_in_dim(gains, me * part, part, axis=1)
    final = (
        gains[0],
        scattered(totals[1], 0),
        scattered(totals[2], 0),
        scattered(totals[3], 0),
        scattered(totals[4], 1),
        gains[1],
        scattered(totals[6], 0),
        scattered(totals[7], 0),
        scattered(totals[8], 1),
    )

    def unpack(rows, b, through):
        seq, pos = slots[b]
        everything = lax.all_gather(rows, "dp", axis=0, tiled=True)
        wanted = count + jnp.arange(spare)
        chosen = jnp.logical_and(seq.reshape(-1)[None, :] == me, pos.reshape(-1)[None, :] == wanted[:, None])
        back = jnp.dot(chosen.astype(BF16), everything, preferred_element_type=F32).astype(BF16)
        live = (jnp.arange(seq_len) < lens[b, me])[:, None]
        return jnp.where(live, jnp.concatenate([rows, back], axis=0), through)

    acts = jnp.stack(
        [unpack(jnp.where(first, results[b], results[b + 1]), b, inputs[b, 0]) for b in range(micro)]
    )
    back = jnp.stack(
        [
            unpack(jnp.where(first, grads_in[micro - b], grads_in[micro - 1 - b]), b, cotangent[b, 0])
            for b in range(micro)
        ]
    )
    return (acts[None, :, None], back[None, :, None]) + tuple(item[None] for item in final)


def solution(mesh):
    placed = (
        P(None, "dp", None, None),
        P(None, "dp", None, None),
        P(None, "dp"),
        P("section", None),
        P("section", None, "tensor"),
        P("section", None, "tensor"),
        P("section", None, "tensor"),
        P("section", "tensor", None),
        P("section", None),
        P("section", None, "tensor"),
        P("section", None, "tensor"),
        P("section", "tensor", None),
    )
    return jax.shard_map(
        on_device,
        mesh=mesh,
        in_specs=placed,
        out_specs=(
            P("section", None, "dp", None, None),
            P("section", None, "dp", None, None),
            P("section", "dp"),
            P("section", "dp", "tensor"),
            P("section", "dp", "tensor"),
            P("section", "dp", "tensor"),
            P("section", "tensor", "dp"),
            P("section", "dp"),
            P("section", "dp", "tensor"),
            P("section", "dp", "tensor"),
            P("section", "tensor", "dp"),
        ),
        check_vma=False,
    )
```

time: 1400 us -> 1120 us (0.80)
  waiting for transfers between devices: 1050 us -> 198 us
  Pallas kernels: 0 us -> 429 us
  blocking collectives: 7.01 us -> 98.4 us
  local copies, waits for them, and re-layouts: 52.6 us -> 101 us
  matrix products: 149 us -> 186 us
  other arithmetic: 109 us -> 74 us
    psum x11 -> x0, waiting for transfers between devices: 795 us -> none  [the longest x3 259 us: forward(): lax.psum(ffn_part.astype(jnp.bfloat16), 'tensor').astype(jnp.float32)]
    pallas_call x0 -> x12, Pallas kernels: none -> 429 us  [line_sum(): pl.pallas_call(functools.partial(line_kernel, half, pieces, 2, 4, normed,...]
    ppermute x4 -> x0, waiting for transfers between devices: 136 us -> none  [from_behind(): lax.ppermute(value, axis, [(source, source + steps) for source in range(l...]
    all_gather x0 -> x6, waiting for transfers between devices: none -> 70 us  [the longest x4 62.5 us: unpack(): everything = lax.all_gather(rows, 'dp', axis=0, tiled=True)]
    psum x0 -> x1, blocking collectives: none -> 58.1 us  [on_device(): gains = lax.psum(jnp.stack([totals[0], totals[5]]), ('tensor', 'dp'))]
    dot_general x39 -> x45, matrix products: 62 us -> 104 us  [the longest x4 15.8 us: unpack(): jnp.dot(chosen.astype(BF16), everything, preferred_element_type=F32)]
    all_gather x0 -> x4, blocking collectives: none -> 40.3 us  [the longest x3 34.4 us: forward(): every = lax.all_gather(own_keys, 'dp', axis=0, tiled=True)]
    unnamed x22 -> x23, waiting for transfers between devices: 18.8 us -> 53.2 us
  transfers between devices with their start and end apart: 22 -> 16, of which waited for: 19 -> 8; matrix products, arithmetic and copies ran while one was open for 8% -> 16% of each run, Pallas kernels for 0% -> 13%
where the time goes in v1:
time: 1120 us; the launch traced here: 1110 us
  Pallas kernels  429 us (38%)
  waiting for transfers between devices  198 us (18%)
  matrix products  186 us (17%)
  local copies, waits for them, and re-layouts  101 us (9%)
  blocking collectives  98.4 us (9%)
  other arithmetic  74 us (7%)
  between operations  17.2 us (2%)
    pallas_call x12, Pallas kernels, line_sum(): pl.pallas_call(functools.partial(line_kernel, half, pieces, 2, 4, normed,...  429 us
    reduce_scatter x3, waiting for transfers between devices, scattered(): lax.psum_scatter(value.astype(BF16), 'dp', scatter_dimension=dim, tiled=T...  75.1 us
    unnamed x394, local copies, waits for them, and re-layouts  66.7 us
    all_gather x4, waiting for transfers between devices, unpack(): everything = lax.all_gather(rows, 'dp', axis=0, tiled=True)  62.5 us
    psum x1, blocking collectives, on_device(): gains = lax.psum(jnp.stack([totals[0], totals[5]]), ('tensor', 'dp'))  58.1 us
    dot_general x21, matrix products, rows_contract(): lax.dot_general(left, right, (((0,), (0,)), ((), ())), preferred_element_...  55.1 us
    unnamed x23, waiting for transfers between devices  53.2 us
    all_gather x3, blocking collectives, forward(): every = lax.all_gather(own_keys, 'dp', axis=0, tiled=True)  34.4 us
  transfers between devices with their start and end apart: 16, of which 8 were waited for; matrix products, arithmetic and copies ran while one was open for 16% of the time, Pallas kernels for 13%

profile of v1, /device:TPU:0, one launch (start us, length us, event | category | flops | bytes accessed | tf_op | source)
XLA Modules:
  0.0 1105.8 jit_solution(7194459901779440387)
XLA Ops:
  32.8 7.5 all-gather.18.cloned.1.call-done
  50.6 15.6 %all_gather.32 = bf16[1280,384]{1,0:T(8,128)(2,1)S(1)} all-gather(bf16[320,384]{1,0:T(8,128)(2,1)} %copy.67), channel_id=1, replica_groups=mesh['section'=2,'dp'=4,'tensor'=4] {'dp'}, dimensions={0}, use_global_device_ids=true | all-gather | bytes 1228800 | tf_op jit(solution)/shard_map/all_gather | solution.py:294
  87.5 35.2 %line_sum_0.3.refs_1_.refs_2_ = bf16[320,1536]{1,0:T(8,128)(2,1)S(1)} custom-call(bf16[320,1536]{1,0:T(8,128)(2,1)S(1)} %convolution_convert_fusion.3.refs_0_, bf16[320,1536]{1,0:T(8,128)(2,1)S(1)} %copy-done.17), custom_call_target="tpu_custom_call" | custom-call | tf_op jit(solution)/shard_map/line_sum_0/pallas_call | solution.py:218
  128.7 37.4 %line_sum_1.3 = (bf16[320,1536]{1,0:T(8,128)(2,1)S(1)}, bf16[320,1536]{1,0:T(8,128)(2,1)S(1)}) custom-call(bf16[320,1536]{1,0:T(8,128)(2,1)S(1)} %fusion.84.refs_0_, bf16[320,1536]{1,0:T(8,128)(2,1)S(1)} %line_sum_0.3.refs_1_.refs_2_), custom_call_target="tpu_custom_call" | custom-call | tf_op jit(solution)/shard_map/line_sum_1/pallas_call | solution.py:218
  179.1 8.9 all_gather.34
  203.6 33.8 %line_sum_0.4.refs_1_.refs_2_ = bf16[320,1536]{1,0:T(8,128)(2,1)S(1)} custom-call(bf16[320,1536]{1,0:T(8,128)(2,1)S(1)} %convolution_convert_fusion.1.refs_0_, bf16[320,1536]{1,0:T(8,128)(2,1)S(1)} %copy-done.22), custom_call_target="tpu_custom_call" | custom-call | tf_op jit(solution)/shard_map/line_sum_0/pallas_call | solution.py:218
  243.4 38.8 %line_sum_1.4 = (bf16[320,1536]{1,0:T(8,128)(2,1)S(1)}, bf16[320,1536]{1,0:T(8,128)(2,1)S(1)}) custom-call(bf16[320,1536]{1,0:T(8,128)(2,1)S(1)} %fusion.87.refs_0_, bf16[320,1536]{1,0:T(8,128)(2,1)S(1)} %line_sum_0.4.refs_1_.refs_2_), custom_call_target="tpu_custom_call" | custom-call | tf_op jit(solution)/shard_map/line_sum_1/pallas_call | solution.py:218
  289.5 9.8 all_gather.36
  314.9 34.0 %line_sum_0.5.refs_1_.refs_2_ = bf16[320,1536]{1,0:T(8,128)(2,1)S(1)} custom-call(bf16[320,1536]{1,0:T(8,128)(2,1)S(1)} %convolution_convert_fusion.refs_0_, bf16[320,1536]{1,0:T(8,128)(2,1)S(1)} %copy-done.12), custom_call_target="tpu_custom_call" | custom-call | tf_op jit(solution)/shard_map/line_sum_0/pallas_call | solution.py:218
  358.9 32.8 %line_sum_2.3 = (bf16[320,1536]{1,0:T(8,128)(2,1)S(1)}, f32[1,1536]{1,0:T(1,128)S(1)}) custom-call(bf16[320,1536]{1,0:T(8,128)(2,1)S(1)} %fusion.81.refs_0_, bf16[320,1536]{1,0:T(8,128)(2,1)S(1)} %broadcast_select_fusion.4.refs_1_, bf16[320,1536]{1,0:T(8,128)(2,1)S(1)} %line_sum_0.5.refs_1_.refs_2_, f32[1,1536]{1,0:T(1,128)S(1)} %copy-done.46), custom_call_target="tpu_custom_call" | custom-call | tf_op jit(solution)/shard_map/line_sum_2/pallas_call | solution.py:218
  419.0 17.6 %reduce-scatter.31.cloned.1.call-done = bf16[320,384]{1,0:T(8,128)(2,1)} async-done(((bf16[1280,384]{1,0:T(8,128)(2,1)}), bf16[320,384]{1,0:T(8,128)(2,1)}) %reduce-scatter.31.cloned.1.call-update) | async-done | bytes 245776
  445.3 40.6 %line_sum_3.3 = (bf16[320,1536]{1,0:T(8,128)(2,1)S(1)}, f32[1,1536]{1,0:T(1,128)S(1)}, bf16[320,1536]{1,0:T(8,128)(2,1)S(1)}) custom-call(bf16[320,1536]{1,0:T(8,128)(2,1)S(1)} %fusion.93.refs_0_, bf16[320,1536]{1,0:T(8,128)(2,1)S(1)} %copy-done.34, bf16[320,1536]{1,0:T(8,128)(2,1)S(1)} %copy-done.13, f32[1,1536]{1,0:T(1,128)S(1)} %copy-done.47), custom_call_target="tpu_custom_call" | custom-call | tf_op jit(solution)/shard_map/line_sum_3/pallas_call | solution.py:218
  493.1 32.1 %line_sum_2.4 = (bf16[320,1536]{1,0:T(8,128)(2,1)S(1)}, f32[1,1536]{1,0:T(1,128)S(1)}) custom-call(bf16[320,1536]{1,0:T(8,128)(2,1)S(1)} %fusion.78.refs_0_, bf16[320,1536]{1,0:T(8,128)(2,1)S(1)} %broadcast_select_fusion.3.refs_1_, bf16[320,1536]{1,0:T(8,128)(2,1)S(1)} %copy-done.2, f32[1,1536]{1,0:T(1,128)S(1)} %copy-done.46), custom_call_target="tpu_custom_call" | custom-call | tf_op jit(solution)/shard_map/line_sum_2/pallas_call | solution.py:218
  552.3 15.5 %reduce-scatter.33.cloned.1.call-done = bf16[320,384]{1,0:T(8,128)(2,1)} async-done(((bf16[1280,384]{1,0:T(8,128)(2,1)}), bf16[320,384]{1,0:T(8,128)(2,1)}) %reduce-scatter.33.cloned.1.call-update) | async-done | bytes 245776
  576.4 40.6 %line_sum_3.4 = (bf16[320,1536]{1,0:T(8,128)(2,1)S(1)}, f32[1,1536]{1,0:T(1,128)S(1)}, bf16[320,1536]{1,0:T(8,128)(2,1)S(1)}) custom-call(bf16[320,1536]{1,0:T(8,128)(2,1)S(1)} %fusion.94.refs_0_, bf16[320,1536]{1,0:T(8,128)(2,1)S(1)} %copy-done.36, bf16[320,1536]{1,0:T(8,128)(2,1)S(1)} %copy-done.23, f32[1,1536]{1,0:T(1,128)S(1)} %copy-done.47), custom_call_target="tpu_custom_call" | custom-call | tf_op jit(solution)/shard_map/line_sum_3/pallas_call | solution.py:218
  622.3 32.1 %line_sum_2.5 = (bf16[320,1536]{1,0:T(8,128)(2,1)S(1)}, f32[1,1536]{1,0:T(1,128)S(1)}) custom-call(bf16[320,1536]{1,0:T(8,128)(2,1)S(1)} %fusion.75.refs_0_, bf16[320,1536]{1,0:T(8,128)(2,1)S(1)} %broadcast_select_fusion.2.refs_1_, bf16[320,1536]{1,0:T(8,128)(2,1)S(1)} %copy-done.8, f32[1,1536]{1,0:T(1,128)S(1)} %copy-done.46), custom_call_target="tpu_custom_call" | custom-call | tf_op jit(solution)/shard_map/line_sum_2/pallas_call | solution.py:218
  678.1 35.2 %line_sum_1.5 = (bf16[320,1536]{1,0:T(8,128)(2,1)S(1)}, bf16[320,1536]{1,0:T(8,128)(2,1)}) custom-call(bf16[320,1536]{1,0:T(8,128)(2,1)S(1)} %fusion.90.refs_0_, bf16[320,1536]{1,0:T(8,128)(2,1)S(1)} %copy-done.6), custom_call_target="tpu_custom_call" | custom-call | tf_op jit(solution)/shard_map/line_sum_1/pallas_call | solution.py:218
  800.1 36.7 %line_sum_3.5 = (bf16[320,1536]{1,0:T(8,128)(2,1)S(1)}, f32[1,1536]{1,0:T(1,128)S(1)}, bf16[320,1536]{1,0:T(8,128)(2,1)}) custom-call(bf16[320,1536]{1,0:T(8,128)(2,1)S(1)} %fusion.95.refs_0_, bf16[320,1536]{1,0:T(8,128)(2,1)S(1)} %copy-done.32, bf16[320,1536]{1,0:T(8,128)(2,1)S(1)} %copy-done.20, f32[1,1536]{1,0:T(1,128)S(1)} %copy-done.47), custom_call_target="tpu_custom_call" | custom-call | tf_op jit(solution)/shard_map/line_sum_3/pallas_call | solution.py:218
  841.0 58.1 %psum.7 = f32[2,1536]{1,0:T(2,128)S(1)} all-reduce(f32[2,1536]{1,0:T(2,128)S(1)} %pad_maximum_fusion.16), channel_id=1, replica_groups=mesh['section'=2,'dp'=4,'tensor'=4] {'tensor','dp'}, use_global_device_ids=true, to_apply=%region_26.27 | all-reduce | flops 3072 | bytes 24576 | tf_op jit(solution)/shard_map/psum | solution.py:448
  916.0 18.0 %reduce-scatter.43.cloned.1.call-done = bf16[384,1024]{1,0:T(8,128)(2,1)} async-done(((bf16[1536,1024]{1,0:T(8,128)(2,1)}), bf16[384,1024]{1,0:T(8,128)(2,1)}) %reduce-scatter.43.cloned.1.call-update) | async-done | bytes 786448
  938.6 36.4 %reduce-scatter.29.cloned.1.call-done = bf16[384,1024]{1,0:T(8,128)(2,1)} async-done(((bf16[1536,1024]{1,0:T(8,128)(2,1)}), bf16[384,1024]{1,0:T(8,128)(2,1)}) %reduce-scatter.29.cloned.1.call-update) | async-done | bytes 786448 | tf_op jit(solution)/shard_map/reduce_scatter | solution.py:446
  977.5 38.7 %reduce-scatter.27.cloned.1.call-done = bf16[384,1024]{1,0:T(8,128)(2,1)} async-done(((bf16[1536,1024]{1,0:T(8,128)(2,1)}), bf16[384,1024]{1,0:T(8,128)(2,1)}) %reduce-scatter.27.cloned.1.call-update) | async-done | bytes 786448 | tf_op jit(solution)/shard_map/reduce_scatter | solution.py:446
  1018.7 32.0 %all-gather.14.cloned.1.call-done = bf16[1280,1536]{1,0:T(8,128)(2,1)} async-done(((bf16[320,1536]{1,0:T(8,128)(2,1)}), bf16[1280,1536]{1,0:T(8,128)(2,1)}) %all-gather.14.cloned.1.call-update) | async-done | bytes 3932176 | tf_op jit(solution)/shard_map/all_gather | solution.py:465
  1054.6 30.5 %all-gather.16.cloned.1.call-done = bf16[1280,1536]{1,0:T(8,128)(2,1)} async-done(((bf16[320,1536]{1,0:T(8,128)(2,1)}), bf16[1280,1536]{1,0:T(8,128)(2,1)}) %all-gather.16.cloned.1.call-update) | async-done | bytes 3932176 | tf_op jit(solution)/shard_map/all_gather | solution.py:465
  (672 shorter events, 370.7 us)
Async XLA Ops:
  7.2 117.1 %copy-start = (bf16[1,1536,1024]{2,1,0:T(8,128)(2,1)S(1)}, bf16[1,1536,1024]{2,1,0:T(8,128)(2,1)}, u32[]{:S(2)}) copy-start(bf16[1,1536,1024]{2,1,0:T(8,128)(2,1)} %param.22) | copy-start | bytes 9437188
  7.2 33.1 %all-gather.18.cloned.1.call-start = ((), (), s32[]{:S(2)}) async-start(), calls=%async_computation.17 | async-start | bytes 2949120 | tf_op jit(solution)/shard_map/all_gather | solution.py:411
  13.3 154.7 %all-gather.20.cloned.1.call-start = ((), (), s32[]{:S(2)}) async-start(), calls=%async_computation.18 | async-start | bytes 2949120 | tf_op jit(solution)/shard_map/all_gather | solution.py:411
  14.1 422.5 %reduce-scatter.31.cloned.1.call-start = ((), (), s32[]{:S(2)}) async-start(), calls=%async_computation.19 | async-start | bytes 1228800
  28.7 40.9 %copy-start.81 = (f32[320,96]{0,1:T(8,128)}, f32[320,96]{0,1:T(8,128)S(1)}, u32[]{:S(2)}) copy-start(f32[320,96]{0,1:T(8,128)S(1)} %get-tuple-element.168) | copy-start | bytes 368644
  411.4 156.3 %reduce-scatter.33.cloned.1.call-start = ((), (), s32[]{:S(2)}) async-start(), calls=%async_computation.20 | async-start | bytes 1228800
  443.8 42.3 %copy-start.182 = (f32[320,1024]{1,0:T(8,128)S(1)}, f32[320,1024]{1,0:T(8,128)}, u32[]{:S(2)}) copy-start(f32[320,1024]{1,0:T(8,128)} %get-tuple-element.215) | copy-start | bytes 3932164
  445.3 40.8 %copy-start.174 = (bf16[1,1024,1536]{2,1,0:T(8,128)(2,1)S(1)}, bf16[1,1024,1536]{2,1,0:T(8,128)(2,1)}, u32[]{:S(2)}) copy-start(bf16[1,1024,1536]{2,1,0:T(8,128)(2,1)} %param.23) | copy-start | bytes 9437188
  544.9 199.4 %reduce-scatter.35.cloned.1.call-start = ((), (), s32[]{:S(2)}) async-start(), calls=%async_computation.21 | async-start | bytes 1228800
  574.9 42.2 %copy-start.181 = (f32[320,1024]{1,0:T(8,128)S(1)}, f32[320,1024]{1,0:T(8,128)}, u32[]{:S(2)}) copy-start(f32[320,1024]{1,0:T(8,128)} %get-tuple-element.210) | copy-start | bytes 3932164
  576.4 40.8 %copy-start.178 = (f32[320,1024]{1,0:T(8,128)S(1)}, f32[320,1024]{1,0:T(8,128)}, u32[]{:S(2)}) copy-start(f32[320,1024]{1,0:T(8,128)} %copy-done.177) | copy-start | bytes 3932164
  674.2 225.5 %all-gather.12.cloned.1.call-start = ((), (), s32[]{:S(2)}) async-start(), calls=%async_computation.11 | async-start | bytes 4915200 | tf_op jit(solution)/shard_map/all_gather | solution.py:465
  714.9 189.3 %all-gather.10.cloned.1.call-start = ((), (), s32[]{:S(2)}) async-start(), calls=%async_computation.10 | async-start | bytes 4915200 | tf_op jit(solution)/shard_map/all_gather | solution.py:465
  715.6 192.8 %reduce-scatter.41.cloned.1.call-start = ((), (), s32[]{:S(2)}) async-start(), calls=%async_computation.24 | async-start | bytes 1474560
  723.4 187.1 %reduce-scatter.25.cloned.1.call-start = ((), (), s32[]{:S(2)}) async-start(), calls=%async_computation.14 | async-start | bytes 1474560 | tf_op jit(solution)/shard_map/reduce_scatter | solution.py:446
  734.3 178.0 %reduce-scatter.39.cloned.1.call-start = ((), (), s32[]{:S(2)}) async-start(), calls=%async_computation.23 | async-start | bytes 983040
  749.6 163.7 %reduce-scatter.37.cloned.1.call-start = ((), (), s32[]{:S(2)}) async-start(), calls=%async_computation.22 | async-start | bytes 983040
  761.4 172.6 %reduce-scatter.43.cloned.1.call-start = ((), (), s32[]{:S(2)}) async-start(), calls=%async_computation.25 | async-start | bytes 3932160
  776.3 198.8 %reduce-scatter.29.cloned.1.call-start = ((), (), s32[]{:S(2)}) async-start(), calls=%async_computation.16 | async-start | bytes 3932160 | tf_op jit(solution)/shard_map/reduce_scatter | solution.py:446
  785.7 230.6 %reduce-scatter.27.cloned.1.call-start = ((), (), s32[]{:S(2)}) async-start(), calls=%async_computation.15 | async-start | bytes 3932160 | tf_op jit(solution)/shard_map/reduce_scatter | solution.py:446
  795.2 255.4 %all-gather.14.cloned.1.call-start = ((), (), s32[]{:S(2)}) async-start(), calls=%async_computation.12 | async-start | bytes 4915200 | tf_op jit(solution)/shard_map/all_gather | solution.py:465
  838.3 61.4 %copy-start.148 = (s32[1280]{0:T(1024)S(1)}, s32[1280]{0:T(1024)}, u32[]{:S(2)}) copy-start(s32[1280]{0:T(1024)} %copy-done.147) | copy-start | bytes 15364
  838.3 61.4 %copy-start.159 = (pred[1280]{0:T(1024)(128)(4,1)S(1)}, pred[1280]{0:T(1024)(128)(4,1)}, u32[]{:S(2)}) copy-start(pred[1280]{0:T(1024)(128)(4,1)} %get-tuple-element.104) | copy-start | bytes 3844
  838.4 246.7 %all-gather.16.cloned.1.call-start = ((), (), s32[]{:S(2)}) async-start(), calls=%async_computation.13 | async-start | bytes 4915200 | tf_op jit(solution)/shard_map/all_gather | solution.py:465
  (181 other events, 1008.2 us)
Sparse Core Ops, SparseCore 0:
  13.5 26.8 all-gather.17
  42.5 29.3 all-gather.19
  411.6 24.9 reduce-scatter.30
  545.1 22.6 reduce-scatter.32
  674.3 22.6 reduce-scatter.34
  715.0 33.2 all-gather.11
  749.9 32.9 all-gather.9
  785.7 25.7 reduce-scatter.40
  814.6 25.7 reduce-scatter.24
  843.5 23.4 reduce-scatter.38
  870.1 23.3 reduce-scatter.36
  896.0 37.9 reduce-scatter.42
  937.1 37.9 reduce-scatter.28
  978.2 37.9 reduce-scatter.26
  1017.6 32.9 all-gather.13
  1052.1 32.9 all-gather.15

commit v2 on v1

v2 whole, which is shorter than its diff:
```python
import functools

import jax
import jax.numpy as jnp
from jax import lax
from jax.experimental import pallas as pl
from jax.experimental.pallas import tpu as pltpu
from jax.sharding import PartitionSpec as P

HD = 96

epsilon = 1e-05
rope_base = 100000.0
negative = -1e30
MESH = pl.DeviceIdType.MESH
F32 = jnp.float32
BF16 = jnp.bfloat16


def remote(src, dst, s_sem, r_sem, where):
    return pltpu.make_async_remote_copy(
        src_ref=src, dst_ref=dst, send_sem=s_sem, recv_sem=r_sem, device_id=where, device_id_type=MESH
    )


def greet(where):
    pl.semaphore_signal(pltpu.get_barrier_semaphore(), inc=1, device_id=where, device_id_type=MESH)


def dp_bits(groups):
    return groups.bit_length() - 1


def dp_partner(level):
    me = lax.axis_index("dp")
    bit = lax.rem(me // (1 << level), 2)
    return {"dp": me + (1 - 2 * bit) * (1 << level)}, bit


class Scatter:
    def __init__(self, groups, rows, chunks, refs):
        self.levels = dp_bits(groups)
        self.groups, self.rows, self.chunks, self.size = groups, rows, chunks, rows // chunks
        self.value, self.out = refs[0], refs[1]
        m = self.levels
        self.arrive = refs[2 : 2 + m]
        self.held = refs[2 + m : 1 + 2 * m]
        self.s_sem = refs[1 + 2 * m : 1 + 3 * m]
        self.r_sem = refs[1 + 3 * m : 1 + 4 * m]
        self.links = [dp_partner(k) for k in range(m)]

    @staticmethod
    def scratch(groups, rows, width, chunks, dtype):
        m = dp_bits(groups)
        sizes = [groups >> (k + 1) for k in range(m)]
        return (
            [pltpu.VMEM((size * rows, width), dtype) for size in sizes]
            + [pltpu.VMEM((size * rows, width), dtype) for size in sizes[:-1]]
            + [pltpu.SemaphoreType.DMA((size, chunks)) for size in sizes] * 2
        )

    def at(self, block, c):
        return pl.ds(pl.multiple_of(block * self.rows + c * self.size, self.size), self.size)

    def copy(self, level, slot, c):
        where, bit = self.links[level]
        source = self.value if level == 0 else self.held[level - 1]
        return remote(
            source.at[self.at(2 * slot + 1 - bit, c)],
            self.arrive[level].at[self.at(slot, c)],
            self.s_sem[level].at[slot, c],
            self.r_sem[level].at[slot, c],
            where,
        )

    def order(self, level):
        count = self.groups >> (level + 1)
        if count == 1:
            return [(0, False)]
        bit = self.links[level + 1][1]
        return [(2 * i + 1 - bit, True) for i in range(count // 2)] + [(2 * i + bit, False) for i in range(count // 2)]

    def start(self):
        def one(c, carry):
            for slot, _ in self.order(0):
                self.copy(0, slot, c).start()
            return carry

        lax.fori_loop(0, self.chunks, one, 0)

    def step(self, i, lag):
        for level in range(self.levels):
            c = i - level * lag

            @pl.when(jnp.logical_and(c >= 0, c < self.chunks))
            def _():
                bit = self.links[level][1]
                source = self.value if level == 0 else self.held[level - 1]
                for slot, goes in self.order(level):
                    self.copy(level, slot, c).wait_recv()
                    here = self.at(slot, c)
                    total = source[self.at(2 * slot + bit, c)].astype(F32) + self.arrive[level][here].astype(F32)
                    if level == self.levels - 1:
                        self.out[here] = total.astype(self.out.dtype)
                    else:
                        self.held[level][here] = total.astype(self.held[level].dtype)
                        if goes:
                            self.copy(level + 1, slot // 2, c).start()

    def steps(self, lag):
        return self.chunks + (self.levels - 1) * lag

    def finish(self):
        def one(c, carry):
            for level in range(self.levels):
                for slot in range(self.groups >> (level + 1)):
                    self.copy(level, slot, c).wait_send()
            return carry

        lax.fori_loop(0, self.chunks, one, 0)


def return_kernel(groups, rows, chunks, plans, *refs):
    refs = list(refs)

    def take(count):
        taken = refs[:count]
        del refs[:count]
        return taken

    m = dp_bits(groups)
    count = 4 * m - 1
    value, gains = take(2)
    grads = take(len(plans))
    out, gains_out = take(2)
    totals = take(len(plans))
    gains_all, gains_sum, g_s, g_r = take(4)
    task = Scatter(groups, rows, chunks, [value, out] + take(count))
    small = Scatter(groups, 8, 1, [gains_sum, gains_out] + take(count))
    large = [
        Scatter(groups, block, parts, [grad, total] + take(count))
        for (block, parts), grad, total in zip(plans, grads, totals)
    ]
    t = lax.axis_index("tensor")
    for where, _ in task.links:
        greet(where)
    for k in range(1, 4):
        greet({"tensor": lax.rem(t + k, 4)})
    pl.semaphore_wait(pltpu.get_barrier_semaphore(), m + 3)

    def spread(k):
        return remote(gains, gains_all.at[k - 1], g_s.at[k - 1], g_r.at[k - 1], {"tensor": lax.rem(t + k, 4)})

    for k in range(1, 4):
        spread(k).start()
    task.start()
    for item in large:
        item.start()
    for k in range(1, 4):
        spread(k).wait()
    gains_sum[...] = gains[...] + gains_all[0] + gains_all[1] + gains_all[2]
    small.start()

    def body(i, c):
        small.step(i, 1)
        task.step(i, 2)
        for item in large:
            item.step(i, 4)
        return c

    lax.fori_loop(0, max([task.steps(2), small.steps(1)] + [item.steps(4) for item in large]), body, 0)
    small.finish()
    task.finish()
    for item in large:
        item.finish()


def return_rows(value, gains, grads, groups, cid, chunks):
    rows, width = value.shape[0] // groups, value.shape[1]
    vmem = pl.BlockSpec(memory_space=pltpu.VMEM)
    part = gains.shape[1]
    plans, outs = [], [jax.ShapeDtypeStruct((rows, width), BF16), jax.ShapeDtypeStruct((8, part), F32)]
    scratch = [
        pltpu.VMEM((3,) + gains.shape, F32),
        pltpu.VMEM(gains.shape, F32),
        pltpu.SemaphoreType.DMA((3,)),
        pltpu.SemaphoreType.DMA((3,)),
    ]
    scratch += Scatter.scratch(groups, rows, width, chunks, BF16) + Scatter.scratch(groups, 8, part, 1, F32)
    for grad in grads:
        block = grad.shape[0] // groups
        plans.append((block, max(1, block // 48)))
        outs.append(jax.ShapeDtypeStruct((block, grad.shape[1]), F32))
        scratch += Scatter.scratch(groups, block, grad.shape[1], plans[-1][1], BF16)
    return pl.pallas_call(
        functools.partial(return_kernel, groups, rows, chunks, plans),
        out_shape=outs,
        in_specs=[vmem] * (2 + len(grads)),
        out_specs=[vmem] * len(outs),
        scratch_shapes=scratch,
        compiler_params=pltpu.CompilerParams(
            collective_id=cid, has_side_effects=True, vmem_limit_bytes=VMEM_LIMIT
        ),
        name="return_%d" % cid,
    )(value, gains, *grads)


def gather_kernel(groups, count, *refs):
    values, outs = refs[:count], refs[count : 2 * count]
    s_sem, r_sem, own = refs[2 * count :]
    m = dp_bits(groups)
    me = lax.axis_index("dp")
    links = [dp_partner(k) for k in range(m)]
    for where, _ in links:
        greet(where)
    pl.semaphore_wait(pltpu.get_barrier_semaphore(), m)

    def place(a, block):
        rows = values[a].shape[0]
        return outs[a].at[pl.ds(pl.multiple_of(block * rows, rows), rows)]

    def copy(a, level, i, mine):
        where, bit = links[level]
        low = lax.rem(me, 1 << (level + 1))
        if not mine:
            low = low + (1 - 2 * bit) * (1 << level)
        block = i * (1 << (level + 1)) + low
        return remote(place(a, block), place(a, block), s_sem.at[a, level, i], r_sem.at[a, level, i], where)

    locals_ = [pltpu.make_async_copy(values[a], place(a, me), own.at[a]) for a in range(count)]
    for item in locals_:
        item.start()
    for item in locals_:
        item.wait()
    for level in reversed(range(m)):
        for i in range(groups >> (level + 1)):
            for a in range(count):
                copy(a, level, i, True).start()
        for i in range(groups >> (level + 1)):
            for a in range(count):
                copy(a, level, i, False).wait_recv()
    for level in range(m):
        for i in range(groups >> (level + 1)):
            for a in range(count):
                copy(a, level, i, True).wait_send()


def gather_rows(values, groups, cid):
    vmem = pl.BlockSpec(memory_space=pltpu.VMEM)
    m, count = dp_bits(groups), len(values)
    dma = pltpu.SemaphoreType.DMA
    return pl.pallas_call(
        functools.partial(gather_kernel, groups, count),
        out_shape=[jax.ShapeDtypeStruct((groups * v.shape[0], v.shape[1]), v.dtype) for v in values],
        in_specs=[vmem] * count,
        out_specs=[vmem] * count,
        scratch_shapes=[dma((count, m, groups // 2)), dma((count, m, groups // 2)), dma((count,))],
        compiler_params=pltpu.CompilerParams(
            collective_id=cid, has_side_effects=True, vmem_limit_bytes=48 * 2**20
        ),
        name="gather_%d" % cid,
    )(*values)


class Line:
    lag_b, lag_c, lag_o = 2, 4, 6

    def __init__(self, first, half, pieces, part, base, out, scratch, norm=None, moved=None):
        self.first, self.half, self.pieces, self.size = first, half, pieces, half // pieces
        self.part, self.base, self.out = part, base, out
        (self.rin, self.smid, self.rmid) = scratch[:3]
        (self.s_up, self.r_up, self.s_mid, self.r_mid, self.s_b1, self.s_b2, self.r_b, self.s_c, self.r_c) = scratch[3:12]
        self.norm, self.moved = norm, moved
        if moved:
            self.arrived, self.shift = moved
            self.s_s, self.r_s = scratch[12:14]
            section = lax.axis_index("section")
            self.sends = section == (0 if self.shift > 0 else 1)
            self.partner = {"section": 1 - section}
        t = lax.axis_index("tensor")
        self.mid = jnp.logical_or(t == 1, t == 2)
        self.outside = jnp.logical_not(self.mid)
        self.outer = {"tensor": jnp.where(t == 1, 0, 3)}
        self.other = {"tensor": jnp.where(t == 1, 2, 1)}
        self.nbr = {"tensor": jnp.where(t == 0, 1, 2)}
        self.near = jnp.where(t < 2, 0, half)
        self.far = half - self.near

    @staticmethod
    def scratch(half, pieces, width, moved):
        dma = pltpu.SemaphoreType.DMA
        kinds = [
            pltpu.VMEM((2 * half, width), BF16),
            pltpu.VMEM((half, width), BF16),
            pltpu.VMEM((half, width), BF16),
            dma((2, pieces)),
            dma((2, pieces)),
        ] + [dma((pieces,))] * 7
        return kinds + ([dma((2, pieces))] * 2 if moved else [])

    @staticmethod
    def greet():
        t = lax.axis_index("tensor")

        @pl.when(t > 0)
        def _():
            greet({"tensor": jnp.maximum(t - 1, 0)})

        @pl.when(t < 3)
        def _():
            greet({"tensor": jnp.minimum(t + 1, 3)})

    def greet_sender(self):
        if self.moved:

            @pl.when(jnp.logical_not(self.sends))
            def _():
                greet(self.partner)

    def enter(self, others):
        bar = pltpu.get_barrier_semaphore()
        count = jnp.where(self.mid, 2, 1) + others
        if self.moved:
            count = count + jnp.where(self.sends, 1, 0)
        pl.semaphore_wait(bar, count)

    def local(self, start, p):
        return pl.ds(pl.multiple_of(start + p * self.size, self.size), self.size)

    def rows(self, start, p):
        return pl.ds(pl.multiple_of(self.first + start + p * self.size, self.size), self.size)

    def shifted(self, start, p):
        side = start // self.half
        here = self.rows(start, p)
        return remote(self.out.at[here], self.arrived.at[here], self.s_s.at[side, p], self.r_s.at[side, p], self.partner)

    def pass_on(self, start, p):
        if self.moved:

            @pl.when(self.sends)
            def _():
                self.shifted(start, p).start()

    def outcome(self, s_sem, r_sem, where, start, p):
        here = self.rows(start, p)
        return remote(self.out.at[here], self.out.at[here], s_sem.at[p], r_sem.at[p], where)

    def up(self, start, p, k, where):
        return remote(
            self.part.at[self.rows(start, p)], self.rin.at[self.local(start, p)], self.s_up.at[k, p], self.r_up.at[k, p], where
        )

    def cross(self, p):
        return remote(
            self.smid.at[self.local(0, p)], self.rmid.at[self.local(0, p)], self.s_mid.at[p], self.r_mid.at[p], self.other
        )

    def start(self):
        @pl.when(self.outside)
        def _():
            def begin(p, c):
                self.up(self.far, p, 0, self.nbr).start()
                self.up(self.near, p, 1, self.nbr).start()
                return c

            lax.fori_loop(0, self.pieces, begin, 0)

    def outer_step(self, i):
        p = i - self.lag_o

        @pl.when(jnp.logical_and(p >= 0, p < self.pieces))
        def _():
            self.outcome(self.s_b2, self.r_b, self.nbr, self.near, p).wait_recv()
            self.pass_on(self.near, p)
            self.outcome(self.s_c, self.r_c, self.nbr, self.far, p).wait_recv()
            self.pass_on(self.far, p)

    def mid_step(self, i):
        @pl.when(jnp.logical_and(i >= 0, i < self.pieces))
        def _():
            self.up(self.far, i, 0, self.outer).wait_recv()
            total = self.part[self.rows(self.far, i)].astype(F32) + self.rin[self.local(self.far, i)].astype(F32)
            self.smid[self.local(0, i)] = total.astype(BF16)
            self.cross(i).start()

        j = i - self.lag_b

        @pl.when(jnp.logical_and(j >= 0, j < self.pieces))
        def _():
            self.up(self.near, j, 1, self.outer).wait_recv()
            self.cross(j).wait_recv()
            here = self.rows(self.near, j)
            total = self.part[here].astype(F32) + self.rin[self.local(self.near, j)].astype(F32)
            total = total + self.rmid[self.local(0, j)].astype(F32)
            if self.norm:
                xrow, gain, gsum = self.norm
                x = xrow[here].astype(F32)
                scale = lax.rsqrt(jnp.mean(x * x, axis=-1, keepdims=True) + epsilon)
                unit = x * scale
                gsum[...] += jnp.sum(total * unit, axis=0, keepdims=True)
                inner = total * gain[...]
                total = scale * (inner - unit * jnp.mean(inner * unit, axis=-1, keepdims=True))
            self.out[here] = (self.base[here].astype(F32) + total).astype(BF16)
            self.outcome(self.s_b1, self.r_b, self.other, self.near, j).start()
            self.outcome(self.s_b2, self.r_b, self.outer, self.near, j).start()
            self.pass_on(self.near, j)

        k = i - self.lag_c

        @pl.when(jnp.logical_and(k >= 0, k < self.pieces))
        def _():
            self.outcome(self.s_b1, self.r_b, self.other, self.far, k).wait_recv()
            self.outcome(self.s_c, self.r_c, self.outer, self.far, k).start()
            self.pass_on(self.far, k)

    @property
    def steps(self):
        return self.pieces + self.lag_o

    def step(self, i):
        @pl.when(self.mid)
        def _():
            self.mid_step(i)

        @pl.when(self.outside)
        def _():
            self.outer_step(i)

    def finish(self):
        @pl.when(self.mid)
        def _():
            def one(p, c):
                self.cross(p).wait_send()
                self.outcome(self.s_b1, self.r_b, self.other, self.near, p).wait_send()
                self.outcome(self.s_b2, self.r_b, self.outer, self.near, p).wait_send()
                self.outcome(self.s_c, self.r_c, self.outer, self.far, p).wait_send()
                return c

            lax.fori_loop(0, self.pieces, one, 0)

        @pl.when(self.outside)
        def _():
            def one(p, c):
                self.up(self.far, p, 0, self.nbr).wait_send()
                self.up(self.near, p, 1, self.nbr).wait_send()
                return c

            lax.fori_loop(0, self.pieces, one, 0)

        if self.moved:

            def close(p, c):
                @pl.when(self.sends)
                def _():
                    self.shifted(0, p).wait_send()
                    self.shifted(self.half, p).wait_send()

                @pl.when(jnp.logical_not(self.sends))
                def _():
                    self.shifted(0, p).wait_recv()
                    self.shifted(self.half, p).wait_recv()

                return c

            lax.fori_loop(0, self.pieces, close, 0)


def run_steps(begin, end, *planned):
    def body(i, c):
        for step, offset in planned:
            step(i - offset)
        return c

    lax.fori_loop(begin, end, body, 0)


class Gather:
    def __init__(self, groups, rows, out, s_sem, r_sem):
        self.groups, self.rows, self.out, self.s_sem, self.r_sem = groups, rows, out, s_sem, r_sem
        self.levels = dp_bits(groups)
        self.links = [dp_partner(k) for k in range(self.levels)]
        self.me = lax.axis_index("dp")

    @staticmethod
    def scratch(groups):
        return [pltpu.SemaphoreType.DMA((dp_bits(groups), groups // 2))] * 2

    def copy(self, level, i, mine):
        where, bit = self.links[level]
        low = lax.rem(self.me, 1 << (level + 1))
        if not mine:
            low = low + (1 - 2 * bit) * (1 << level)
        block = i * (1 << (level + 1)) + low
        place = self.out.at[pl.ds(pl.multiple_of(block * self.rows, self.rows), self.rows)]
        return remote(place, place, self.s_sem.at[level, i], self.r_sem.at[level, i], where)

    def start(self, level):
        for i in range(self.groups >> (level + 1)):
            self.copy(level, i, True).start()

    def arrive(self, level):
        for i in range(self.groups >> (level + 1)):
            self.copy(level, i, False).wait_recv()

    def finish(self):
        for level in range(self.levels):
            for i in range(self.groups >> (level + 1)):
                self.copy(level, i, True).wait_send()


def with_transpose(left, right):
    return lax.dot_general(left, right, (((1,), (1,)), ((), ())), preferred_element_type=F32)


def rows_contract(left, right):
    return lax.dot_general(left, right, (((0,), (0,)), ((), ())), preferred_element_type=F32)


def times(left, right):
    return jnp.dot(left, right, preferred_element_type=F32)


LANES = 128
TILE = 256


def lanes(i, size=LANES):
    return pl.ds(pl.multiple_of(i * size, size), size)


def normalize(rows, gain):
    rows = rows.astype(F32)
    scale = lax.rsqrt(jnp.mean(rows * rows, axis=-1, keepdims=True) + epsilon)
    return (rows * scale * gain).astype(BF16)


def normalize_into(target, source, gain, first, count, block=32):
    def one(i, c):
        here = pl.ds(pl.multiple_of(first + i * block, block), block)
        target[here] = normalize(source[here], gain[...])
        return c

    lax.fori_loop(0, count // block, one, 0)


def rolled(value, cosine, sine):
    return value * cosine + pltpu.roll(value, LANES // 2, 1) * sine


def block_rows(keys):
    for rows in (160, 80, 32):
        if rows * keys <= 160 * 1280:
            return rows
    return 16


def score_rows(q, kv, h, g, here, qcode, qstart, kcode):
    scores = with_transpose(q[here, lanes(h)], kv[:, lanes(g)]) * HD ** (-0.5)
    code = kcode[...]
    return scores, jnp.logical_and(code <= qcode[here], code >= qstart[here])


def load_all(pairs, sems):
    copies = [pltpu.make_async_copy(src, dst, sems.at[i]) for i, (src, dst) in enumerate(pairs)]
    for item in copies:
        item.start()
    return copies


def forward_kernel(groups, q_heads, k_heads, pieces, *refs):
    refs = list(refs)

    def take(count):
        taken = refs[:count]
        del refs[:count]
        return taken

    x, cosine, sine, qcode, qstart, kcode, gain_one, gain_two = take(8)
    far_weights = take(5)
    q, kv, lse, mixed, resid, gate, up, act, y, arrived = take(10)
    near_weights = take(5)
    wqkv, wout, wgate, wup, wdown = near_weights
    part_one, part_two, n1, n2, w_sem = take(5)
    gather = Gather(groups, x.shape[0], kv, *take(2))
    count, width = x.shape
    quarter = count // 4
    lines = []
    for k in range(4):
        first = (k % 2) * 2 * quarter
        source = (part_one, x, resid) if k < 2 else (part_two, resid, y)
        lines.append(
            Line(first, quarter, pieces, *source, take(12 if k < 2 else 14), moved=None if k < 2 else (arrived, 1))
        )
    one_a, one_b, two_a, two_b = lines

    loads = load_all(list(zip(far_weights, near_weights)), w_sem)
    Line.greet()
    two_a.greet_sender()
    for where, _ in gather.links:
        greet(where)
    normalize_into(n1, x, gain_one, 0, count)
    loads[0].wait()

    mine = pl.ds(pl.multiple_of(lax.axis_index("dp") * count, count), count)
    for g in range(k_heads):
        column = (q_heads + g) * LANES
        value = times(n1[...], wqkv[:, column : column + LANES])
        kv[mine, g * LANES : (g + 1) * LANES] = rolled(value, cosine[...], sine[...]).astype(BF16)
        column += k_heads * LANES
        kv[mine, (k_heads + g) * LANES : (k_heads + g + 1) * LANES] = times(
            n1[...], wqkv[:, column : column + LANES]
        ).astype(BF16)

    two_a.enter(gather.levels)

    top = gather.levels - 1
    gather.start(top)

    def queries(h, c):
        value = times(n1[...], wqkv[:, lanes(h)])
        q[:, lanes(h)] = rolled(value, cosine[...], sine[...]).astype(BF16)
        return c

    lax.fori_loop(0, q_heads, queries, 0)
    for level in range(top, -1, -1):
        gather.arrive(level)
        if level:
            gather.start(level - 1)

    rows = block_rows(kv.shape[0])
    blocks = count // rows

    def attend(i, c):
        h, b = i // blocks, lax.rem(i, blocks)
        g = h // (q_heads // k_heads)
        here = pl.ds(pl.multiple_of(b * rows, rows), rows)
        scores, allowed = score_rows(q, kv, h, g, here, qcode, qstart, kcode)
        scores = jnp.where(allowed, scores, negative)
        row_max = jnp.max(scores, axis=-1, keepdims=True)
        expo = jnp.exp(scores - row_max)
        row_total = jnp.sum(expo, axis=-1, keepdims=True)
        prob = (expo / row_total).astype(BF16)
        mixed[here, lanes(h)] = times(prob, kv[:, lanes(k_heads + g)]).astype(BF16)
        there = pl.ds(pl.multiple_of(h * count + b * rows, rows), rows)
        lse[there] = jnp.broadcast_to(row_max + jnp.log(row_total), (rows, LANES))
        return c

    lax.fori_loop(0, q_heads * blocks, attend, 0)
    loads[1].wait()

    def projected(target, left, right, first, each=None):
        here = pl.ds(first, 2 * quarter)

        def one(i, c):
            target[here, lanes(i, TILE)] = times(left[here], right[:, lanes(i, TILE)]).astype(BF16)
            if each:
                each(i)
            return c

        lax.fori_loop(0, width // TILE, one, 0)

    projected(part_one, mixed, wout, 0)
    one_a.start()
    projected(part_one, mixed, wout, 2 * quarter)
    one_b.start()
    run_steps(0, one_a.steps, (one_a.step, 0), (one_b.step, pieces))
    loads[2].wait()
    loads[3].wait()
    loads[4].wait()

    def hidden(first, each):
        here = pl.ds(first, 2 * quarter)
        normalize_into(n2, resid, gain_two, first, 2 * quarter)

        def one(i, c):
            columns = lanes(i, TILE)
            gate_pre = times(n2[here], wgate[:, columns])
            up_pre = times(n2[here], wup[:, columns])
            gate[here, columns] = gate_pre.astype(BF16)
            up[here, columns] = up_pre.astype(BF16)
            act[here, columns] = (gate_pre * jax.nn.sigmoid(gate_pre) * up_pre).astype(BF16)
            each(i)
            return c

        lax.fori_loop(0, gate.shape[1] // TILE, one, 0)

    tiles = gate.shape[1] // TILE
    done = one_a.steps - pieces
    hidden(0, lambda i: one_b.step(done + i))
    projected(part_two, act, wdown, 0)
    two_a.start()
    run_steps(done + tiles, one_b.steps, (one_b.step, 0))
    hidden(2 * quarter, lambda i: two_a.step(i))
    projected(part_two, act, wdown, 2 * quarter)
    two_b.start()
    run_steps(tiles, two_b.steps + tiles, (two_a.step, 0), (two_b.step, tiles))
    gather.finish()
    for line in lines:
        line.finish()


VMEM_LIMIT = 58 * 2**20


def forward_tick(x, spots, weights, groups, q_heads, k_heads, cid):
    norm_one, wqkv, wout, norm_two, wgate, wup, wdown = weights
    count, width = x.shape
    hidden = wgate.shape[1]
    pieces = 5
    vmem = pl.BlockSpec(memory_space=pltpu.VMEM)
    far = pl.BlockSpec(memory_space=pl.ANY)

    def shape(*dims, dtype=BF16):
        return jax.ShapeDtypeStruct(dims, dtype)

    outs = [
        shape(count, q_heads * LANES),
        shape(groups * count, 2 * k_heads * LANES),
        shape(q_heads * count, LANES, dtype=F32),
        shape(count, q_heads * LANES),
        shape(count, width),
        shape(count, hidden),
        shape(count, hidden),
        shape(count, hidden),
        shape(count, width),
        shape(count, width),
    ]
    far_weights = [wqkv, wout, wgate, wup, wdown]
    scratch = [pltpu.VMEM(item.shape, BF16) for item in far_weights]
    scratch += [pltpu.VMEM((count, width), BF16)] * 4 + [pltpu.SemaphoreType.DMA((5,))]
    scratch += Gather.scratch(groups)
    for k in range(4):
        scratch += Line.scratch(count // 4, pieces, width, k >= 2)
    q, kv, lse, mixed, resid, gate, up, act, y, arrived = pl.pallas_call(
        functools.partial(forward_kernel, groups, q_heads, k_heads, pieces),
        out_shape=outs,
        in_specs=[vmem] * 8 + [far] * 5,
        out_specs=[vmem] * len(outs),
        scratch_shapes=scratch,
        compiler_params=pltpu.CompilerParams(
            collective_id=cid, has_side_effects=True, vmem_limit_bytes=VMEM_LIMIT
        ),
        name="forward_tick",
    )(x, *spots, norm_one[None], norm_two[None], *far_weights)
    return y, arrived, (x, q, kv, lse, mixed, resid, gate, up, act)


def back_ffn_kernel(pieces, *refs):
    dy, gate, up, resid, gain = refs[:5]
    far_weights = refs[5:8]
    dresid, gsum, dgate, dup = refs[8:12]
    wdown, wgate, wup = near_weights = refs[12:15]
    part, w_sem = refs[15:17]
    count, width = dy.shape
    quarter = count // 4
    a, b = [
        Line(k * 2 * quarter, quarter, pieces, part, dy, dresid, refs[17 + 12 * k : 29 + 12 * k], norm=(resid, gain, gsum))
        for k in range(2)
    ]
    loads = load_all(list(zip(far_weights, near_weights)), w_sem)
    Line.greet()
    gsum[...] = jnp.zeros_like(gsum)

    def hidden(first, each=None):
        here = pl.ds(first, 2 * quarter)

        def one(i, c):
            columns = lanes(i, TILE)
            d_act = with_transpose(dy[here], wdown[columns, :])
            gate_pre, up_pre = gate[here, columns].astype(F32), up[here, columns].astype(F32)
            sigma = jax.nn.sigmoid(gate_pre)
            d_silu = d_act * sigma
            dup[here, columns] = (d_silu * gate_pre).astype(BF16)
            dgate[here, columns] = (d_silu * up_pre * (1.0 + gate_pre * (1.0 - sigma))).astype(BF16)
            if each:
                each(i)
            return c

        lax.fori_loop(0, gate.shape[1] // TILE, one, 0)

    def back(first):
        here = pl.ds(first, 2 * quarter)

        def one(i, c):
            columns = lanes(i, TILE)
            total = with_transpose(dgate[here], wgate[columns, :]) + with_transpose(dup[here], wup[columns, :])
            part[here, columns] = total.astype(BF16)
            return c

        lax.fori_loop(0, width // TILE, one, 0)

    loads[0].wait()
    hidden(0)
    loads[1].wait()
    loads[2].wait()
    back(0)
    a.enter(0)
    a.start()
    tiles = gate.shape[1] // TILE
    hidden(2 * quarter, lambda i: a.step(i))
    back(2 * quarter)
    b.start()
    run_steps(tiles, b.steps + tiles, (a.step, 0), (b.step, tiles))
    a.finish()
    b.finish()


def back_ffn(dy, kept, weights, cid):
    norm_one, wqkv, wout, norm_two, wgate, wup, wdown = weights
    x, q, kv, lse, mixed, resid, gate, up, act = kept
    count, width = dy.shape
    pieces = 5
    vmem = pl.BlockSpec(memory_space=pltpu.VMEM)
    far = pl.BlockSpec(memory_space=pl.ANY)
    far_weights = [wdown, wgate, wup]
    scratch = [pltpu.VMEM(item.shape, BF16) for item in far_weights]
    scratch += [pltpu.VMEM((count, width), BF16), pltpu.SemaphoreType.DMA((3,))]
    scratch += Line.scratch(count // 4, pieces, width, False) * 2
    return pl.pallas_call(
        functools.partial(back_ffn_kernel, pieces),
        out_shape=[
            jax.ShapeDtypeStruct((count, width), BF16),
            jax.ShapeDtypeStruct((1, width), F32),
            jax.ShapeDtypeStruct(gate.shape, BF16),
            jax.ShapeDtypeStruct(gate.shape, BF16),
        ],
        in_specs=[vmem] * 5 + [far] * 3,
        out_specs=[vmem] * 4,
        scratch_shapes=scratch,
        compiler_params=pltpu.CompilerParams(
            collective_id=cid, has_side_effects=True, vmem_limit_bytes=VMEM_LIMIT
        ),
        name="back_ffn",
    )(dy, gate, up, resid, norm_two[None], *far_weights)


def back_attn_kernel(groups, q_heads, k_heads, pieces, shift, plans, *refs):
    refs = list(refs)

    def take(count):
        taken = refs[:count]
        del refs[:count]
        return taken

    dresid, x, q, kv, lse, cosine, sine, qcode, qstart, kcode, gain = take(11)
    far_weights = take(2)
    values = take(len(plans))
    dx, gsum, dqkv = take(3)
    (arrived,) = take(1) if shift else (None,)
    totals = take(len(plans))
    wout, wqkv = near_weights = take(2)
    part, dmixed, dkv, w_sem = take(4)
    levels = dp_bits(groups)
    count, width = x.shape
    quarter = count // 4
    keys = kv.shape[0]
    shares, owns, scatters = [], [], []
    for g in range(k_heads):
        share, own = take(2)
        shares.append(share)
        owns.append(own)
        scatters.append(Scatter(groups, count, 5, [share, own] + take(4 * levels - 1)))
    tasks = [
        Scatter(groups, rows, chunks, [value, total] + take(4 * levels - 1))
        for (rows, chunks), value, total in zip(plans, values, totals)
    ]
    moved = (arrived, shift) if shift else None
    a, b = [
        Line(
            k * 2 * quarter,
            quarter,
            pieces,
            part,
            dresid,
            dx,
            take(14 if shift else 12),
            norm=(x, gain, gsum),
            moved=moved,
        )
        for k in range(2)
    ]
    loads = load_all(list(zip(far_weights, near_weights)), w_sem)
    Line.greet()
    for where, _ in scatters[0].links:
        greet(where)
    a.greet_sender()
    gsum[...] = jnp.zeros_like(gsum)
    dkv[...] = jnp.zeros_like(dkv)
    a.enter(levels)
    for task in tasks:
        task.start()
    loads[0].wait()

    def mix(h, c):
        dmixed[:, lanes(h)] = with_transpose(dresid[...], wout[lanes(h), :]).astype(BF16)
        return c

    lax.fori_loop(0, q_heads, mix, 0)
    rows = block_rows(keys)
    blocks = count // rows
    repeat = q_heads // k_heads
    lag = 4
    scale = HD ** (-0.5)

    for g in range(k_heads):

        def one(i, c):
            h, n = g * repeat + i // blocks, lax.rem(i, blocks)
            here = pl.ds(pl.multiple_of(n * rows, rows), rows)
            there = pl.ds(pl.multiple_of(h * count + n * rows, rows), rows)
            scores, allowed = score_rows(q, kv, h, g, here, qcode, qstart, kcode)
            prob = jnp.where(allowed, jnp.exp(scores - lse[there][:, :1]), 0.0)
            dm = dmixed[here, lanes(h)]
            d_prob = with_transpose(dm, kv[:, lanes(k_heads + g)])
            row_dot = jnp.sum(prob * d_prob, axis=-1, keepdims=True)
            d_scores = (prob * (d_prob - row_dot)).astype(BF16)
            d_query = times(d_scores, kv[:, lanes(g)]) * scale
            dqkv[here, lanes(h)] = rolled(d_query, cosine[here], -sine[here]).astype(BF16)
            dkv[:, lanes(g)] += rows_contract(d_scores, q[here, lanes(h)]) * scale
            dkv[:, lanes(k_heads + g)] += rows_contract(prob.astype(BF16), dm)
            for task in tasks:
                task.step(g * repeat * blocks + i, lag)
            return c

        lax.fori_loop(0, repeat * blocks, one, 0)

        def narrow(i, c):
            here = pl.ds(pl.multiple_of(i * LANES, LANES), LANES)
            shares[g][here, :LANES] = dkv[here, lanes(g)].astype(BF16)
            shares[g][here, LANES:] = dkv[here, lanes(k_heads + g)].astype(BF16)
            return c

        lax.fori_loop(0, keys // LANES, narrow, 0)
        scatters[g].start()
    run_steps(0, scatters[0].steps(1), *[(functools.partial(lambda s, i: s.step(i, 1), s), 0) for s in scatters])
    for g in range(k_heads):
        dqkv[:, lanes(q_heads + g)] = rolled(owns[g][:, :LANES], cosine[...], -sine[...]).astype(BF16)
        dqkv[:, lanes(q_heads + k_heads + g)] = owns[g][:, LANES:].astype(BF16)
    loads[1].wait()

    def back(first, each=None):
        here = pl.ds(first, 2 * quarter)

        def one(i, c):
            columns = lanes(i, TILE)
            part[here, columns] = with_transpose(dqkv[here], wqkv[columns, :]).astype(BF16)
            if each:
                each(i)
            return c

        lax.fori_loop(0, width // TILE, one, 0)

    back(0)
    a.start()
    back(2 * quarter)
    b.start()
    begun = q_heads * blocks
    more = [(functools.partial(lambda s, i: s.step(i + begun, lag), s), 0) for s in tasks]
    last = max([b.steps + pieces] + [s.steps(lag) - begun for s in tasks])
    run_steps(0, last, (a.step, 0), (b.step, pieces), *more)
    a.finish()
    b.finish()
    for item in scatters + tasks:
        item.finish()


def back_attn(dresid, kept, spots, weights, groups, q_heads, k_heads, cid, shift, sums=()):
    norm_one, wqkv, wout, norm_two, wgate, wup, wdown = weights
    x, q, kv, lse, mixed, resid, gate, up, act = kept
    count, width = x.shape
    keys = kv.shape[0]
    pieces = 5
    vmem = pl.BlockSpec(memory_space=pltpu.VMEM)
    far = pl.BlockSpec(memory_space=pl.ANY)
    outs = [
        jax.ShapeDtypeStruct((count, width), BF16),
        jax.ShapeDtypeStruct((1, width), F32),
        jax.ShapeDtypeStruct((count, wqkv.shape[1]), BF16),
    ]
    if shift:
        outs.append(jax.ShapeDtypeStruct((count, width), BF16))
    scratch = [
        pltpu.VMEM(wout.shape, BF16),
        pltpu.VMEM(wqkv.shape, BF16),
        pltpu.VMEM((count, width), BF16),
        pltpu.VMEM(q.shape, BF16),
        pltpu.VMEM(kv.shape, F32),
        pltpu.SemaphoreType.DMA((2,)),
    ]
    for _ in range(k_heads):
        scratch += [pltpu.VMEM((keys, 2 * LANES), BF16), pltpu.VMEM((count, 2 * LANES), F32)]
        scratch += Scatter.scratch(groups, count, 2 * LANES, 5, BF16)
    plans = []
    for value in sums:
        rows = value.shape[0] // groups
        parts = max(1, min(8, rows // 16))
        while rows % (parts * 16):
            parts -= 1
        plans.append((rows, parts))
        outs.append(jax.ShapeDtypeStruct((rows, value.shape[1]), F32))
        scratch += Scatter.scratch(groups, rows, value.shape[1], parts, BF16)
    scratch += Line.scratch(count // 4, pieces, width, bool(shift)) * 2
    return pl.pallas_call(
        functools.partial(back_attn_kernel, groups, q_heads, k_heads, pieces, shift, plans),
        out_shape=outs,
        in_specs=[vmem] * 11 + [far] * 2 + [vmem] * len(sums),
        out_specs=[vmem] * len(outs),
        scratch_shapes=scratch,
        compiler_params=pltpu.CompilerParams(
            collective_id=cid, has_side_effects=True, vmem_limit_bytes=VMEM_LIMIT
        ),
        name="back_attn_%d" % cid,
    )(dresid, x, q, kv, lse, *spots, norm_one[None], wout, wqkv, *sums)


def rope_tables(pos):
    half_width = HD // 2
    inverse = rope_base ** (-(jnp.arange(half_width, dtype=F32) * 2.0 / HD))
    angle = pos.astype(F32)[:, None] * inverse[None, :]
    blank = jnp.zeros((pos.shape[0], LANES // 2 - half_width), F32)
    cosine, sine = jnp.cos(angle), jnp.sin(angle)
    return (
        jnp.concatenate([cosine, blank, cosine, blank], axis=1),
        jnp.concatenate([-sine, blank, sine, blank], axis=1),
    )


def spreader(heads, turned):
    feature = jnp.arange(HD)
    place = jnp.where(feature < HD // 2, feature, feature - HD // 2 + LANES // 2) if turned else feature
    lane = (jnp.arange(heads)[:, None] * LANES + place[None, :]).reshape(-1)
    return (lane[:, None] == jnp.arange(heads * LANES)[None, :]).astype(BF16)


def slots_of(lens, count):
    groups = lens.shape[0]
    kept = jnp.minimum(lens, count)
    free, extra = count - kept, lens - kept
    free_off = jnp.cumsum(free) - free
    extra_end = jnp.cumsum(extra)
    slot = jnp.arange(count)
    own = slot[None, :] < kept[:, None]
    index = free_off[:, None] + slot[None, :] - kept[:, None]
    source = jnp.sum(index[:, :, None] >= extra_end[None, None, :], axis=-1)
    begins = jnp.sum(jnp.where(index[:, :, None] >= extra_end[None, None, :], extra[None, None, :], 0), axis=-1)
    seq = jnp.where(own, jnp.arange(groups)[:, None], source)
    pos = jnp.where(own, slot[None, :], count + index - begins)
    return seq, pos, own


def on_device(
    inputs,
    cotangent,
    lengths,
    norm_attn,
    w_query,
    w_key,
    w_value,
    w_out,
    norm_ffn,
    w_gate,
    w_up,
    w_down,
):
    first = lax.axis_index("section") == 0
    me = lax.axis_index("dp")
    groups = lax.axis_size("dp")
    micro, seq_len, width = inputs.shape[0], inputs.shape[2], inputs.shape[3]
    count = seq_len * 5 // 8
    spare = seq_len - count
    q_heads, k_heads = w_query.shape[2] // HD, w_key.shape[2] // HD
    spread_q, spread_k = spreader(q_heads, True), spreader(k_heads, True)
    spread_v, spread_o = spreader(k_heads, False), spreader(q_heads, False)
    wqkv = jnp.concatenate(
        [times(w_query[0], spread_q), times(w_key[0], spread_k), times(w_value[0], spread_v)], axis=1
    ).astype(BF16)
    wout = rows_contract(spread_o, w_out[0]).astype(BF16)
    weights = (norm_attn[0], wqkv, wout, norm_ffn[0], w_gate[0], w_up[0], w_down[0])

    source = jnp.where(first, inputs[:, 0], cotangent[:, 0])
    length_rows = jnp.broadcast_to(lengths[:, 0].astype(F32)[:, None], (micro, 128))
    length_rows = jnp.concatenate([length_rows, jnp.zeros((8 - micro, 128), F32)], axis=0)
    first_extra, length_all = gather_rows([source[0, count:], length_rows], groups, 4)
    lens = length_all.reshape(groups, 8, 128)[:, :micro, 0].T.astype(jnp.int32)
    packed, slots = [], []
    for b in range(micro):
        seq, pos, own = slots_of(lens[b], count)
        slots.append((seq, pos))
        extra = first_extra if b == 0 else lax.all_gather(source[b, count:], "dp", axis=0, tiled=True)
        wanted = seq[me] * spare + pos[me] - count
        chosen = jnp.logical_and(jnp.arange(groups * spare)[None, :] == wanted[:, None], ~own[me][:, None])
        brought = jnp.dot(chosen.astype(BF16), extra, preferred_element_type=F32).astype(BF16)
        packed.append(jnp.where(own[me][:, None], source[b, :count], brought))

    def spots_of(b):
        seq, pos = slots[b]
        code = seq * seq_len + pos
        return rope_tables(pos[me]) + (code[me][:, None], (seq[me] * seq_len)[:, None], code.reshape(1, -1))

    spots = [spots_of(b) for b in range(micro)]

    def spots_at(tick):
        early, late = spots[min(tick, micro - 1)], spots[max(tick - 1, 0)]
        return tuple(jnp.where(first, a, b) for a, b in zip(early, late))

    empty = jnp.zeros((count, width), BF16)
    arriving = empty
    results, saved = [], []
    for tick in range(micro + 1):
        stream = jnp.where(first, packed[tick] if tick < micro else empty, arriving)
        result, arriving, kept = forward_tick(stream, spots_at(tick), weights, groups, q_heads, k_heads, 0)
        results.append(result)
        saved.append(kept)
    norm_one, norm_two = weights[0], weights[3]
    arriving = empty
    grads_in, before, gain_sums = [], [], []

    def all_rows(now, index):
        old = [item[index] for item in before]
        return jnp.concatenate([jnp.where(first, now, old[0])] + old[1:], axis=0)

    for tick in range(micro + 1):
        kept = saved[micro - tick]
        x, mixed, resid, act = kept[0], kept[4], kept[5], kept[8]
        incoming = jnp.where(first, arriving, packed[micro - 1 - tick] if tick < micro else empty)
        d_resid, gain_two, d_gate, d_up = back_ffn(incoming, kept, weights, 1)
        place = spots_at(micro - tick)
        if tick < micro:
            d_stream, gain_one, d_qkv, arriving = back_attn(
                d_resid, kept, place, weights, groups, q_heads, k_heads, 2, -1
            )
            before.append((resid, d_gate, d_up, incoming, act, x, d_qkv, d_resid, mixed))
        else:
            n2 = normalize(all_rows(resid, 0), norm_two)
            grad_gate = rows_contract(n2, all_rows(d_gate, 1)).astype(BF16)
            grad_up = rows_contract(n2, all_rows(d_up, 2)).astype(BF16)
            grad_down = rows_contract(all_rows(incoming, 3), all_rows(act, 4)).astype(BF16)
            ffn_grads = (grad_gate, grad_up, grad_down)
            beside = len(ffn_grads) if groups * count <= 2048 else 1
            d_stream, gain_one, d_qkv, *ffn_sums = back_attn(
                d_resid,
                kept,
                place,
                weights,
                groups,
                q_heads,
                k_heads,
                3,
                0,
                sums=ffn_grads[:beside],
            )
            n1 = normalize(all_rows(x, 5), norm_one)
            back_spread = [(spread_q, 0, q_heads), (spread_k, q_heads, k_heads), (spread_v, q_heads + k_heads, k_heads)]
            dqkv = all_rows(d_qkv, 6)
            dqkv = jnp.concatenate(
                [with_transpose(dqkv[:, i * LANES : (i + n) * LANES], item) for item, i, n in back_spread], axis=1
            ).astype(BF16)
            mix = with_transpose(all_rows(mixed, 8), spread_o).astype(BF16)
            grad_attn = jnp.concatenate(
                [rows_contract(n1, dqkv).astype(BF16), rows_contract(all_rows(d_resid, 7), mix).astype(BF16)], axis=1
            )
        grads_in.append(d_stream)
        gain_sums.append(jnp.concatenate([gain_one, gain_two], axis=0))

    gains = sum(gain_sums[1:], gain_sums[0])
    gains = jnp.concatenate([gains, jnp.zeros((6, width), F32)], axis=0)
    gains = gains.reshape(8, groups, -1).transpose(1, 0, 2).reshape(groups * 8, -1)

    def holder(b):
        seq, pos = slots[b]
        row = jnp.arange(groups * spare)[:, None]
        return jnp.logical_and(row == seq[me][None, :] * spare + pos[me][None, :] - count, pos[me][None, :] >= count)

    def spread(rows, b):
        return jnp.dot(holder(b).astype(BF16), rows, preferred_element_type=F32).astype(BF16)

    def unpack(rows, back, b, through):
        live = (jnp.arange(seq_len) < lens[b, me])[:, None]
        return jnp.where(live, jnp.concatenate([rows, back], axis=0), through)

    def come_back(rows, b):
        return lax.psum_scatter(spread(rows, b), "dp", scatter_dimension=0, tiled=True)

    acts = []
    for b in range(micro):
        rows = jnp.where(first, results[b], results[b + 1])
        acts.append(unpack(rows, come_back(rows, b), b, inputs[b, 0]))
    backs = []
    for b in range(micro):
        rows = jnp.where(first, grads_in[micro - b], grads_in[micro - 1 - b])
        if b == 0:
            back, gains, grad_attn, *rest = return_rows(
                spread(rows, b), gains, (grad_attn,) + ffn_grads[beside:], groups, 5, spare // 16
            )
            grad_gate, grad_up, grad_down = ffn_sums + rest
        else:
            back = come_back(rows, b)
        backs.append(unpack(rows, back, b, cotangent[b, 0]))
    acts, backs = jnp.stack(acts), jnp.stack(backs)
    ends = [0]
    for item in (w_query, w_key, w_value, w_query):
        ends.append(ends[-1] + item.shape[2])
    grad_query, grad_key, grad_value, grad_out = (grad_attn[:, a:b] for a, b in zip(ends, ends[1:]))
    final = (
        gains[0],
        grad_query,
        grad_key,
        grad_value,
        grad_out.T,
        gains[1],
        grad_gate,
        grad_up,
        grad_down.T,
    )
    return (acts[None, :, None], backs[None, :, None]) + tuple(item[None] for item in final)


def solution(mesh):
    placed = (
        P(None, "dp", None, None),
        P(None, "dp", None, None),
        P(None, "dp"),
        P("section", None),
        P("section", None, "tensor"),
        P("section", None, "tensor"),
        P("section", None, "tensor"),
        P("section", "tensor", None),
        P("section", None),
        P("section", None, "tensor"),
        P("section", None, "tensor"),
        P("section", "tensor", None),
    )
    return jax.shard_map(
        on_device,
        mesh=mesh,
        in_specs=placed,
        out_specs=(
            P("section", None, "dp", None, None),
            P("section", None, "dp", None, None),
            P("section", "dp"),
            P("section", "dp", "tensor"),
            P("section", "dp", "tensor"),
            P("section", "dp", "tensor"),
            P("section", "tensor", "dp"),
            P("section", "dp"),
            P("section", "dp", "tensor"),
            P("section", "dp", "tensor"),
            P("section", "tensor", "dp"),
        ),
        check_vma=False,
    )
```

time: 1120 us -> 876 us (0.78)
  Pallas kernels: 429 us -> 738 us
  waiting for transfers between devices: 198 us -> 0.07 us
  matrix products: 186 us -> 45.9 us
  blocking collectives: 98.4 us -> 0 us
  local copies, waits for them, and re-layouts: 101 us -> 28.6 us
  other arithmetic: 74 us -> 39.2 us
    pallas_call x12 -> x11, Pallas kernels: 429 us -> 738 us  [the longest x3 293 us: forward_tick(): pl.pallas_call(functools.partial(forward_kernel, groups, q_heads, k_heads...]
    dot_general x43 -> x7, matrix products: 95.5 us -> 14.7 us  [the longest x4 12.5 us: spread(): jnp.dot(holder(b).astype(BF16), rows, preferred_element_type=F32)]
    reduce_scatter x3, waiting for transfers between devices: 75.1 us -> 0.01 us  [come_back(): lax.psum_scatter(spread(rows, b), 'dp', scatter_dimension=0, tiled=True)]
    all_gather x6 -> x1, waiting for transfers between devices: 70 us -> 0.01 us  [on_device(): lax.all_gather(source[b, count:], 'dp', axis=0, tiled=True)]
    psum x1 -> x0, blocking collectives: 58.1 us -> none  [on_device(): gains = lax.psum(jnp.stack([totals[0], totals[5]]), ('tensor', 'dp'))]
    unnamed x23 -> x4, waiting for transfers between devices: 53.2 us -> 0.07 us
    unnamed x394 -> x119, local copies, waits for them, and re-layouts: 66.7 us -> 18.1 us
    all_gather x4 -> x0, blocking collectives: 40.3 us -> none  [the longest x3 34.4 us: forward(): every = lax.all_gather(own_keys, 'dp', axis=0, tiled=True)]
  transfers between devices with their start and end apart: 16 -> 4, of which waited for: 8 -> 0; matrix products, arithmetic and copies ran while one was open for 16% -> 9% of each run, Pallas kernels for 13% -> 75%
where the time goes in v2:
time: 876 us; the launch traced here: 867 us
  Pallas kernels  738 us (84%)
  matrix products  45.9 us (5%)
  other arithmetic  39.2 us (4%)
  local copies, waits for them, and re-layouts  28.6 us (3%)
  between operations  14.9 us (2%)
    pallas_call x3, Pallas kernels, forward_tick(): pl.pallas_call(functools.partial(forward_kernel, groups, q_heads, k_heads...  293 us
    pallas_call x3, Pallas kernels, back_attn(): pl.pallas_call(functools.partial(back_attn_kernel, groups, q_heads, k_hea...  249 us
    pallas_call x3, Pallas kernels, back_ffn(): pl.pallas_call(functools.partial(back_ffn_kernel, pieces), out_shape=[jax...  127 us
    pallas_call x1, Pallas kernels, return_rows(): pl.pallas_call(functools.partial(return_kernel, groups, rows, chunks, pla...  45.8 us
    pallas_call x1, Pallas kernels, gather_rows(): pl.pallas_call(functools.partial(gather_kernel, groups, count), out_shape...  24.5 us
    dot_general x6, matrix products, rows_contract(): lax.dot_general(left, right, (((0,), (0,)), ((), ())), preferred_element_...  21.4 us
    unnamed x119, local copies, waits for them, and re-layouts  18.1 us
  transfers between devices with their start and end apart: 4, of which 0 were waited for; matrix products, arithmetic and copies ran while one was open for 9% of the time, Pallas kernels for 75%

profile of v2, /device:TPU:0, one launch (start us, length us, event | category | flops | bytes accessed | tf_op | source)
XLA Modules:
  0.0 867.3 jit_solution(4198832090747962465)
XLA Ops:
  7.2 3.2 fusion.6
  13.3 24.5 %gather_4.1 = (bf16[768,1536]{1,0:T(8,128)(2,1)S(1)}, f32[32,128]{1,0:T(8,128)S(1)}) custom-call(bf16[192,1536]{1,0:T(8,128)(2,1)S(1)} %get-tuple-element.179.refs_0_, f32[8,128]{1,0:T(8,128)S(1)} %concatenate.124.refs_1_), custom_call_target="tpu_custom_call" | custom-call | tf_op jit(solution)/shard_map/gather_4/pallas_call | solution.py:252
  58.7 100.4 %forward_tick.3 = (bf16[320,512]{1,0:T(8,128)(2,1)}, bf16[1280,512]{1,0:T(8,128)(2,1)}, f32[1280,128]{1,0:T(8,128)}, bf16[320,512]{1,0:T(8,128)(2,1)}, bf16[320,...) custom-call(bf16[320,1536]{1,0:T(8,128)(2,1)} %get-tuple-element.238, ...), custom_call_target="tpu_custom_call" | custom-call | tf_op jit(solution)/shard_map/forward_tick/pallas_call | solution.py:735
  160.6 4.6 broadcast_select_fusion.8
  165.1 92.2 %forward_tick.4 = (bf16[320,512]{1,0:T(8,128)(2,1)}, bf16[1280,512]{1,0:T(8,128)(2,1)}, f32[1280,128]{1,0:T(8,128)}, bf16[320,512]{1,0:T(8,128)(2,1)}, bf16[320,...) custom-call(bf16[320,1536]{1,0:T(8,128)(2,1)} %get-tuple-element.191, ...), custom_call_target="tpu_custom_call" | custom-call | tf_op jit(solution)/shard_map/forward_tick/pallas_call | solution.py:735
  257.4 2.9 convolution_convert_fusion.7
  264.0 100.2 %forward_tick.5 = (bf16[320,512]{1,0:T(8,128)(2,1)}, bf16[1280,512]{1,0:T(8,128)(2,1)}, f32[1280,128]{1,0:T(8,128)}, bf16[320,512]{1,0:T(8,128)(2,1)}, bf16[320,...) custom-call(bf16[320,1536]{1,0:T(8,128)(2,1)} %get-tuple-element.187, ...), custom_call_target="tpu_custom_call" | custom-call | tf_op jit(solution)/shard_map/forward_tick/pallas_call | solution.py:735
  364.2 2.8 convolution_convert_fusion.6
  367.1 43.2 %back_ffn.3 = (bf16[320,1536]{1,0:T(8,128)(2,1)}, f32[1,1536]{1,0:T(1,128)}, bf16[320,1024]{1,0:T(8,128)(2,1)}, bf16[320,1024]{1,0:T(8,128)(2,1)}) custom-call(bf16[320,1536]{1,0:T(8,128)(2,1)} %get-tuple-element.190.refs_0_, bf16[320,1024]{1,0:T(8,128)(2,1)} %get-tuple-element.78.refs_1_, bf16[320,1024]{1,0:T(8,128)(2,1)} %get-tuple-element.79.refs_2_, ...), custom_call_target="tpu_custom_call" | custom-call | tf_op jit(solution)/shard_map/back_ffn/pallas_call | solution.py:820
  410.3 70.6 %back_attn_2.2 = (bf16[320,1536]{1,0:T(8,128)(2,1)}, f32[1,1536]{1,0:T(1,128)}, bf16[320,1024]{1,0:T(8,128)(2,1)}, bf16[320,1536]{1,0:T(8,128)(2,1)}) custom-call(bf16[320,1536]{1,0:T(8,128)(2,1)} %get-tuple-element.81.refs_0_, bf16[320,1536]{1,0:T(8,128)(2,1)} %get-tuple-element.187.refs_0_.refs_1_, bf16[320,512]{1,0:T(8,128)(2,1)} %get-tuple-element.82.refs_2_, ...), custom_call_target="tpu_custom_call" | custom-call | tf_op jit(solution)/shard_map/back_attn_2/pallas_call | solution.py:1004
  483.2 42.1 %back_ffn.4 = (bf16[320,1536]{1,0:T(8,128)(2,1)}, f32[1,1536]{1,0:T(1,128)}, bf16[320,1024]{1,0:T(8,128)(2,1)}, bf16[320,1024]{1,0:T(8,128)(2,1)}) custom-call(bf16[320,1536]{1,0:T(8,128)(2,1)} %broadcast_select_fusion.7.refs_0_, bf16[320,1024]{1,0:T(8,128)(2,1)} %get-tuple-element.86.refs_1_, bf16[320,1024]{1,0:T(8,128)(2,1)} %get-tuple-element.87.refs_2_, ...), custom_call_target="tpu_custom_call" | custom-call | tf_op jit(solution)/shard_map/back_ffn/pallas_call | solution.py:820
  525.3 67.3 %back_attn_2.3 = (bf16[320,1536]{1,0:T(8,128)(2,1)}, f32[1,1536]{1,0:T(1,128)}, bf16[320,1024]{1,0:T(8,128)(2,1)}, bf16[320,1536]{1,0:T(8,128)(2,1)}) custom-call(bf16[320,1536]{1,0:T(8,128)(2,1)} %get-tuple-element.89.refs_0_, bf16[320,1536]{1,0:T(8,128)(2,1)} %get-tuple-element.191.refs_0_.refs_1_, bf16[320,512]{1,0:T(8,128)(2,1)} %get-tuple-element.90.refs_2_, ...), custom_call_target="tpu_custom_call" | custom-call | tf_op jit(solution)/shard_map/back_attn_2/pallas_call | solution.py:1004
  595.0 41.3 %back_ffn.5 = (bf16[320,1536]{1,0:T(8,128)(2,1)}, f32[1,1536]{1,0:T(1,128)}, bf16[320,1024]{1,0:T(8,128)(2,1)}, bf16[320,1024]{1,0:T(8,128)(2,1)}) custom-call(bf16[320,1536]{1,0:T(8,128)(2,1)} %get-tuple-element.189.refs_0_, bf16[320,1024]{1,0:T(8,128)(2,1)} %get-tuple-element.94.refs_1_, bf16[320,1024]{1,0:T(8,128)(2,1)} %get-tuple-element.95.refs_2_, ...), custom_call_target="tpu_custom_call" | custom-call | tf_op jit(solution)/shard_map/back_ffn/pallas_call | solution.py:820
  636.3 2.5 broadcast_select_fusion.1
  641.8 4.0 convolution_convert_fusion.refs_15_
  645.8 4.3 convolution_convert_fusion.1.refs_14_
  650.1 4.2 convolution_convert_fusion.2.refs_13_
  654.3 110.7 %back_attn_3.1 = (bf16[320,1536]{1,0:T(8,128)(2,1)}, f32[1,1536]{1,0:T(1,128)}, bf16[320,1024]{1,0:T(8,128)(2,1)}, f32[384,1024]{1,0:T(8,128)}, f32[384,1024]{1,0:T(8,128)}, /*index=5*/f32[384,1024]{1,0:T(8,128)}) custom-call(bf16[320,1536]{1,0:T(8,128)(2,1)} %get-tuple-element.97.refs_0_, bf16[320,1536]{1,0:T(8,128)(2,1)} %get-tuple-element.238.refs_0_.refs_1_, ...), custom_call_target="tpu_custom_call" | custom-call | tf_op jit(solution)/shard_map/back_attn_3/pallas_call | solution.py:1004
  766.7 2.8 convolution_convert_fusion.3
  770.9 3.0 copy.88
  777.3 4.5 convolution_convert_fusion.10
  781.7 4.1 convolution_convert_fusion.5.refs_0_
  790.1 45.8 %return_5.1 = (bf16[192,1536]{1,0:T(8,128)(2,1)}, f32[8,384]{1,0:T(8,128)}, f32[384,1152]{1,0:T(8,128)}) custom-call(bf16[768,1536]{1,0:T(8,128)(2,1)} %convolution_convert_fusion.5.refs_0_, f32[32,384]{1,0:T(8,128)} %bitcast.162, bf16[1536,1152]{1,0:T(8,128)(2,1)} %pad_maximum_fusion.refs_2_), custom_call_target="tpu_custom_call" | custom-call | tf_op jit(solution)/shard_map/return_5/pallas_call | solution.py:195
  846.8 6.6 maximum_select_fusion
  (232 shorter events, 64.6 us)
Async XLA Ops:
  7.2 41.8 %copy-start = (bf16[1,384,1536]{2,1,0:T(8,128)(2,1)S(1)}, bf16[1,384,1536]{2,1,0:T(8,128)(2,1)}, u32[]{:S(2)}) copy-start(bf16[1,384,1536]{2,1,0:T(8,128)(2,1)} %param.19) | copy-start | bytes 3538948
  7.2 153.4 %all-gather.3.cloned.1.call-start = ((), (), s32[]{:S(2)}) async-start(), calls=%async_computation.6 | async-start | bytes 2949120 | tf_op jit(solution)/shard_map/all_gather | solution.py:1090
  13.1 833.7 %reduce-scatter.4.cloned.1.call-start = ((), (), s32[]{:S(2)}) async-start(), calls=%async_computation.3 | async-start | bytes 2949120 | tf_op jit(solution)/shard_map/reduce_scatter | solution.py:1183
  39.3 8.6 copy-start.36
  42.7 117.2 %copy-start.14 = (s32[320,1]{1,0:T(8,128)}, s32[320,1]{1,0:T(8,128)S(1)}, u32[]{:S(2)}) copy-start(s32[320,1]{1,0:T(8,128)S(1)} %copy.71.refs_3_.refs_7_) | copy-start | bytes 3844
  43.7 115.5 %copy-start.15 = (s32[320,1]{1,0:T(8,128)}, s32[320,1]{1,0:T(8,128)S(1)}, u32[]{:S(2)}) copy-start(s32[320,1]{1,0:T(8,128)S(1)} %copy.73.refs_4_.refs_8_) | copy-start | bytes 3844
  58.7 100.5 %copy-start.13 = (s32[320,1]{1,0:T(8,128)S(1)}, s32[320,1]{1,0:T(8,128)}, u32[]{:S(2)}) copy-start(s32[320,1]{1,0:T(8,128)} %copy.70.refs_4_.refs_8_) | copy-start | bytes 3844
  58.7 101.2 %copy-start.12 = (s32[320,1]{1,0:T(8,128)S(1)}, s32[320,1]{1,0:T(8,128)}, u32[]{:S(2)}) copy-start(s32[320,1]{1,0:T(8,128)} %copy.69.refs_3_.refs_7_) | copy-start | bytes 3844
  165.1 92.3 %copy-start.20 = (bf16[320,1536]{1,0:T(8,128)(2,1)S(1)}, bf16[320,1536]{1,0:T(8,128)(2,1)}, u32[]{:S(2)}) copy-start(bf16[320,1536]{1,0:T(8,128)(2,1)} %get-tuple-element.73) | copy-start | bytes 2949124
  260.3 586.5 %reduce-scatter.6.cloned.1.call-start = ((), (), s32[]{:S(2)}) async-start(), calls=%async_computation.4 | async-start | bytes 2949120 | tf_op jit(solution)/shard_map/reduce_scatter | solution.py:1183
  264.0 100.2 %copy-start.22 = (bf16[320,1536]{1,0:T(8,128)(2,1)S(1)}, bf16[320,1536]{1,0:T(8,128)(2,1)}, u32[]{:S(2)}) copy-start(bf16[320,1536]{1,0:T(8,128)(2,1)} %get-tuple-element.75) | copy-start | bytes 2949124
  367.1 479.7 %reduce-scatter.8.cloned.1.call-start = ((), (), s32[]{:S(2)}) async-start(), calls=%async_computation.5 | async-start | bytes 2949120 | tf_op jit(solution)/shard_map/reduce_scatter | solution.py:1183
  525.3 67.4 %copy-start.28 = (bf16[320,1536]{1,0:T(8,128)(2,1)S(1)}, bf16[320,1536]{1,0:T(8,128)(2,1)}, u32[]{:S(2)}) copy-start(bf16[320,1536]{1,0:T(8,128)(2,1)} %get-tuple-element.240) | copy-start | bytes 2949124
  595.0 41.3 %copy-start.7 = (bf16[320,1536]{1,0:T(8,128)(2,1)S(1)}, bf16[320,1536]{1,0:T(8,128)(2,1)}, u32[]{:S(2)}) copy-start(bf16[320,1536]{1,0:T(8,128)(2,1)} %get-tuple-element.96.refs_3_) | copy-start | bytes 2949124
  595.0 41.3 %copy-start.9 = (bf16[320,1536]{1,0:T(8,128)(2,1)S(1)}, bf16[320,1536]{1,0:T(8,128)(2,1)}, u32[]{:S(2)}) copy-start(bf16[320,1536]{1,0:T(8,128)(2,1)} %get-tuple-element.80.refs_3_) | copy-start | bytes 2949124
  595.0 41.3 %copy-start.10 = (bf16[320,1536]{1,0:T(8,128)(2,1)S(1)}, bf16[320,1536]{1,0:T(8,128)(2,1)}, u32[]{:S(2)}) copy-start(bf16[320,1536]{1,0:T(8,128)(2,1)} %get-tuple-element.81.refs_0_) | copy-start | bytes 2949124
  645.8 4.3 copy-start.52
  654.2 110.7 %copy-start.4 = (bf16[320,1536]{1,0:T(8,128)(2,1)S(1)}, bf16[320,1536]{1,0:T(8,128)(2,1)}, u32[]{:S(2)}) copy-start(bf16[320,1536]{1,0:T(8,128)(2,1)} %get-tuple-element.191.refs_0_.refs_1_) | copy-start | bytes 2949124
  654.2 111.2 %copy-start.29 = (bf16[320,1024]{1,0:T(8,128)(2,1)S(1)}, bf16[320,1024]{1,0:T(8,128)(2,1)}, u32[]{:S(2)}) copy-start(bf16[320,1024]{1,0:T(8,128)(2,1)} %get-tuple-element.119) | copy-start | bytes 1966084
  769.5 4.4 copy-start.16
  781.7 4.1 copy-start.42
  781.7 4.1 copy-start.43
  781.7 4.1 copy-start.55
  838.1 5.5 copy-start.21
  (36 other events, 64.7 us)
Sparse Core Ops, SparseCore 0:
  13.2 31.3 all-gather.2
  260.4 35.8 reduce-scatter.3
  367.2 34.3 reduce-scatter.5
  769.7 30.9 reduce-scatter.7

commit v3 on v2

--- a/solution.py
+++ b/solution.py
@@ -262,11 +262,61 @@
     )(*values)
 
 
+class OwnScatter(Scatter):
+    def __init__(self, groups, rows, chunks, refs):
+        m = dp_bits(groups)
+        super().__init__(groups, rows, chunks, list(refs[: 2 + m]) + [None] * (m - 1) + list(refs[2 + m :]))
+        self.me = lax.axis_index("dp")
+
+    @staticmethod
+    def scratch(groups, rows, width, chunks, dtype):
+        m = dp_bits(groups)
+        kinds = Scatter.scratch(groups, rows, width, chunks, dtype)
+        return kinds[:m] + kinds[2 * m - 1 :]
+
+    @staticmethod
+    def refs(groups):
+        return 3 * dp_bits(groups)
+
+    def whole(self, level, slot, c):
+        return self.at(slot * (1 << level) + lax.rem(self.me, 1 << level), c)
+
+    def copy(self, level, slot, c):
+        where, bit = self.links[level]
+        return remote(
+            self.value.at[self.whole(level, 2 * slot + 1 - bit, c)],
+            self.arrive[level].at[self.at(slot, c)],
+            self.s_sem[level].at[slot, c],
+            self.r_sem[level].at[slot, c],
+            where,
+        )
+
+    def step(self, i, lag):
+        for level in range(self.levels):
+            c = i - level * lag
+
+            @pl.when(jnp.logical_and(c >= 0, c < self.chunks))
+            def _():
+                bit = self.links[level][1]
+                for slot, goes in self.order(level):
+                    self.copy(level, slot, c).wait_recv()
+                    here = self.whole(level, 2 * slot + bit, c)
+                    total = self.value[here].astype(F32) + self.arrive[level][self.at(slot, c)].astype(F32)
+                    if level == self.levels - 1:
+                        self.out[self.at(0, c)] = total.astype(self.out.dtype)
+                    else:
+                        self.value[here] = total.astype(self.value.dtype)
+                        if goes:
+                            self.copy(level + 1, slot // 2, c).start()
+
+
 class Line:
-    lag_b, lag_c, lag_o = 2, 4, 6
-
-    def __init__(self, first, half, pieces, part, base, out, scratch, norm=None, moved=None):
-        self.first, self.half, self.pieces, self.size = first, half, pieces, half // pieces
+    lag_b, lag_c, lag_o = 2, 4, 5
+
+    def __init__(self, first, half, pieces, part, base, out, scratch, norm=None, moved=None, at=(0, 0, 0), turns=1):
+        self.first, self.half, self.size = first, half, half // pieces
+        self.each, self.pieces = pieces, pieces * turns
+        self.base_at, self.out_at, self.moved_at = at
         self.part, self.base, self.out = part, base, out
         (self.rin, self.smid, self.rmid) = scratch[:3]
         (self.s_up, self.r_up, self.s_mid, self.r_mid, self.s_b1, self.s_b2, self.r_b, self.s_c, self.r_c) = scratch[3:12]
@@ -287,8 +337,9 @@
         self.far = half - self.near
 
     @staticmethod
-    def scratch(half, pieces, width, moved):
+    def scratch(half, pieces, width, moved, turns=1):
         dma = pltpu.SemaphoreType.DMA
+        half, pieces = half * turns, pieces * turns
         kinds = [
             pltpu.VMEM((2 * half, width), BF16),
             pltpu.VMEM((half, width), BF16),
@@ -325,15 +376,20 @@
         pl.semaphore_wait(bar, count)
 
     def local(self, start, p):
+        if self.each < self.pieces:
+            start, p = start + (p // self.each) * (2 * self.half), lax.rem(p, self.each)
         return pl.ds(pl.multiple_of(start + p * self.size, self.size), self.size)
 
-    def rows(self, start, p):
-        return pl.ds(pl.multiple_of(self.first + start + p * self.size, self.size), self.size)
+    def own(self, p):
+        return pl.ds(pl.multiple_of(p * self.size, self.size), self.size)
+
+    def rows(self, start, p, at=0):
+        return self.local(self.first + at + start, p)
 
     def shifted(self, start, p):
         side = start // self.half
-        here = self.rows(start, p)
-        return remote(self.out.at[here], self.arrived.at[here], self.s_s.at[side, p], self.r_s.at[side, p], self.partner)
+        here, there = self.rows(start, p, self.out_at), self.rows(start, p, self.moved_at)
+        return remote(self.out.at[here], self.arrived.at[there], self.s_s.at[side, p], self.r_s.at[side, p], self.partner)
 
     def pass_on(self, start, p):
         if self.moved:
@@ -343,7 +399,7 @@
                 self.shifted(start, p).start()
 
     def outcome(self, s_sem, r_sem, where, start, p):
-        here = self.rows(start, p)
+        here = self.rows(start, p, self.out_at)
         return remote(self.out.at[here], self.out.at[here], s_sem.at[p], r_sem.at[p], where)
 
     def up(self, start, p, k, where):
@@ -353,10 +409,10 @@
 
     def cross(self, p):
         return remote(
-            self.smid.at[self.local(0, p)], self.rmid.at[self.local(0, p)], self.s_mid.at[p], self.r_mid.at[p], self.other
+            self.smid.at[self.own(p)], self.rmid.at[self.own(p)], self.s_mid.at[p], self.r_mid.at[p], self.other
         )
 
-    def start(self):
+    def start(self, turn=0):
         @pl.when(self.outside)
         def _():
             def begin(p, c):
@@ -364,7 +420,7 @@
                 self.up(self.near, p, 1, self.nbr).start()
                 return c
 
-            lax.fori_loop(0, self.pieces, begin, 0)
+            lax.fori_loop(turn * self.each, (turn + 1) * self.each, begin, 0)
 
     def outer_step(self, i):
         p = i - self.lag_o
@@ -381,7 +437,7 @@
         def _():
             self.up(self.far, i, 0, self.outer).wait_recv()
             total = self.part[self.rows(self.far, i)].astype(F32) + self.rin[self.local(self.far, i)].astype(F32)
-            self.smid[self.local(0, i)] = total.astype(BF16)
+            self.smid[self.own(i)] = total.astype(BF16)
             self.cross(i).start()
 
         j = i - self.lag_b
@@ -390,9 +446,9 @@
         def _():
             self.up(self.near, j, 1, self.outer).wait_recv()
             self.cross(j).wait_recv()
-            here = self.rows(self.near, j)
-            total = self.part[here].astype(F32) + self.rin[self.local(self.near, j)].astype(F32)
-            total = total + self.rmid[self.local(0, j)].astype(F32)
+            here = self.rows(self.near, j, self.base_at)
+            total = self.part[self.rows(self.near, j)].astype(F32) + self.rin[self.local(self.near, j)].astype(F32)
+            total = total + self.rmid[self.own(j)].astype(F32)
             if self.norm:
                 xrow, gain, gsum = self.norm
                 x = xrow[here].astype(F32)
@@ -401,7 +457,8 @@
                 gsum[...] += jnp.sum(total * unit, axis=0, keepdims=True)
                 inner = total * gain[...]
                 total = scale * (inner - unit * jnp.mean(inner * unit, axis=-1, keepdims=True))
-            self.out[here] = (self.base[here].astype(F32) + total).astype(BF16)
+            total = self.base[here].astype(F32) + total
+            self.out[self.rows(self.near, j, self.out_at)] = total.astype(BF16)
             self.outcome(self.s_b1, self.r_b, self.other, self.near, j).start()
             self.outcome(self.s_b2, self.r_b, self.outer, self.near, j).start()
             self.pass_on(self.near, j)
@@ -450,17 +507,21 @@
 
         if self.moved:
 
-            def close(p, c):
-                @pl.when(self.sends)
-                def _():
+            @pl.when(self.sends)
+            def _():
+                def close(p, c):
                     self.shifted(0, p).wait_send()
                     self.shifted(self.half, p).wait_send()
-
-                @pl.when(jnp.logical_not(self.sends))
-                def _():
-                    self.shifted(0, p).wait_recv()
-                    self.shifted(self.half, p).wait_recv()
-
+                    return c
+
+                lax.fori_loop(0, self.pieces, close, 0)
+
+    def receive(self):
+        @pl.when(jnp.logical_not(self.sends))
+        def _():
+            def close(p, c):
+                self.shifted(0, p).wait_recv()
+                self.shifted(self.half, p).wait_recv()
                 return c
 
             lax.fori_loop(0, self.pieces, close, 0)
@@ -523,6 +584,7 @@
 
 LANES = 128
 TILE = 256
+WIDE = 512
 
 
 def lanes(i, size=LANES):
@@ -535,10 +597,11 @@
     return (rows * scale * gain).astype(BF16)
 
 
-def normalize_into(target, source, gain, first, count, block=32):
+def normalize_into(target, source, gain, first, count, block=32, source_at=0):
     def one(i, c):
         here = pl.ds(pl.multiple_of(first + i * block, block), block)
-        target[here] = normalize(source[here], gain[...])
+        there = pl.ds(pl.multiple_of(source_at + first + i * block, block), block)
+        target[here] = normalize(source[there], gain[...])
         return c
 
     lax.fori_loop(0, count // block, one, 0)
@@ -640,7 +703,7 @@
         row_max = jnp.max(scores, axis=-1, keepdims=True)
         expo = jnp.exp(scores - row_max)
         row_total = jnp.sum(expo, axis=-1, keepdims=True)
-        prob = (expo / row_total).astype(BF16)
+        prob = (expo * (1.0 / row_total)).astype(BF16)
         mixed[here, lanes(h)] = times(prob, kv[:, lanes(k_heads + g)]).astype(BF16)
         there = pl.ds(pl.multiple_of(h * count + b * rows, rows), rows)
         lse[there] = jnp.broadcast_to(row_max + jnp.log(row_total), (rows, LANES))
@@ -698,6 +761,8 @@
     gather.finish()
     for line in lines:
         line.finish()
+    two_a.receive()
+    two_b.receive()
 
 
 VMEM_LIMIT = 58 * 2**20
@@ -961,6 +1026,9 @@
     run_steps(0, last, (a.step, 0), (b.step, pieces), *more)
     a.finish()
     b.finish()
+    if shift:
+        a.receive()
+        b.receive()
     for item in scatters + tasks:
         item.finish()
 
@@ -1014,6 +1082,1004 @@
     )(dresid, x, q, kv, lse, *spots, norm_one[None], wout, wqkv, *sums)
 
 
+def announce(sems, neighbours):
+    for here, where, k in neighbours:
+
+        @pl.when(here)
+        def _():
+            pl.semaphore_signal(sems.at[k], inc=1, device_id=where, device_id_type=MESH)
+
+
+def heard(sems, neighbours):
+    for k, (here, _, _) in enumerate(neighbours):
+
+        @pl.when(here)
+        def _():
+            pl.semaphore_wait(sems.at[k], 1)
+
+
+def main_kernel(groups, q_heads, k_heads, pieces, *refs):
+    refs = list(refs)
+
+    def take(count):
+        taken = refs[:count]
+        del refs[:count]
+        return taken
+
+    packed, cosine, sine, qcode, qstart, kcode, gain_one, gain_two, holder = take(9)
+    far_weights = take(5)
+    y_out, dx_out, back_out, xs, q, kv, lse, mixed, resid, gate, up, act, dys, dresid, dgate, dup, dqkv, gsum_one, gsum_two = take(19)
+    wqkv, wout, wgate, wup, wdown = near_weights = take(5)
+    part_one, part_two, normed, y, dmixed, dkv, w_sem, io_sem, meet_sem = take(9)
+    levels = dp_bits(groups)
+    gather_sems = take(2)
+    line_scratch = [take(12) for _ in range(4)]
+    forth_s, forth_r, back_s, back_r = take(4)
+    spares, returned = take(2)
+    spare = returned.shape[0]
+    give_lag = Line.lag_o + pieces
+    give = OwnScatter(groups, spare, spare // 32, [spares, returned] + take(OwnScatter.refs(groups)))
+    count, width = part_one.shape
+    keys = groups * count
+    quarter = count // 4
+    half = 2 * quarter
+    shares, owns, scatters = [], [], []
+    for g in range(k_heads):
+        share, own = take(2)
+        shares.append(share)
+        owns.append(own)
+        scatters.append(Scatter(groups, count, 5, [share, own] + take(4 * levels - 1)))
+    section = lax.axis_index("section")
+    t = lax.axis_index("tensor")
+    tiles, wide = gate.shape[1] // WIDE, width // WIDE
+    repeat = q_heads // k_heads
+    rows = block_rows(keys)
+    blocks = half // rows
+    scale = HD ** (-0.5)
+
+    def span(first, size):
+        return pl.ds(pl.multiple_of(first, 32), size)
+
+    neighbours = [
+        (t > 0, {"tensor": jnp.maximum(t - 1, 0)}, 1),
+        (t < 3, {"tensor": jnp.minimum(t + 1, 3)}, 0),
+    ]
+    for k in range(levels):
+        neighbours.append((t >= 0, dp_partner(k)[0], 2 + k))
+
+    for _, where, _ in neighbours[2:]:
+        greet(where)
+    Line.greet()
+    greet({"section": 1 - section})
+
+    loads = load_all(list(zip(far_weights, near_weights)), w_sem)
+
+    def fetch(slot, target):
+        place = span(slot * count, count)
+        return pltpu.make_async_copy(packed.at[place], target.at[place], io_sem.at[slot])
+
+    for slot in range(2):
+
+        @pl.when(section == 0)
+        def _():
+            fetch(slot, xs).start()
+
+        @pl.when(section == 1)
+        def _():
+            fetch(slot, dys).start()
+
+    pl.semaphore_wait(pltpu.get_barrier_semaphore(), jnp.where(jnp.logical_or(t == 1, t == 2), 2, 1) + levels + 1)
+    announce(meet_sem, neighbours)
+    gsum_one[...] = jnp.zeros_like(gsum_one)
+    gsum_two[...] = jnp.zeros_like(gsum_two)
+    for slot in range(2):
+
+        @pl.when(section == 0)
+        def _():
+            fetch(slot, xs).wait()
+
+        @pl.when(section == 1)
+        def _():
+            fetch(slot, dys).wait()
+
+    def projected(target, left, right, first, left_at, each=None):
+        here, there = span(first, half), span(first + left_at, half)
+
+        def one(i, c):
+            target[here, lanes(i, WIDE)] = times(left[there], right[:, lanes(i, WIDE)]).astype(BF16)
+            if each:
+                each(i)
+            return c
+
+        lax.fori_loop(0, wide, one, 0)
+
+    def give_back(slot, now, line):
+        @pl.when(now)
+        def _():
+            spares[...] = times(holder[span(slot * groups * spare, groups * spare)], y[...]).astype(BF16)
+            give.start()
+
+        def one(i, c):
+            line.step(i)
+
+            @pl.when(now)
+            def _():
+                give.step(i, give_lag)
+
+            return c
+
+        lax.fori_loop(0, line.steps, one, 0)
+
+    def give_rest(now, line, begun):
+        def one(i, c):
+            line.step(i)
+
+            @pl.when(now)
+            def _():
+                give.step(i - begun + give_lag, give_lag)
+
+            return c
+
+        lax.fori_loop(begun, max(line.steps, begun + give.steps(give_lag) - give_lag), one, 0)
+
+    def given(slot, now):
+        @pl.when(now)
+        def _():
+            give.finish()
+            pltpu.make_async_copy(returned, back_out.at[span(slot * spare, spare)], io_sem.at[1]).start()
+            pltpu.make_async_copy(returned, back_out.at[span(slot * spare, spare)], io_sem.at[1]).wait()
+
+    def forward(slot, carry):
+        base = slot * count
+        whole = span(base, count)
+        moved = (xs, 1)
+        lines = []
+        for k in range(4):
+            first = (k % 2) * half
+            scratch = list(line_scratch[k])
+            if k < 2:
+                lines.append(Line(first, quarter, pieces, part_one, xs, resid, scratch, at=(base, base, 0)))
+            else:
+                scratch += [forth_s.at[k - 2], forth_r.at[2 * slot + k - 2]]
+                lines.append(
+                    Line(first, quarter, pieces, part_two, resid, y, scratch, moved=moved, at=(base, 0, base))
+                )
+        one_a, one_b, two_a, two_b = lines
+        gather = Gather(groups, count, kv.at[span(slot * keys, keys)], *gather_sems)
+        two_a.receive()
+        two_b.receive()
+        normalize_into(normed, xs, gain_one, 0, count, source_at=base)
+
+        @pl.when(slot == 0)
+        def _():
+            loads[0].wait()
+
+        mine = span(slot * keys + lax.axis_index("dp") * count, count)
+        middle = (q_heads + k_heads) * LANES
+        value = times(normed[...], wqkv[:, q_heads * LANES : middle])
+        for g in range(k_heads):
+            here = slice(g * LANES, (g + 1) * LANES)
+            kv[mine, here] = rolled(value[:, here], cosine[whole], sine[whole]).astype(BF16)
+        kv[mine, k_heads * LANES :] = times(normed[...], wqkv[:, middle:]).astype(BF16)
+        heard(meet_sem, neighbours)
+        gather.start(levels - 1)
+        for first in range(0, q_heads, 2):
+            value = times(normed[...], wqkv[:, first * LANES : (first + 2) * LANES])
+            for h in range(2):
+                here = slice((first + h) * LANES, (first + h + 1) * LANES)
+                q[whole, here] = rolled(
+                    value[:, h * LANES : (h + 1) * LANES], cosine[whole], sine[whole]
+                ).astype(BF16)
+        for level in range(levels - 1, -1, -1):
+            gather.arrive(level)
+            if level:
+                gather.start(level - 1)
+
+        def attend(first, each=None):
+            def one(i, c):
+                h, b = i // blocks, lax.rem(i, blocks)
+                g = h // repeat
+                here = span(base + first + b * rows, rows)
+                scores = with_transpose(q[here, lanes(h)], kv[span(slot * keys, keys), lanes(g)]) * scale
+                code = kcode[slot]
+                allowed = jnp.logical_and(code <= qcode[here], code >= qstart[here])
+                scores = jnp.where(allowed, scores, negative)
+                row_max = jnp.max(scores, axis=-1, keepdims=True)
+                expo = jnp.exp(scores - row_max)
+                row_total = jnp.sum(expo, axis=-1, keepdims=True)
+                prob = (expo * (1.0 / row_total)).astype(BF16)
+                mixed[here, lanes(h)] = times(prob, kv[span(slot * keys, keys), lanes(k_heads + g)]).astype(BF16)
+                lse[span((slot * q_heads + h) * count + first + b * rows, rows)] = jnp.broadcast_to(
+                    row_max + jnp.log(row_total), (rows, LANES)
+                )
+                if each:
+                    each(i)
+                return c
+
+            lax.fori_loop(0, q_heads * blocks, one, 0)
+
+        attend(0)
+
+        @pl.when(slot == 0)
+        def _():
+            loads[1].wait()
+
+        projected(part_one, mixed, wout, 0, base)
+        one_a.start()
+        attend(half)
+        projected(part_one, mixed, wout, half, base)
+        one_b.start()
+        give_back(0, slot == 1, one_a)
+
+        @pl.when(slot == 0)
+        def _():
+            for item in loads[2:]:
+                item.wait()
+
+        def hidden(first, each):
+            here, there = span(first, half), span(base + first, half)
+            normalize_into(normed, resid, gain_two, first, half, source_at=base)
+
+            def one(i, c):
+                columns = lanes(i, WIDE)
+                gate_pre = times(normed[here], wgate[:, columns])
+                up_pre = times(normed[here], wup[:, columns])
+                gate[there, columns] = gate_pre.astype(BF16)
+                up[there, columns] = up_pre.astype(BF16)
+                act[there, columns] = (gate_pre * jax.nn.sigmoid(gate_pre) * up_pre).astype(BF16)
+                each(i)
+                return c
+
+            lax.fori_loop(0, tiles, one, 0)
+
+        hidden(0, one_b.step)
+        projected(part_two, act, wdown, 0, base)
+        two_a.start()
+        give_rest(slot == 1, one_b, tiles)
+        hidden(half, two_a.step)
+        projected(part_two, act, wdown, half, base)
+        two_b.start()
+        run_steps(tiles, two_a.steps, (two_a.step, 0))
+        run_steps(0, two_b.steps, (two_b.step, 0))
+        out = pltpu.make_async_copy(y, y_out.at[whole], io_sem.at[0])
+        out.start()
+        gather.finish()
+        for line in lines:
+            line.finish()
+        given(0, slot == 1)
+        out.wait()
+        announce(meet_sem, neighbours)
+        return carry
+
+    lax.fori_loop(0, 2, forward, 0)
+
+    def backward(tick, carry):
+        slot = 1 - tick
+        base = slot * count
+        whole = span(base, count)
+        lines = []
+        for k in range(4):
+            first = (k % 2) * half
+            scratch = list(line_scratch[k])
+            if k < 2:
+                norm = (resid, gain_two, gsum_two)
+                lines.append(Line(first, quarter, pieces, part_one, dys, dresid, scratch, norm=norm, at=(base, base, 0)))
+            else:
+                scratch += [back_s.at[k - 2], back_r.at[2 * slot + k - 2]]
+                norm = (xs, gain_one, gsum_one)
+                lines.append(
+                    Line(
+                        first, quarter, pieces, part_two, dresid, y, scratch, norm=norm, moved=(dys, -1), at=(base, 0, base)
+                    )
+                )
+        one_a, one_b, two_a, two_b = lines
+        two_a.receive()
+        two_b.receive()
+        dkv[...] = jnp.zeros_like(dkv)
+        heard(meet_sem, neighbours)
+
+        def hidden(first, each=None):
+            here = span(base + first, half)
+
+            def one(i, c):
+                columns = lanes(i, WIDE)
+                d_act = with_transpose(dys[here], wdown[columns, :])
+                gate_pre, up_pre = gate[here, columns].astype(F32), up[here, columns].astype(F32)
+                sigma = jax.nn.sigmoid(gate_pre)
+                d_silu = d_act * sigma
+                dup[here, columns] = (d_silu * gate_pre).astype(BF16)
+                dgate[here, columns] = (d_silu * up_pre * (1.0 + gate_pre * (1.0 - sigma))).astype(BF16)
+                if each:
+                    each(i)
+                return c
+
+            lax.fori_loop(0, tiles, one, 0)
+
+        def back_hidden(first):
+            here, there = span(first, half), span(base + first, half)
+
+            def one(i, c):
+                columns = lanes(i, WIDE)
+                total = with_transpose(dgate[there], wgate[columns, :]) + with_transpose(dup[there], wup[columns, :])
+                part_one[here, columns] = total.astype(BF16)
+                return c
+
+            lax.fori_loop(0, wide, one, 0)
+
+        hidden(0)
+        back_hidden(0)
+        one_a.start()
+        hidden(half)
+        back_hidden(half)
+        one_b.start()
+        give_back(1, tick == 0, one_a)
+
+        def attend(first, g, each=None):
+            def one(i, c):
+                h, n = g * repeat + i // blocks, lax.rem(i, blocks)
+                here = span(base + first + n * rows, rows)
+                near = span(first + n * rows, rows)
+                k_rows = kv[span(slot * keys, keys), lanes(g)]
+                scores = with_transpose(q[here, lanes(h)], k_rows) * scale
+                code = kcode[slot]
+                allowed = jnp.logical_and(code <= qcode[here], code >= qstart[here])
+                known = lse[span((slot * q_heads + h) * count + first + n * rows, rows)][:, :1]
+                prob = jnp.where(allowed, jnp.exp(scores - known), 0.0)
+                dm = dmixed[near, lanes(h)]
+                d_prob = with_transpose(dm, kv[span(slot * keys, keys), lanes(k_heads + g)])
+                row_dot = jnp.sum(prob * d_prob, axis=-1, keepdims=True)
+                d_scores = (prob * (d_prob - row_dot)).astype(BF16)
+                d_query = times(d_scores, k_rows) * scale
+                dqkv[here, lanes(h)] = rolled(d_query, cosine[here], -sine[here]).astype(BF16)
+                dkv[lanes(g), :] += rows_contract(q[here, lanes(h)], d_scores) * scale
+                dkv[lanes(k_heads + g), :] += rows_contract(dm, prob.astype(BF16))
+                if each:
+                    each(i)
+                return c
+
+            lax.fori_loop(0, repeat * blocks, one, 0)
+
+        def mix(first):
+            here, there = span(first, half), span(base + first, half)
+
+            def one(h, c):
+                dmixed[here, lanes(h)] = with_transpose(dresid[there], wout[lanes(h), :]).astype(BF16)
+                return c
+
+            lax.fori_loop(0, q_heads, one, 0)
+
+        mix(0)
+        turns = repeat * blocks
+        for g in range(k_heads):
+            attend(0, g, lambda i: one_b.step(g * turns + i))
+        give_rest(tick == 0, one_b, k_heads * turns)
+        mix(half)
+        for g in range(k_heads):
+            attend(half, g)
+
+            shares[g][:, :LANES] = jnp.transpose(dkv[lanes(g), :]).astype(BF16)
+            shares[g][:, LANES:] = jnp.transpose(dkv[lanes(k_heads + g), :]).astype(BF16)
+            scatters[g].start()
+        run_steps(0, scatters[0].steps(1), *[(functools.partial(lambda s, i: s.step(i, 1), s), 0) for s in scatters])
+        for g in range(k_heads):
+            dqkv[whole, lanes(q_heads + g)] = rolled(owns[g][:, :LANES], cosine[whole], -sine[whole]).astype(BF16)
+            dqkv[whole, lanes(q_heads + k_heads + g)] = owns[g][:, LANES:].astype(BF16)
+
+        def back(first, each=None):
+            here, there = span(first, half), span(base + first, half)
+
+            def one(i, c):
+                columns = lanes(i, WIDE)
+                part_two[here, columns] = with_transpose(dqkv[there], wqkv[columns, :]).astype(BF16)
+                if each:
+                    each(i)
+                return c
+
+            lax.fori_loop(0, wide, one, 0)
+
+        back(0)
+        two_a.start()
+        back(half)
+        two_b.start()
+        run_steps(0, two_a.steps, (two_a.step, 0))
+        run_steps(0, two_b.steps, (two_b.step, 0))
+        out = pltpu.make_async_copy(y, dx_out.at[whole], io_sem.at[0])
+        out.start()
+        for line in lines:
+            line.finish()
+        for item in scatters:
+            item.finish()
+        given(1, tick == 0)
+        out.wait()
+        announce(meet_sem, neighbours)
+        return carry
+
+    lax.fori_loop(0, 1 + section, backward, 0)
+    heard(meet_sem, neighbours)
+    for k in range(2):
+        Line(
+            k * half,
+            quarter,
+            pieces,
+            part_two,
+            dresid,
+            y,
+            list(line_scratch[2 + k]) + [back_s.at[k], back_r.at[k]],
+            moved=(dys, -1),
+        ).receive()
+
+
+def main_ticks(packed, spots, holder, weights, groups, q_heads, k_heads, cid):
+    norm_one, wqkv, wout, norm_two, wgate, wup, wdown = weights
+    count, width = packed.shape[0] // 2, packed.shape[1]
+    hidden, keys = wgate.shape[1], groups * count
+    pieces = 5
+    vmem = pl.BlockSpec(memory_space=pltpu.VMEM)
+    far = pl.BlockSpec(memory_space=pl.ANY)
+    dma = pltpu.SemaphoreType.DMA
+
+    def shape(columns, rows=2 * count, dtype=BF16):
+        return jax.ShapeDtypeStruct((rows, columns), dtype)
+
+    heads, both = q_heads * LANES, (q_heads + 2 * k_heads) * LANES
+    spare = holder.shape[0] // (2 * groups)
+    outs = [
+        shape(width),
+        shape(width),
+        shape(width, 2 * spare),
+        shape(width),
+        shape(heads),
+        shape(2 * k_heads * LANES, 2 * keys),
+        shape(LANES, 2 * q_heads * count, F32),
+        shape(heads),
+        shape(width),
+        shape(hidden),
+        shape(hidden),
+        shape(hidden),
+        shape(width),
+        shape(width),
+        shape(hidden),
+        shape(hidden),
+        shape(both),
+        shape(width, 1, F32),
+        shape(width, 1, F32),
+    ]
+    far_weights = [wqkv, wout, wgate, wup, wdown]
+    scratch = [pltpu.VMEM(item.shape, BF16) for item in far_weights]
+    scratch += [pltpu.VMEM((count, width), BF16)] * 4 + [
+        pltpu.VMEM((count, heads), BF16),
+        pltpu.VMEM((2 * k_heads * LANES, keys), F32),
+        dma((5,)),
+        dma((2,)),
+        pltpu.SemaphoreType.REGULAR((2 + dp_bits(groups),)),
+    ]
+    scratch += Gather.scratch(groups)
+    for k in range(4):
+        scratch += Line.scratch(quarter_rows(count), pieces, width, False)
+    scratch += [dma((2, 2, pieces)), dma((4, 2, pieces))] * 2
+    scratch += [pltpu.VMEM((groups * spare, width), BF16), pltpu.VMEM((spare, width), BF16)]
+    scratch += OwnScatter.scratch(groups, spare, width, spare // 32, BF16)
+    for _ in range(k_heads):
+        scratch += [pltpu.VMEM((keys, 2 * LANES), BF16), pltpu.VMEM((count, 2 * LANES), F32)]
+        scratch += Scatter.scratch(groups, count, 2 * LANES, 5, BF16)
+    return pl.pallas_call(
+        functools.partial(main_kernel, groups, q_heads, k_heads, pieces),
+        out_shape=outs,
+        in_specs=[far] + [vmem] * 8 + [far] * 5,
+        out_specs=[far] * 3 + [vmem] * (len(outs) - 3),
+        scratch_shapes=scratch,
+        compiler_params=pltpu.CompilerParams(
+            collective_id=cid, has_side_effects=True, vmem_limit_bytes=VMEM_LIMIT
+        ),
+        name="main_ticks",
+    )(packed, *spots, norm_one[None], norm_two[None], holder, *far_weights)
+
+
+def quarter_rows(count):
+    return count // 4
+
+
+def weight_job(target, left, right, i, block=256):
+    here = lanes(i, block)
+    target[here, :] = rows_contract(left[:, here], right[...]).astype(BF16)
+
+
+def last_ffn_kernel(groups, pieces, chunks, *refs):
+    refs = list(refs)
+
+    def take(count):
+        taken = refs[:count]
+        del refs[:count]
+        return taken
+
+    gain, holder = take(2)
+    sources = take(12)
+    first_dresid, gsum, g_up, down_sum, gate_sum, returned = take(6)
+    wdown, wgate, wup, dys, act, gate, up, dgate, dup, resid = kept = take(10)
+    n2, part, g_down, g_gate, spares, dx, w_sem = take(7)
+    (scratch,) = (take(12),)
+    count, width = part.shape
+    half = count // 2
+    line_a, line_b = [
+        Line(k * half, half // 2, pieces, part, dys, first_dresid, item, norm=(resid, gain, gsum))
+        for k, item in enumerate((scratch, take(12)))
+    ]
+    down = OwnScatter(groups, width // groups, chunks, [g_down, down_sum] + take(OwnScatter.refs(groups)))
+    gated = OwnScatter(groups, width // groups, chunks, [g_gate, gate_sum] + take(OwnScatter.refs(groups)))
+    spare = returned.shape[0]
+    give = OwnScatter(groups, spare, spare // 32, [spares, returned] + take(OwnScatter.refs(groups)))
+    section = lax.axis_index("section")
+    mine = section == 0
+    tiles, wide, blocks = act.shape[1] // WIDE, width // WIDE, width // TILE
+
+    def load(k):
+        if k in (7, 8):
+            return pltpu.make_async_copy(sources[k].at[count:], kept[k].at[count:], w_sem.at[k])
+        return pltpu.make_async_copy(sources[k], kept[k], w_sem.at[k])
+
+    lacks = [
+        pltpu.make_async_copy(sources[7].at[:count], kept[7].at[:count], w_sem.at[10]),
+        pltpu.make_async_copy(sources[8].at[:count], kept[8].at[:count], w_sem.at[11]),
+        pltpu.make_async_copy(sources[10].at[:count], first_dresid, w_sem.at[12]),
+    ]
+    last_dx = pltpu.make_async_copy(sources[11].at[count:], dx, w_sem.at[13])
+    loads = [load(k) for k in range(10)]
+    for k in (3, 0, 5, 6, 1, 2):
+        loads[k].start()
+    last_dx.start()
+    for k in (4, 9, 7, 8):
+        loads[k].start()
+
+    @pl.when(section > 0)
+    def _():
+        for item in lacks:
+            item.start()
+
+    Line.greet()
+    for where, _ in down.links:
+        greet(where)
+    gsum[...] = jnp.zeros_like(gsum)
+    line_a.enter(down.levels)
+    for k in (3, 0, 5, 6):
+        loads[k].wait()
+
+    def hidden(first):
+        here = pl.ds(first, half)
+
+        def one(i, c):
+            columns = lanes(i, WIDE)
+            d_act = with_transpose(dys[here], wdown[columns, :])
+            gate_pre, up_pre = gate[here, columns].astype(F32), up[here, columns].astype(F32)
+            sigma = jax.nn.sigmoid(gate_pre)
+            d_silu = d_act * sigma
+            dup[here, columns] = (d_silu * gate_pre).astype(BF16)
+            dgate[here, columns] = (d_silu * up_pre * (1.0 + gate_pre * (1.0 - sigma))).astype(BF16)
+            return c
+
+        lax.fori_loop(0, tiles, one, 0)
+
+    def back(first):
+        here = pl.ds(first, half)
+
+        def one(i, c):
+            columns = lanes(i, WIDE)
+            total = with_transpose(dgate[here], wgate[columns, :]) + with_transpose(dup[here], wup[columns, :])
+            part[here, columns] = total.astype(BF16)
+            return c
+
+        lax.fori_loop(0, wide, one, 0)
+
+    @pl.when(mine)
+    def _():
+        hidden(0)
+
+    loads[1].wait()
+    loads[2].wait()
+
+    @pl.when(mine)
+    def _():
+        back(0)
+        line_a.start()
+
+    last_dx.wait()
+    spares[...] = times(holder[...], dx[...]).astype(BF16)
+    give.start()
+
+    @pl.when(mine)
+    def _():
+        hidden(half)
+        back(half)
+        line_b.start()
+
+    for k in (4, 9, 7, 8):
+        loads[k].wait()
+
+    kinds = ((g_down, dys, act), (g_gate, n2, dgate), (g_up, n2, dup))
+
+    def job(k):
+        for which, (target, left, right) in enumerate(kinds):
+
+            @pl.when(k // blocks == which)
+            def _():
+                weight_job(target, left, right, lax.rem(k, blocks))
+
+    normalize_into(n2, resid, gain, 0, 2 * count)
+    for k in range(2):
+        job(k)
+
+    @pl.when(section > 0)
+    def _():
+        lacks[0].wait()
+        lacks[1].wait()
+
+    lag = 4
+    first_part = blocks - 2
+    begin_down, begin_gate = first_part, first_part + blocks
+
+    def step(i, c):
+        @pl.when(mine)
+        def _():
+            line_a.step(i)
+            line_b.step(i - line_a.steps)
+
+        @pl.when(i + 2 < 3 * blocks)
+        def _():
+            job(i + 2)
+
+        @pl.when(i == begin_down - 1)
+        def _():
+            down.start()
+
+        @pl.when(i == begin_gate - 1)
+        def _():
+            gated.start()
+
+        give.step(i, 6)
+        down.step(i - begin_down, lag)
+        gated.step(i - begin_gate, lag)
+        return c
+
+    ending = max(
+        line_a.steps + line_b.steps, 3 * blocks - 2, begin_down + down.steps(lag), begin_gate + gated.steps(lag), give.steps(6)
+    )
+    lax.fori_loop(0, ending, step, 0)
+
+    @pl.when(mine)
+    def _():
+        line_a.finish()
+        line_b.finish()
+
+    @pl.when(section > 0)
+    def _():
+        lacks[2].wait()
+
+    give.finish()
+    down.finish()
+    gated.finish()
+
+
+def last_ffn(known, holder, weights, groups, cid):
+    norm_one, wqkv, wout, norm_two, wgate, wup, wdown = weights
+    dys, act, gate, up, dgate, dup, resid, dresid, dx = known
+    spare = holder.shape[0] // groups
+    count, width = dys.shape[0] // 2, dys.shape[1]
+    hidden = act.shape[1]
+    pieces, chunks = 5, 8
+    vmem = pl.BlockSpec(memory_space=pltpu.VMEM)
+    far = pl.BlockSpec(memory_space=pl.ANY)
+    sources = [wdown, wgate, wup, dys, act, gate, up, dgate, dup, resid]
+    scratch = [pltpu.VMEM(item.shape, BF16) for item in sources]
+    scratch += [
+        pltpu.VMEM((2 * count, width), BF16),
+        pltpu.VMEM((count, width), BF16),
+        pltpu.VMEM((width, hidden), BF16),
+        pltpu.VMEM((width, hidden), BF16),
+        pltpu.VMEM((groups * spare, width), BF16),
+        pltpu.VMEM((count, width), BF16),
+        pltpu.SemaphoreType.DMA((14,)),
+    ]
+    scratch += Line.scratch(count // 4, pieces, width, False) * 2
+    scratch += OwnScatter.scratch(groups, width // groups, hidden, chunks, BF16) * 2
+    scratch += OwnScatter.scratch(groups, spare, width, spare // 32, BF16)
+    return pl.pallas_call(
+        functools.partial(last_ffn_kernel, groups, pieces, chunks),
+        out_shape=[
+            jax.ShapeDtypeStruct((count, width), BF16),
+            jax.ShapeDtypeStruct((1, width), F32),
+            jax.ShapeDtypeStruct((width, hidden), BF16),
+            jax.ShapeDtypeStruct((width // groups, hidden), F32),
+            jax.ShapeDtypeStruct((width // groups, hidden), F32),
+            jax.ShapeDtypeStruct((spare, width), BF16),
+        ],
+        in_specs=[vmem] * 2 + [far] * 12,
+        out_specs=[vmem] * 6,
+        scratch_shapes=scratch,
+        compiler_params=pltpu.CompilerParams(
+            collective_id=cid, has_side_effects=True, vmem_limit_bytes=VMEM_LIMIT
+        ),
+        name="last_ffn",
+    )(norm_two[None], holder, *sources, dresid, dx)
+
+
+def last_attn_kernel(groups, q_heads, k_heads, pieces, chunks, spare_chunks, *refs):
+    refs = list(refs)
+
+    def take(count):
+        taken = refs[:count]
+        del refs[:count]
+        return taken
+
+    cosine, sine, qcode, qstart, kcode, gain, dresid, holder, gains, spread_q, spread_k, spread_v, spread_o = take(13)
+    sources = take(10)
+    (dx_known,) = take(1)
+    dx, returned, gains_out, up_sum, attn_sum = take(5)
+    wout, wqkv, x, q, kv, lse, mixed, dqkv, other_dresid, g_up = kept = take(10)
+    part, dmixed, dkv, n1, g_attn, spares, gsum, gains_own, gains_all, gains_sum, w_sem, g_s, g_r = take(13)
+    levels = dp_bits(groups)
+    count, width = part.shape
+    half = count // 2
+    keys = kv.shape[0]
+    shares, owns, scatters = [], [], []
+    for g in range(k_heads):
+        share, own = take(2)
+        shares.append(share)
+        owns.append(own)
+        scatters.append(OwnScatter(groups, count, 5, [share, own] + take(OwnScatter.refs(groups))))
+    block = width // groups
+    up_task, attn_task = [
+        OwnScatter(groups, block, chunks, [value, total] + take(OwnScatter.refs(groups)))
+        for value, total in ((g_up, up_sum), (g_attn, attn_sum))
+    ]
+    spare = spares.shape[0] // groups
+    back_task = OwnScatter(groups, spare, spare_chunks, [spares, returned] + take(OwnScatter.refs(groups)))
+    small = OwnScatter(groups, 8, 1, [gains_sum, gains_out] + take(OwnScatter.refs(groups)))
+    line_a, line_b = [
+        Line(k * half, half // 2, pieces, part, dresid, dx, take(12), norm=(x, gain, gsum)) for k in range(2)
+    ]
+    section, t = lax.axis_index("section"), lax.axis_index("tensor")
+    mine = section == 0
+    order = [9, 0, 3, 4, 5, 1, 2, 6, 7, 8]
+    loads = [pltpu.make_async_copy(sources[k], kept[k], w_sem.at[k]) for k in range(10)]
+    for k in order:
+        loads[k].start()
+    known = pltpu.make_async_copy(dx_known.at[:count], dx, w_sem.at[11])
+
+    @pl.when(section > 0)
+    def _():
+        known.start()
+
+    for k in range(1, 4):
+        greet({"tensor": lax.rem(t + k, 4)})
+    for where, _ in up_task.links:
+        greet(where)
+    gsum[...] = jnp.zeros_like(gsum)
+    dkv[...] = jnp.zeros_like(dkv)
+    pl.semaphore_wait(pltpu.get_barrier_semaphore(), 3 + levels)
+    loads[9].wait()
+    up_task.start()
+    for k in order[1:]:
+        loads[k].wait()
+
+    wide, jobs = width // WIDE, width // TILE
+    repeat = q_heads // k_heads
+    rows = block_rows(keys)
+    blocks = half // rows
+    turns = repeat * blocks
+    scale = HD ** (-0.5)
+    lag = 6
+
+    begun = k_heads * turns
+
+    def early(i):
+        @pl.when(lax.rem(i, 2) == 0)
+        def _():
+            up_task.step(i // 2, lag)
+
+    def sums(i):
+        up_task.step(i, lag)
+
+    def mix(first):
+        here = pl.ds(first, half)
+
+        def one(h, c):
+            dmixed[here, lanes(h)] = with_transpose(dresid[here], wout[lanes(h), :]).astype(BF16)
+            return c
+
+        lax.fori_loop(0, q_heads, one, 0)
+
+    def attend(first, g, each):
+        def one(i, c):
+            h, n = g * repeat + i // blocks, lax.rem(i, blocks)
+            here = pl.ds(pl.multiple_of(first + n * rows, rows), rows)
+            scores, allowed = score_rows(q, kv, h, g, here, qcode, qstart, kcode)
+            there = pl.ds(pl.multiple_of(h * count + first + n * rows, rows), rows)
+            prob = jnp.where(allowed, jnp.exp(scores - lse[there][:, :1]), 0.0)
+            dm = dmixed[here, lanes(h)]
+            d_prob = with_transpose(dm, kv[:, lanes(k_heads + g)])
+            row_dot = jnp.sum(prob * d_prob, axis=-1, keepdims=True)
+            d_scores = (prob * (d_prob - row_dot)).astype(BF16)
+            d_query = times(d_scores, kv[:, lanes(g)]) * scale
+            dqkv[here, lanes(h)] = rolled(d_query, cosine[here], -sine[here]).astype(BF16)
+            dkv[lanes(g), :] += rows_contract(q[here, lanes(h)], d_scores) * scale
+            dkv[lanes(k_heads + g), :] += rows_contract(dm, prob.astype(BF16))
+            each(i)
+            return c
+
+        lax.fori_loop(0, turns, one, 0)
+
+    def back(first):
+        here = pl.ds(first, half)
+
+        def one(i, c):
+            columns = lanes(i, WIDE)
+            part[here, columns] = with_transpose(dqkv[here], wqkv[columns, :]).astype(BF16)
+            return c
+
+        lax.fori_loop(0, wide, one, 0)
+
+    @pl.when(mine)
+    def _():
+        mix(0)
+        mix(half)
+        for g in range(k_heads):
+            for first in (0, half):
+                at = 2 * g * turns + (turns if first else 0)
+                attend(first, g, lambda i: early(at + i))
+
+            shares[g][:, :LANES] = jnp.transpose(dkv[lanes(g), :]).astype(BF16)
+            shares[g][:, LANES:] = jnp.transpose(dkv[lanes(k_heads + g), :]).astype(BF16)
+            scatters[g].start()
+        run_steps(0, scatters[0].steps(1), *[(functools.partial(lambda s, i: s.step(i, 1), s), 0) for s in scatters])
+        for g in range(k_heads):
+            dqkv[:count, lanes(q_heads + g)] = rolled(owns[g][:, :LANES], cosine[...], -sine[...]).astype(BF16)
+            dqkv[:count, lanes(q_heads + k_heads + g)] = owns[g][:, LANES:].astype(BF16)
+        back(0)
+        line_a.start()
+        back(half)
+        line_b.start()
+
+    @pl.when(section > 0)
+    def _():
+        run_steps(0, begun, (sums, 0))
+        known.wait()
+
+    normalize_into(n1, x, gain, 0, 2 * count)
+    ends = [0]
+    for item in (spread_q, spread_k, spread_v, spread_o):
+        ends.append(ends[-1] + item.shape[0])
+    starts = [0, q_heads, q_heads + k_heads, q_heads + 2 * k_heads]
+    plain = [
+        with_transpose(dqkv[:, a * LANES : b * LANES], item[...]).astype(BF16)
+        for a, b, item in zip(starts, starts[1:], (spread_q, spread_k, spread_v))
+    ]
+    plain = jnp.concatenate(plain, axis=1)
+    plain_mixed = with_transpose(mixed[...], spread_o[...]).astype(BF16)
+    other_dresid[:count] = dresid[...]
+
+    def job(i, c):
+        here = lanes(i, TILE)
+        g_attn[here, : ends[3]] = rows_contract(n1[:, here], plain).astype(BF16)
+        g_attn[here, ends[3] :] = rows_contract(other_dresid[:, here], plain_mixed).astype(BF16)
+        return c
+
+    lax.fori_loop(0, jobs, job, 0)
+    attn_task.start()
+
+    def spread(k):
+        return remote(gains_own, gains_all.at[k - 1], g_s.at[k - 1], g_r.at[k - 1], {"tensor": lax.rem(t + k, 4)})
+
+    def steps(line, at):
+        def one(i, c):
+            @pl.when(mine)
+            def _():
+                line.step(i)
+
+            sums(begun + at + i)
+            attn_task.step(at + i - 2, lag)
+            return c
+
+        lax.fori_loop(0, line.steps, one, 0)
+
+    steps(line_a, 0)
+    steps(line_b, line_a.steps)
+    past = line_a.steps + line_b.steps
+    spares[...] = times(holder[...], dx[...]).astype(BF16)
+    back_task.start()
+    section_one = jnp.where(mine, 1.0, 0.0)
+    gains_own[...] = gains[...]
+    gains_own[:1] = gains[:1] + gsum[...] * section_one
+    for k in range(1, 4):
+        spread(k).start()
+    for k in range(1, 4):
+        spread(k).wait()
+    total = gains_own[...] + gains_all[0] + gains_all[1] + gains_all[2]
+    part_width = width // groups
+    for d in range(groups):
+        gains_sum[8 * d : 8 * d + 8, :] = total[:, d * part_width : (d + 1) * part_width]
+    small.start()
+    ending = max(
+        up_task.steps(lag) - begun - past,
+        attn_task.steps(lag) + 2 - past,
+        back_task.steps(2),
+        small.steps(1),
+    )
+
+    def close(i, c):
+        sums(begun + past + i)
+        attn_task.step(past + i - 2, lag)
+        small.step(i, 1)
+        back_task.step(i, 2)
+        return c
+
+    lax.fori_loop(0, ending, close, 0)
+
+    @pl.when(mine)
+    def _():
+        line_a.finish()
+        line_b.finish()
+        for item in scatters:
+            item.finish()
+
+    for item in (up_task, attn_task, back_task, small):
+        item.finish()
+
+
+def last_attn(known, spots, dresid, dx, holder, gains, spreads, grads, weights, groups, q_heads, k_heads, cid):
+    norm_one, wqkv, wout, norm_two, wgate, wup, wdown = weights
+    x, q, kv, lse, mixed, dqkv, other_dresid = known
+    count, width = dresid.shape
+    keys = kv.shape[0]
+    spare = holder.shape[0] // groups
+    pieces, chunks, spare_chunks = 5, 8, spare // 32
+    vmem = pl.BlockSpec(memory_space=pltpu.VMEM)
+    far = pl.BlockSpec(memory_space=pl.ANY)
+    dma = pltpu.SemaphoreType.DMA
+    sources = [wout, wqkv, x, q, kv, lse, mixed, dqkv, other_dresid, *grads]
+    attn_width = sum(item.shape[0] for item in spreads)
+    block = width // groups
+    scratch = [pltpu.VMEM(item.shape, item.dtype) for item in sources]
+    scratch += [
+        pltpu.VMEM((count, width), BF16),
+        pltpu.VMEM(q.shape, BF16),
+        pltpu.VMEM((kv.shape[1], keys), F32),
+        pltpu.VMEM((2 * count, width), BF16),
+        pltpu.VMEM((width, attn_width), BF16),
+        pltpu.VMEM((groups * spare, width), BF16),
+        pltpu.VMEM((1, width), F32),
+        pltpu.VMEM(gains.shape, F32),
+        pltpu.VMEM((3,) + gains.shape, F32),
+        pltpu.VMEM((groups * 8, block), F32),
+        dma((12,)),
+        dma((3,)),
+        dma((3,)),
+    ]
+    for _ in range(k_heads):
+        scratch += [pltpu.VMEM((keys, 2 * LANES), BF16), pltpu.VMEM((count, 2 * LANES), F32)]
+        scratch += OwnScatter.scratch(groups, count, 2 * LANES, 5, BF16)
+    for columns in (grads[0].shape[1], attn_width):
+        scratch += OwnScatter.scratch(groups, block, columns, chunks, BF16)
+    scratch += OwnScatter.scratch(groups, spare, width, spare_chunks, BF16)
+    scratch += OwnScatter.scratch(groups, 8, block, 1, F32)
+    scratch += Line.scratch(count // 4, pieces, width, False) * 2
+    return pl.pallas_call(
+        functools.partial(last_attn_kernel, groups, q_heads, k_heads, pieces, chunks, spare_chunks),
+        out_shape=[
+            jax.ShapeDtypeStruct((count, width), BF16),
+            jax.ShapeDtypeStruct((spare, width), BF16),
+            jax.ShapeDtypeStruct((8, block), F32),
+            jax.ShapeDtypeStruct((block, grads[0].shape[1]), F32),
+            jax.ShapeDtypeStruct((block, attn_width), F32),
+        ],
+        in_specs=[vmem] * 13 + [far] * 11,
+        out_specs=[vmem] * 5,
+        scratch_shapes=scratch,
+        compiler_params=pltpu.CompilerParams(
+            collective_id=cid, has_side_effects=True, vmem_limit_bytes=VMEM_LIMIT
+        ),
+        name="last_attn",
+    )(*spots, norm_one[None], dresid, holder, gains, *spreads, *sources, dx)
+
+
 def rope_tables(pos):
     half_width = HD // 2
     inverse = rope_base ** (-(jnp.arange(half_width, dtype=F32) * 2.0 / HD))
@@ -1100,73 +2166,6 @@
 
     spots = [spots_of(b) for b in range(micro)]
 
-    def spots_at(tick):
-        early, late = spots[min(tick, micro - 1)], spots[max(tick - 1, 0)]
-        return tuple(jnp.where(first, a, b) for a, b in zip(early, late))
-
-    empty = jnp.zeros((count, width), BF16)
-    arriving = empty
-    results, saved = [], []
-    for tick in range(micro + 1):
-        stream = jnp.where(first, packed[tick] if tick < micro else empty, arriving)
-        result, arriving, kept = forward_tick(stream, spots_at(tick), weights, groups, q_heads, k_heads, 0)
-        results.append(result)
-        saved.append(kept)
-    norm_one, norm_two = weights[0], weights[3]
-    arriving = empty
-    grads_in, before, gain_sums = [], [], []
-
-    def all_rows(now, index):
-        old = [item[index] for item in before]
-        return jnp.concatenate([jnp.where(first, now, old[0])] + old[1:], axis=0)
-
-    for tick in range(micro + 1):
-        kept = saved[micro - tick]
-        x, mixed, resid, act = kept[0], kept[4], kept[5], kept[8]
-        incoming = jnp.where(first, arriving, packed[micro - 1 - tick] if tick < micro else empty)
-        d_resid, gain_two, d_gate, d_up = back_ffn(incoming, kept, weights, 1)
-        place = spots_at(micro - tick)
-        if tick < micro:
-            d_stream, gain_one, d_qkv, arriving = back_attn(
-                d_resid, kept, place, weights, groups, q_heads, k_heads, 2, -1
-            )
-            before.append((resid, d_gate, d_up, incoming, act, x, d_qkv, d_resid, mixed))
-        else:
-            n2 = normalize(all_rows(resid, 0), norm_two)
-            grad_gate = rows_contract(n2, all_rows(d_gate, 1)).astype(BF16)
-            grad_up = rows_contract(n2, all_rows(d_up, 2)).astype(BF16)
-            grad_down = rows_contract(all_rows(incoming, 3), all_rows(act, 4)).astype(BF16)
-            ffn_grads = (grad_gate, grad_up, grad_down)
-            beside = len(ffn_grads) if groups * count <= 2048 else 1
-            d_stream, gain_one, d_qkv, *ffn_sums = back_attn(
-                d_resid,
-                kept,
-                place,
-                weights,
-                groups,
-                q_heads,
-                k_heads,
-                3,
-                0,
-                sums=ffn_grads[:beside],
-            )
-            n1 = normalize(all_rows(x, 5), norm_one)
-            back_spread = [(spread_q, 0, q_heads), (spread_k, q_heads, k_heads), (spread_v, q_heads + k_heads, k_heads)]
-            dqkv = all_rows(d_qkv, 6)
-            dqkv = jnp.concatenate(
-                [with_transpose(dqkv[:, i * LANES : (i + n) * LANES], item) for item, i, n in back_spread], axis=1
-            ).astype(BF16)
-            mix = with_transpose(all_rows(mixed, 8), spread_o).astype(BF16)
-            grad_attn = jnp.concatenate(
-                [rows_contract(n1, dqkv).astype(BF16), rows_contract(all_rows(d_resid, 7), mix).astype(BF16)], axis=1
-            )
-        grads_in.append(d_stream)
-        gain_sums.append(jnp.concatenate([gain_one, gain_two], axis=0))
-
-    gains = sum(gain_sums[1:], gain_sums[0])
-    gains = jnp.concatenate([gains, jnp.zeros((6, width), F32)], axis=0)
-    gains = gains.reshape(8, groups, -1).transpose(1, 0, 2).reshape(groups * 8, -1)
-
     def holder(b):
         seq, pos = slots[b]
         row = jnp.arange(groups * spare)[:, None]
@@ -1182,14 +2181,113 @@
     def come_back(rows, b):
         return lax.psum_scatter(spread(rows, b), "dp", scatter_dimension=0, tiled=True)
 
+    norm_one, norm_two = weights[0], weights[3]
+    all_in_one = micro == 2 and groups * count <= 2048
+    empty = jnp.zeros((count, width), BF16)
+
+    def spots_at(tick):
+        early, late = spots[min(tick, micro - 1)], spots[max(tick - 1, 0)]
+        return tuple(jnp.where(first, a, b) for a, b in zip(early, late))
+
+    grads_in, before, gain_sums = [], [], []
+    if all_in_one:
+        joined = [jnp.concatenate(items, axis=0) for items in zip(*spots)]
+        joined[4] = joined[4][:, None]
+        held = jnp.concatenate([holder(b) for b in range(micro)], axis=0).astype(BF16)
+        y, dx, y_back, x, q, kv, lse, mixed, resid, gate, up, act, dy, d_resid, d_gate, d_up, d_qkv, gain_one, gain_two = main_ticks(
+            jnp.concatenate(packed, axis=0), joined, held, weights, groups, q_heads, k_heads, 0
+        )
+        results = [y[:count], y[count:]]
+        first_dresid, gain_last, grad_up, grad_down, grad_gate, back_last = last_ffn(
+            (dy, act, gate, up, d_gate, d_up, resid, d_resid, dx), held[groups * spare :], weights, groups, 1
+        )
+        gain_last = jnp.where(first, gain_last, jnp.zeros_like(gain_last))
+        gains = jnp.concatenate([gain_one, gain_two + gain_last, jnp.zeros((6, width), F32)], axis=0)
+        last_dx, back_first, gains, grad_up, grad_attn = last_attn(
+            (x, q[:count], kv[: groups * count], lse[: q_heads * count], mixed, d_qkv, d_resid),
+            spots[0],
+            first_dresid,
+            dx,
+            held[: groups * spare],
+            gains,
+            (spread_q, spread_k, spread_v, spread_o),
+            (grad_up,),
+            weights,
+            groups,
+            q_heads,
+            k_heads,
+            2,
+        )
+        grads_at = [last_dx, dx[count:]]
+
+    else:
+        arriving = empty
+        results, saved = [], []
+        for tick in range(micro + 1):
+            stream = jnp.where(first, packed[tick] if tick < micro else empty, arriving)
+            result, arriving, kept = forward_tick(stream, spots_at(tick), weights, groups, q_heads, k_heads, 0)
+            results.append(result)
+            saved.append(kept)
+        results = [jnp.where(first, results[b], results[b + 1]) for b in range(micro)]
+        arriving = empty
+        for tick in range(micro):
+            kept = saved[micro - tick]
+            incoming = jnp.where(first, arriving, packed[micro - 1 - tick])
+            d_resid, gain_two, d_gate, d_up = back_ffn(incoming, kept, weights, 1)
+            d_stream, gain_one, d_qkv, arriving = back_attn(
+                d_resid, kept, spots_at(micro - tick), weights, groups, q_heads, k_heads, 2, -1
+            )
+            before.append((kept[5], d_gate, d_up, incoming, kept[8], kept[0], d_qkv, d_resid, kept[4]))
+            grads_in.append(d_stream)
+            gain_sums.append(jnp.concatenate([gain_one, gain_two], axis=0))
+        kept_last = saved[0]
+        last_in, last_spots = jnp.where(first, arriving, empty), spots_at(0)
+        grads_at = [grads_in[micro - 1 - b] if b == 0 else jnp.where(first, grads_in[micro - b], grads_in[micro - 1 - b]) for b in range(micro)]
+
+        def all_rows(now, index):
+            old = [item[index] for item in before]
+            return jnp.concatenate([jnp.where(first, now, old[0])] + old[1:], axis=0)
+
+        x, mixed, resid, act = kept_last[0], kept_last[4], kept_last[5], kept_last[8]
+        d_resid, gain_two, d_gate, d_up = back_ffn(last_in, kept_last, weights, 1)
+        n2 = normalize(all_rows(resid, 0), norm_two)
+        grad_gate = rows_contract(n2, all_rows(d_gate, 1)).astype(BF16)
+        grad_up = rows_contract(n2, all_rows(d_up, 2)).astype(BF16)
+        grad_down = rows_contract(all_rows(last_in, 3), all_rows(act, 4)).astype(BF16)
+        ffn_grads = (grad_gate, grad_up, grad_down)
+        beside = len(ffn_grads) if groups * count <= 2048 else 1
+        d_stream, gain_one, d_qkv, *ffn_sums = back_attn(
+            d_resid, kept_last, last_spots, weights, groups, q_heads, k_heads, 3, 0, sums=ffn_grads[:beside]
+        )
+        n1 = normalize(all_rows(x, 5), norm_one)
+        back_spread = [(spread_q, 0, q_heads), (spread_k, q_heads, k_heads), (spread_v, q_heads + k_heads, k_heads)]
+        dqkv = all_rows(d_qkv, 6)
+        dqkv = jnp.concatenate(
+            [with_transpose(dqkv[:, i * LANES : (i + n) * LANES], item) for item, i, n in back_spread], axis=1
+        ).astype(BF16)
+        mix = with_transpose(all_rows(mixed, 8), spread_o).astype(BF16)
+        grad_attn = jnp.concatenate(
+            [rows_contract(n1, dqkv).astype(BF16), rows_contract(all_rows(d_resid, 7), mix).astype(BF16)], axis=1
+        )
+        grads_at[0] = jnp.where(first, d_stream, grads_at[0])
+        last_gains = jnp.concatenate([gain_one, gain_two], axis=0)
+        gain_sums.append(jnp.where(first, last_gains, jnp.zeros_like(last_gains)))
+
+        gains = sum(gain_sums[1:], gain_sums[0])
+        gains = jnp.concatenate([gains, jnp.zeros((6, width), F32)], axis=0)
+        gains = gains.reshape(8, groups, -1).transpose(1, 0, 2).reshape(groups * 8, -1)
+
     acts = []
     for b in range(micro):
-        rows = jnp.where(first, results[b], results[b + 1])
-        acts.append(unpack(rows, come_back(rows, b), b, inputs[b, 0]))
+        rows = results[b]
+        back = y_back[b * spare : (b + 1) * spare] if all_in_one else come_back(rows, b)
+        acts.append(unpack(rows, back, b, inputs[b, 0]))
     backs = []
     for b in range(micro):
-        rows = jnp.where(first, grads_in[micro - b], grads_in[micro - 1 - b])
-        if b == 0:
+        rows = grads_at[b]
+        if all_in_one:
+            back = back_first if b == 0 else back_last
+        elif b == 0:
             back, gains, grad_attn, *rest = return_rows(
                 spread(rows, b), gains, (grad_attn,) + ffn_grads[beside:], groups, 5, spare // 16
             )

time: 876 us -> 749 us (0.86)
  Pallas kernels: 738 us -> 652 us
  matrix products: 45.9 us -> 8.36 us
  other arithmetic: 39.2 us -> 27.3 us
  local copies, waits for them, and re-layouts: 28.6 us -> 39.1 us
    pallas_call x10 -> x3, Pallas kernels: 714 us -> 627 us  [the longest x1 455 us: main_ticks(): pl.pallas_call(functools.partial(main_kernel, groups, q_heads, k_heads, p...]
    dot_general x6 -> x1, matrix products: 21.4 us -> 2.24 us  [rows_contract(): lax.dot_general(left, right, (((0,), (0,)), ((), ())), preferred_element_...]
    dot_general x7 -> x0, matrix products: 15.8 us -> none  [the longest x4 12.5 us: spread(): jnp.dot(holder(b).astype(BF16), rows, preferred_element_type=F32)]
    select_n x12 -> x0, other arithmetic: 12.7 us -> none  [the longest x7 7.4 us: all_rows(): return jnp.concatenate([jnp.where(first, now, old[0])] + old[1:], axis=0)]
    unnamed x119 -> x45, local copies, waits for them, and re-layouts: 18.1 us -> 17.2 us
  transfers between devices with their start and end apart: 4 -> 1, of which waited for: 0 -> 0; matrix products, arithmetic and copies ran while one was open for 9% -> 3% of each run, Pallas kernels for 75% -> 3%
where the time goes in v3:
time: 749 us; the launch traced here: 741 us
  Pallas kernels  652 us (87%)
  local copies, waits for them, and re-layouts  39.1 us (5%)
  other arithmetic  27.3 us (4%)
  between operations  14.6 us (2%)
  matrix products  8.36 us (1%)
    pallas_call x1, Pallas kernels, main_ticks(): pl.pallas_call(functools.partial(main_kernel, groups, q_heads, k_heads, p...  455 us
    pallas_call x1, Pallas kernels, last_attn(): pl.pallas_call(functools.partial(last_attn_kernel, groups, q_heads, k_hea...  103 us
    pallas_call x1, Pallas kernels, last_ffn(): pl.pallas_call(functools.partial(last_ffn_kernel, groups, pieces, chunks)...  68.6 us
    pallas_call x1, Pallas kernels, gather_rows(): pl.pallas_call(functools.partial(gather_kernel, groups, count), out_shape...  24.5 us
    unnamed x45, local copies, waits for them, and re-layouts  17.2 us
  transfers between devices with their start and end apart: 1, of which 0 were waited for; matrix products, arithmetic and copies ran while one was open for 3% of the time, Pallas kernels for 3%

profile of v3, /device:TPU:0, one launch (start us, length us, event | category | flops | bytes accessed | tf_op | source)
XLA Modules:
  0.0 741.3 jit_solution(11421449562385179080)
XLA Ops:
  7.2 3.2 fusion
  10.5 1.7 copy-done.6
  13.2 24.5 %gather_4.1 = (bf16[768,1536]{1,0:T(8,128)(2,1)S(1)}, f32[32,128]{1,0:T(8,128)S(1)}) custom-call(bf16[192,1536]{1,0:T(8,128)(2,1)S(1)} %get-tuple-element.127.refs_0_, f32[8,128]{1,0:T(8,128)S(1)} %concatenate.102.refs_1_), custom_call_target="tpu_custom_call" | custom-call | tf_op jit(solution)/shard_map/gather_4/pallas_call | solution.py:252
  37.8 1.4 copy-done.2
  44.1 1.3 iota_compare_fusion.14
  57.2 2.2 convolution_convert_fusion.refs_10_.refs_13_
  60.5 1.9 pad_maximum_fusion.refs_9_.refs_14_
  65.4 2.9 fusion.3
  68.3 1.4 pad_maximum_fusion.1.refs_0_
  69.7 455.4 %main_ticks.1 = (bf16[640,1536]{1,0:T(8,128)(2,1)}, bf16[640,1536]{1,0:T(8,128)(2,1)}, bf16[384,1536]{1,0:T(8,128)(2,1)}, bf16[640,1536]{1,0:T(8,128)(2,1)}, bf1...) custom-call(bf16[640,1536]{1,0:T(8,128)(2,1)} %pad_maximum_fusion.1., ...), custom_call_target="tpu_custom_call" | custom-call | tf_op jit(solution)/shard_map/main_ticks/pallas_call | solution.py:1565
  525.1 1.9 slice.96.refs_16_
  527.0 2.0 slice.98.refs_18_
  529.0 2.5 slice.97.refs_17_
  531.5 68.6 %last_ffn.1 = (bf16[320,1536]{1,0:T(8,128)(2,1)}, f32[1,1536]{1,0:T(1,128)}, bf16[1536,1024]{1,0:T(8,128)(2,1)}, f32[384,1024]{1,0:T(8,128)}, f32[384,1024]{1,0:T(8,128)}, /*index=5*/bf16[192,1536]{1,0:T(8,128)(2,1)}) custom-call(f32[1,1536]{1,0:T(1,128)} %refs_0_.1, bf16[768,320]{1,0:T(8,128)(2,1)} %get-tuple-element.136.refs_1_, ...), custom_call_target="tpu_custom_call" | custom-call | tf_op jit(solution)/shard_map/last_ffn/pallas_call | solution.py:1784
  601.5 103.2 %last_attn.1 = (bf16[320,1536]{1,0:T(8,128)(2,1)}, bf16[192,1536]{1,0:T(8,128)(2,1)}, f32[8,384]{1,0:T(8,128)}, f32[384,1024]{1,0:T(8,128)}, f32[384,1152]{1,0:T(8,128)}) custom-call(f32[320,128]{1,0:T(8,128)} %get-tuple-element.140.refs_0_, f32[320,128]{1,0:T(8,128)} %get-tuple-element.139.refs_1_, s32[320,1]{1,0:T(8,128)} %copy.81.refs_2_, ...), custom_call_target="tpu_custom_call" | custom-call | tf_op jit(solution)/shard_map/last_attn/pallas_call | solution.py:2064
  704.8 2.2 slice_bitcast_fusion.10
  707.0 2.3 slice_bitcast_fusion.6
  711.7 1.4 fusion.49
  713.1 2.1 copy.87
  715.2 1.9 copy.86
  717.9 3.0 copy.88
  720.9 6.3 maximum_select_fusion
  727.2 1.9 maximum_bitcast_fusion
  729.2 1.9 maximum_bitcast_fusion.1
  (128 shorter events, 29.5 us)
Async XLA Ops:
  7.2 50.0 %copy-start = (bf16[1,384,1536]{2,1,0:T(8,128)(2,1)S(1)}, bf16[1,384,1536]{2,1,0:T(8,128)(2,1)}, u32[]{:S(2)}) copy-start(bf16[1,384,1536]{2,1,0:T(8,128)(2,1)} %param.19) | copy-start | bytes 3538948
  7.2 58.2 %all-gather.3.cloned.1.call-start = ((), (), s32[]{:S(2)}) async-start(), calls=%async_computation | async-start | bytes 2949120 | tf_op jit(solution)/shard_map/all_gather | solution.py:2156
  10.5 1.7 copy-start.6
  12.2 1.0 copy-start.18
  37.8 1.4 copy-start.2
  42.8 9.4 %copy-start.14 = (s32[1,1280]{1,0:T(1,128)}, s32[1,1280]{1,0:T(1,128)S(1)}, u32[]{:S(2)}) copy-start(s32[1,1280]{1,0:T(1,128)S(1)} %get-tuple-element.149.refs_4_) | copy-start | bytes 15364
  49.9 4.6 copy-start.12
  50.9 4.1 copy-start.13
  55.9 3.5 copy-start.5
  57.2 2.2 copy-start.17
  60.5 2.8 copy-start.3
  60.5 3.7 copy-start.7
  525.1 3.8 copy-start.4
  531.5 68.6 %copy-start.15 = (f32[1,1536]{1,0:T(1,128)S(1)}, f32[1,1536]{1,0:T(1,128)}, u32[]{:S(2)}) copy-start(f32[1,1536]{1,0:T(1,128)} %get-tuple-element.58) | copy-start | bytes 18436
  531.5 69.3 %copy-start.16 = (f32[1,1536]{1,0:T(1,128)S(1)}, f32[1,1536]{1,0:T(1,128)}, u32[]{:S(2)}) copy-start(f32[1,1536]{1,0:T(1,128)} %get-tuple-element.57) | copy-start | bytes 18436
  704.8 4.6 copy-start.8
  709.3 1.3 copy-start.11
  729.2 1.9 copy-start.9
  731.1 2.0 copy-start.10
  731.1 3.1 copy-start.1
Sparse Core Ops, SparseCore 0:
  13.2 31.3 all-gather.2

commit v4 on v3

--- a/solution.py
+++ b/solution.py
@@ -300,12 +300,12 @@
                 bit = self.links[level][1]
                 for slot, goes in self.order(level):
                     self.copy(level, slot, c).wait_recv()
-                    here = self.whole(level, 2 * slot + bit, c)
-                    total = self.value[here].astype(F32) + self.arrive[level][self.at(slot, c)].astype(F32)
+                    here, there = self.whole(level, 2 * slot + bit, c), self.at(slot, c)
                     if level == self.levels - 1:
+                        total = self.value[here].astype(F32) + self.arrive[level][there].astype(F32)
                         self.out[self.at(0, c)] = total.astype(self.out.dtype)
                     else:
-                        self.value[here] = total.astype(self.value.dtype)
+                        self.value[here] = self.value[here] + self.arrive[level][there]
                         if goes:
                             self.copy(level + 1, slot // 2, c).start()
 
@@ -1106,9 +1106,14 @@
         del refs[:count]
         return taken
 
-    packed, cosine, sine, qcode, qstart, kcode, gain_one, gain_two, holder = take(9)
+    cosine, sine, qcode, qstart, kcode, gain_one, gain_two, holder, chosen = take(9)
+    packed, own_second, extra_second = take(3)
     far_weights = take(5)
-    y_out, dx_out, back_out, xs, q, kv, lse, mixed, resid, gate, up, act, dys, dresid, dgate, dup, dqkv, gsum_one, gsum_two = take(19)
+    y_out, dx_out, back_out = take(3)
+    far_state = take(14)
+    gsum_one, gsum_two = take(2)
+    near_state = xs, q, kv, lse, mixed, resid, gate, up, act, dys, dresid, dgate, dup, dqkv = take(14)
+    state_sem = take(1)[0]
     wqkv, wout, wgate, wup, wdown = near_weights = take(5)
     part_one, part_two, normed, y, dmixed, dkv, w_sem, io_sem, meet_sem = take(9)
     levels = dp_bits(groups)
@@ -1119,6 +1124,7 @@
     spare = returned.shape[0]
     give_lag = Line.lag_o + pieces
     give = OwnScatter(groups, spare, spare // 32, [spares, returned] + take(OwnScatter.refs(groups)))
+    second = Gather(groups, spare, spares, *take(2))
     count, width = part_one.shape
     keys = groups * count
     quarter = count // 4
@@ -1154,33 +1160,40 @@
 
     loads = load_all(list(zip(far_weights, near_weights)), w_sem)
 
-    def fetch(slot, target):
-        place = span(slot * count, count)
-        return pltpu.make_async_copy(packed.at[place], target.at[place], io_sem.at[slot])
-
-    for slot in range(2):
-
-        @pl.when(section == 0)
-        def _():
-            fetch(slot, xs).start()
-
-        @pl.when(section == 1)
-        def _():
-            fetch(slot, dys).start()
+    def fetch(target):
+        return (
+            pltpu.make_async_copy(packed, target.at[:count], io_sem.at[0]),
+            pltpu.make_async_copy(own_second, target.at[count:], io_sem.at[1]),
+        )
+
+    place = span(lax.axis_index("dp") * spare, spare)
+    fetch_extra = pltpu.make_async_copy(extra_second, spares.at[place], io_sem.at[2])
+    fetch_extra.start()
+    for which, target in enumerate((xs, dys)):
+
+        @pl.when(section == which)
+        def _():
+            for item in fetch(target):
+                item.start()
 
     pl.semaphore_wait(pltpu.get_barrier_semaphore(), jnp.where(jnp.logical_or(t == 1, t == 2), 2, 1) + levels + 1)
     announce(meet_sem, neighbours)
     gsum_one[...] = jnp.zeros_like(gsum_one)
     gsum_two[...] = jnp.zeros_like(gsum_two)
-    for slot in range(2):
-
-        @pl.when(section == 0)
-        def _():
-            fetch(slot, xs).wait()
-
-        @pl.when(section == 1)
-        def _():
-            fetch(slot, dys).wait()
+    for which, target in enumerate((xs, dys)):
+
+        @pl.when(section == which)
+        def _():
+            for item in fetch(target):
+                item.wait()
+
+    fetch_extra.wait()
+
+    def keep(index, slot):
+        near, there = near_state[index], far_state[index]
+        part = near.shape[0] // 2
+        here = span(slot * part, part)
+        return pltpu.make_async_copy(near.at[here], there.at[here], state_sem.at[index, slot])
 
     def projected(target, left, right, first, left_at, each=None):
         here, there = span(first, half), span(first + left_at, half)
@@ -1275,6 +1288,10 @@
             if level:
                 gather.start(level - 1)
 
+        @pl.when(slot == 0)
+        def _():
+            second.start(levels - 1)
+
         def attend(first, each=None):
             def one(i, c):
                 h, b = i // blocks, lax.rem(i, blocks)
@@ -1315,6 +1332,9 @@
         def _():
             for item in loads[2:]:
                 item.wait()
+            for level in range(levels - 1, 0, -1):
+                second.arrive(level)
+                second.start(level - 1)
 
         def hidden(first, each):
             here, there = span(first, half), span(base + first, half)
@@ -1339,6 +1359,17 @@
         hidden(half, two_a.step)
         projected(part_two, act, wdown, half, base)
         two_b.start()
+
+        @pl.when(slot == 0)
+        def _():
+            second.arrive(0)
+            brought = times(chosen[...], spares[...])
+            for which, target in enumerate((xs, dys)):
+
+                @pl.when(section == which)
+                def _():
+                    target[count:] = (target[count:].astype(F32) + brought).astype(BF16)
+
         run_steps(tiles, two_a.steps, (two_a.step, 0))
         run_steps(0, two_b.steps, (two_b.step, 0))
         out = pltpu.make_async_copy(y, y_out.at[whole], io_sem.at[0])
@@ -1347,7 +1378,14 @@
         for line in lines:
             line.finish()
         given(0, slot == 1)
+
+        @pl.when(slot == 0)
+        def _():
+            second.finish()
+
         out.wait()
+        for index in range(9):
+            keep(index, slot).start()
         announce(meet_sem, neighbours)
         return carry
 
@@ -1491,6 +1529,8 @@
             item.finish()
         given(1, tick == 0)
         out.wait()
+        for index in range(9, 14):
+            keep(index, slot).start()
         announce(meet_sem, neighbours)
         return carry
 
@@ -1507,11 +1547,26 @@
             list(line_scratch[2 + k]) + [back_s.at[k], back_r.at[k]],
             moved=(dys, -1),
         ).receive()
-
-
-def main_ticks(packed, spots, holder, weights, groups, q_heads, k_heads, cid):
+    for index in range(14):
+        keep(index, 1).wait()
+        if index < 9:
+            keep(index, 0).wait()
+
+    @pl.when(section > 0)
+    def _():
+        for index in range(9, 14):
+            keep(index, 0).wait()
+
+    @pl.when(section == 0)
+    def _():
+        keep(9, 0).start()
+        keep(9, 0).wait()
+
+
+def main_ticks(packed, second, spots, holder, weights, groups, q_heads, k_heads, cid):
     norm_one, wqkv, wout, norm_two, wgate, wup, wdown = weights
-    count, width = packed.shape[0] // 2, packed.shape[1]
+    count, width = packed.shape
+    own_second, extra_second, chosen = second
     hidden, keys = wgate.shape[1], groups * count
     pieces = 5
     vmem = pl.BlockSpec(memory_space=pltpu.VMEM)
@@ -1527,6 +1582,8 @@
         shape(width),
         shape(width),
         shape(width, 2 * spare),
+    ]
+    state = [
         shape(width),
         shape(heads),
         shape(2 * k_heads * LANES, 2 * keys),
@@ -1541,16 +1598,16 @@
         shape(hidden),
         shape(hidden),
         shape(both),
-        shape(width, 1, F32),
-        shape(width, 1, F32),
     ]
+    outs += state + [shape(width, 1, F32)] * 2
     far_weights = [wqkv, wout, wgate, wup, wdown]
-    scratch = [pltpu.VMEM(item.shape, BF16) for item in far_weights]
+    scratch = [pltpu.VMEM(item.shape, item.dtype) for item in state] + [dma((14, 2))]
+    scratch += [pltpu.VMEM(item.shape, BF16) for item in far_weights]
     scratch += [pltpu.VMEM((count, width), BF16)] * 4 + [
         pltpu.VMEM((count, heads), BF16),
         pltpu.VMEM((2 * k_heads * LANES, keys), F32),
         dma((5,)),
-        dma((2,)),
+        dma((3,)),
         pltpu.SemaphoreType.REGULAR((2 + dp_bits(groups),)),
     ]
     scratch += Gather.scratch(groups)
@@ -1559,20 +1616,21 @@
     scratch += [dma((2, 2, pieces)), dma((4, 2, pieces))] * 2
     scratch += [pltpu.VMEM((groups * spare, width), BF16), pltpu.VMEM((spare, width), BF16)]
     scratch += OwnScatter.scratch(groups, spare, width, spare // 32, BF16)
+    scratch += Gather.scratch(groups)
     for _ in range(k_heads):
         scratch += [pltpu.VMEM((keys, 2 * LANES), BF16), pltpu.VMEM((count, 2 * LANES), F32)]
         scratch += Scatter.scratch(groups, count, 2 * LANES, 5, BF16)
     return pl.pallas_call(
         functools.partial(main_kernel, groups, q_heads, k_heads, pieces),
         out_shape=outs,
-        in_specs=[far] + [vmem] * 8 + [far] * 5,
-        out_specs=[far] * 3 + [vmem] * (len(outs) - 3),
+        in_specs=[vmem] * 9 + [far] * 8,
+        out_specs=[far] * (len(outs) - 2) + [vmem] * 2,
         scratch_shapes=scratch,
         compiler_params=pltpu.CompilerParams(
             collective_id=cid, has_side_effects=True, vmem_limit_bytes=VMEM_LIMIT
         ),
         name="main_ticks",
-    )(packed, *spots, norm_one[None], norm_two[None], holder, *far_weights)
+    )(*spots, norm_one[None], norm_two[None], holder, chosen, packed, own_second, extra_second, *far_weights)
 
 
 def quarter_rows(count):
@@ -1592,11 +1650,11 @@
         del refs[:count]
         return taken
 
-    gain, holder = take(2)
-    sources = take(12)
-    first_dresid, gsum, g_up, down_sum, gate_sum, returned = take(6)
+    (gain,) = take(1)
+    sources = take(11)
+    first_dresid, gsum, g_up, down_sum, gate_sum = take(5)
     wdown, wgate, wup, dys, act, gate, up, dgate, dup, resid = kept = take(10)
-    n2, part, g_down, g_gate, spares, dx, w_sem = take(7)
+    n2, part, g_down, g_gate, w_sem = take(5)
     (scratch,) = (take(12),)
     count, width = part.shape
     half = count // 2
@@ -1606,8 +1664,6 @@
     ]
     down = OwnScatter(groups, width // groups, chunks, [g_down, down_sum] + take(OwnScatter.refs(groups)))
     gated = OwnScatter(groups, width // groups, chunks, [g_gate, gate_sum] + take(OwnScatter.refs(groups)))
-    spare = returned.shape[0]
-    give = OwnScatter(groups, spare, spare // 32, [spares, returned] + take(OwnScatter.refs(groups)))
     section = lax.axis_index("section")
     mine = section == 0
     tiles, wide, blocks = act.shape[1] // WIDE, width // WIDE, width // TILE
@@ -1622,12 +1678,8 @@
         pltpu.make_async_copy(sources[8].at[:count], kept[8].at[:count], w_sem.at[11]),
         pltpu.make_async_copy(sources[10].at[:count], first_dresid, w_sem.at[12]),
     ]
-    last_dx = pltpu.make_async_copy(sources[11].at[count:], dx, w_sem.at[13])
     loads = [load(k) for k in range(10)]
-    for k in (3, 0, 5, 6, 1, 2):
-        loads[k].start()
-    last_dx.start()
-    for k in (4, 9, 7, 8):
+    for k in (3, 0, 5, 6, 1, 2, 4, 9, 7, 8):
         loads[k].start()
 
     @pl.when(section > 0)
@@ -1681,9 +1733,14 @@
         back(0)
         line_a.start()
 
-    last_dx.wait()
-    spares[...] = times(holder[...], dx[...]).astype(BF16)
-    give.start()
+    loads[4].wait()
+
+    def down_job(i, c):
+        weight_job(g_down, dys, act, i)
+        return c
+
+    lax.fori_loop(0, blocks, down_job, 0)
+    down.start()
 
     @pl.when(mine)
     def _():
@@ -1691,30 +1748,17 @@
         back(half)
         line_b.start()
 
-    for k in (4, 9, 7, 8):
+    for k in (9, 7, 8):
         loads[k].wait()
-
-    kinds = ((g_down, dys, act), (g_gate, n2, dgate), (g_up, n2, dup))
-
-    def job(k):
-        for which, (target, left, right) in enumerate(kinds):
-
-            @pl.when(k // blocks == which)
-            def _():
-                weight_job(target, left, right, lax.rem(k, blocks))
-
-    normalize_into(n2, resid, gain, 0, 2 * count)
-    for k in range(2):
-        job(k)
 
     @pl.when(section > 0)
     def _():
         lacks[0].wait()
         lacks[1].wait()
 
-    lag = 4
-    first_part = blocks - 2
-    begin_down, begin_gate = first_part, first_part + blocks
+    late = 100
+    spans = 5
+    norm_rows = 2 * count // spans
 
     def step(i, c):
         @pl.when(mine)
@@ -1722,27 +1766,30 @@
             line_a.step(i)
             line_b.step(i - line_a.steps)
 
-        @pl.when(i + 2 < 3 * blocks)
-        def _():
-            job(i + 2)
-
-        @pl.when(i == begin_down - 1)
-        def _():
-            down.start()
-
-        @pl.when(i == begin_gate - 1)
+        down.step(i, late)
+
+        @pl.when(i < spans)
+        def _():
+            normalize_into(n2, resid, gain, i * norm_rows, norm_rows)
+
+        @pl.when(jnp.logical_and(i >= spans, i < spans + blocks))
+        def _():
+            weight_job(g_gate, n2, dgate, i - spans)
+
+        @pl.when(i == spans + blocks - 1)
         def _():
             gated.start()
 
-        give.step(i, 6)
-        down.step(i - begin_down, lag)
-        gated.step(i - begin_gate, lag)
+        gated.step(i - spans - blocks, late)
+
+        @pl.when(jnp.logical_and(i >= spans + blocks, i < spans + 2 * blocks))
+        def _():
+            weight_job(g_up, n2, dup, i - spans - blocks)
+
         return c
 
-    ending = max(
-        line_a.steps + line_b.steps, 3 * blocks - 2, begin_down + down.steps(lag), begin_gate + gated.steps(lag), give.steps(6)
-    )
-    lax.fori_loop(0, ending, step, 0)
+    lax.fori_loop(0, max(line_a.steps + line_b.steps, spans + 2 * blocks, spans + blocks + chunks), step, 0)
+    run_steps(late, late + chunks, (lambda i: down.step(i, late), 0), (lambda i: gated.step(i, late), 0))
 
     @pl.when(mine)
     def _():
@@ -1753,15 +1800,13 @@
     def _():
         lacks[2].wait()
 
-    give.finish()
     down.finish()
     gated.finish()
 
 
-def last_ffn(known, holder, weights, groups, cid):
+def last_ffn(known, weights, groups, cid):
     norm_one, wqkv, wout, norm_two, wgate, wup, wdown = weights
-    dys, act, gate, up, dgate, dup, resid, dresid, dx = known
-    spare = holder.shape[0] // groups
+    dys, act, gate, up, dgate, dup, resid, dresid = known
     count, width = dys.shape[0] // 2, dys.shape[1]
     hidden = act.shape[1]
     pieces, chunks = 5, 8
@@ -1774,13 +1819,10 @@
         pltpu.VMEM((count, width), BF16),
         pltpu.VMEM((width, hidden), BF16),
         pltpu.VMEM((width, hidden), BF16),
-        pltpu.VMEM((groups * spare, width), BF16),
-        pltpu.VMEM((count, width), BF16),
-        pltpu.SemaphoreType.DMA((14,)),
+        pltpu.SemaphoreType.DMA((13,)),
     ]
     scratch += Line.scratch(count // 4, pieces, width, False) * 2
     scratch += OwnScatter.scratch(groups, width // groups, hidden, chunks, BF16) * 2
-    scratch += OwnScatter.scratch(groups, spare, width, spare // 32, BF16)
     return pl.pallas_call(
         functools.partial(last_ffn_kernel, groups, pieces, chunks),
         out_shape=[
@@ -1789,16 +1831,15 @@
             jax.ShapeDtypeStruct((width, hidden), BF16),
             jax.ShapeDtypeStruct((width // groups, hidden), F32),
             jax.ShapeDtypeStruct((width // groups, hidden), F32),
-            jax.ShapeDtypeStruct((spare, width), BF16),
         ],
-        in_specs=[vmem] * 2 + [far] * 12,
-        out_specs=[vmem] * 6,
+        in_specs=[vmem] + [far] * 11,
+        out_specs=[vmem] * 5,
         scratch_shapes=scratch,
         compiler_params=pltpu.CompilerParams(
             collective_id=cid, has_side_effects=True, vmem_limit_bytes=VMEM_LIMIT
         ),
         name="last_ffn",
-    )(norm_two[None], holder, *sources, dresid, dx)
+    )(norm_two[None], *sources, dresid)
 
 
 def last_attn_kernel(groups, q_heads, k_heads, pieces, chunks, spare_chunks, *refs):
@@ -1812,9 +1853,10 @@
     cosine, sine, qcode, qstart, kcode, gain, dresid, holder, gains, spread_q, spread_k, spread_v, spread_o = take(13)
     sources = take(10)
     (dx_known,) = take(1)
-    dx, returned, gains_out, up_sum, attn_sum = take(5)
+    dx, returned, returned_second, gains_out, up_sum, attn_sum = take(6)
     wout, wqkv, x, q, kv, lse, mixed, dqkv, other_dresid, g_up = kept = take(10)
-    part, dmixed, dkv, n1, g_attn, spares, gsum, gains_own, gains_all, gains_sum, w_sem, g_s, g_r = take(13)
+    plain, plain_mixed = take(2)
+    part, dmixed, dkv, n1, g_attn, spares, spares_second, gsum, gains_own, gains_all, gains_sum, w_sem, g_s, g_r = take(14)
     levels = dp_bits(groups)
     count, width = part.shape
     half = count // 2
@@ -1832,6 +1874,7 @@
     ]
     spare = spares.shape[0] // groups
     back_task = OwnScatter(groups, spare, spare_chunks, [spares, returned] + take(OwnScatter.refs(groups)))
+    give = OwnScatter(groups, spare, spare_chunks, [spares_second, returned_second] + take(OwnScatter.refs(groups)))
     small = OwnScatter(groups, 8, 1, [gains_sum, gains_out] + take(OwnScatter.refs(groups)))
     line_a, line_b = [
         Line(k * half, half // 2, pieces, part, dresid, dx, take(12), norm=(x, gain, gsum)) for k in range(2)
@@ -1839,10 +1882,12 @@
     section, t = lax.axis_index("section"), lax.axis_index("tensor")
     mine = section == 0
     order = [9, 0, 3, 4, 5, 1, 2, 6, 7, 8]
-    loads = [pltpu.make_async_copy(sources[k], kept[k], w_sem.at[k]) for k in range(10)]
+    loads = [pltpu.make_async_copy(sources[k].at[: kept[k].shape[0]], kept[k], w_sem.at[k]) for k in range(10)]
     for k in order:
         loads[k].start()
     known = pltpu.make_async_copy(dx_known.at[:count], dx, w_sem.at[11])
+    second = pltpu.make_async_copy(dx_known.at[count:], part, w_sem.at[10])
+    second.start()
 
     @pl.when(section > 0)
     def _():
@@ -1866,17 +1911,13 @@
     blocks = half // rows
     turns = repeat * blocks
     scale = HD ** (-0.5)
-    lag = 6
-
-    begun = k_heads * turns
+    late = 100
+    begun = 2 * k_heads * turns
 
     def early(i):
-        @pl.when(lax.rem(i, 2) == 0)
-        def _():
-            up_task.step(i // 2, lag)
-
-    def sums(i):
-        up_task.step(i, lag)
+        @pl.when(lax.rem(i, 2) == 1)
+        def _():
+            up_task.step(i // 2, late)
 
     def mix(first):
         here = pl.ds(first, half)
@@ -1929,7 +1970,35 @@
             shares[g][:, :LANES] = jnp.transpose(dkv[lanes(g), :]).astype(BF16)
             shares[g][:, LANES:] = jnp.transpose(dkv[lanes(k_heads + g), :]).astype(BF16)
             scatters[g].start()
-        run_steps(0, scatters[0].steps(1), *[(functools.partial(lambda s, i: s.step(i, 1), s), 0) for s in scatters])
+        run_steps(0, scatters[0].chunks, *[(functools.partial(lambda s, i: s.step(i, late), s), 0) for s in scatters])
+
+    @pl.when(section > 0)
+    def _():
+        run_steps(0, begun, (early, 0))
+        known.wait()
+
+    ends = [0]
+    for item in (spread_q, spread_k, spread_v, spread_o):
+        ends.append(ends[-1] + item.shape[0])
+    starts = [0, q_heads, q_heads + k_heads, q_heads + 2 * k_heads]
+    second.wait()
+    spares_second[...] = times(holder[groups * spare :], part[...]).astype(BF16)
+    give.start()
+    normalize_into(n1, x, gain, 0, 2 * count)
+    plain_mixed[...] = with_transpose(mixed[...], spread_o[...]).astype(BF16)
+    other_dresid[:count] = dresid[...]
+
+    def out_job(i, c):
+        here = lanes(i, TILE)
+        g_attn[here, ends[3] :] = rows_contract(other_dresid[:, here], plain_mixed[...]).astype(BF16)
+        return c
+
+    lax.fori_loop(0, jobs, out_job, 0)
+
+    @pl.when(mine)
+    def _():
+        ending = late + scatters[0].chunks
+        run_steps(late, ending, *[(functools.partial(lambda s, i: s.step(i, late), s), 0) for s in scatters])
         for g in range(k_heads):
             dqkv[:count, lanes(q_heads + g)] = rolled(owns[g][:, :LANES], cosine[...], -sine[...]).astype(BF16)
             dqkv[:count, lanes(q_heads + k_heads + g)] = owns[g][:, LANES:].astype(BF16)
@@ -1938,52 +2007,41 @@
         back(half)
         line_b.start()
 
-    @pl.when(section > 0)
-    def _():
-        run_steps(0, begun, (sums, 0))
-        known.wait()
-
-    normalize_into(n1, x, gain, 0, 2 * count)
-    ends = [0]
-    for item in (spread_q, spread_k, spread_v, spread_o):
-        ends.append(ends[-1] + item.shape[0])
-    starts = [0, q_heads, q_heads + k_heads, q_heads + 2 * k_heads]
-    plain = [
-        with_transpose(dqkv[:, a * LANES : b * LANES], item[...]).astype(BF16)
-        for a, b, item in zip(starts, starts[1:], (spread_q, spread_k, spread_v))
-    ]
-    plain = jnp.concatenate(plain, axis=1)
-    plain_mixed = with_transpose(mixed[...], spread_o[...]).astype(BF16)
-    other_dresid[:count] = dresid[...]
-
-    def job(i, c):
-        here = lanes(i, TILE)
-        g_attn[here, : ends[3]] = rows_contract(n1[:, here], plain).astype(BF16)
-        g_attn[here, ends[3] :] = rows_contract(other_dresid[:, here], plain_mixed).astype(BF16)
-        return c
-
-    lax.fori_loop(0, jobs, job, 0)
-    attn_task.start()
-
     def spread(k):
         return remote(gains_own, gains_all.at[k - 1], g_s.at[k - 1], g_r.at[k - 1], {"tensor": lax.rem(t + k, 4)})
 
-    def steps(line, at):
-        def one(i, c):
-            @pl.when(mine)
-            def _():
-                line.step(i)
-
-            sums(begun + at + i)
-            attn_task.step(at + i - 2, lag)
-            return c
-
-        lax.fori_loop(0, line.steps, one, 0)
-
-    steps(line_a, 0)
-    steps(line_b, line_a.steps)
-    past = line_a.steps + line_b.steps
-    spares[...] = times(holder[...], dx[...]).astype(BF16)
+    first_job = begun // 2
+
+    def step(i, c):
+        @pl.when(mine)
+        def _():
+            line_a.step(i)
+            line_b.step(i - line_a.steps)
+
+        up_task.step(i + first_job, late)
+
+        @pl.when(i == 0)
+        def _():
+            for a, b, n, item in zip(starts, starts[1:], ends, (spread_q, spread_k, spread_v)):
+                plain[:, n : n + item.shape[0]] = with_transpose(
+                    dqkv[:, a * LANES : b * LANES], item[...]
+                ).astype(BF16)
+
+        @pl.when(jnp.logical_and(i >= 1, i <= jobs))
+        def _():
+            here = lanes(jnp.clip(i - 1, 0, jobs - 1), TILE)
+            g_attn[here, : ends[3]] = rows_contract(n1[:, here], plain[...]).astype(BF16)
+
+        @pl.when(i == jobs)
+        def _():
+            attn_task.start()
+
+        give.step(i - first_job, late)
+        attn_task.step(i - jobs - 1, late)
+        return c
+
+    lax.fori_loop(0, max(line_a.steps + line_b.steps, jobs + 1 + chunks), step, 0)
+    spares[...] = times(holder[: groups * spare], dx[...]).astype(BF16)
     back_task.start()
     section_one = jnp.where(mine, 1.0, 0.0)
     gains_own[...] = gains[...]
@@ -1997,21 +2055,17 @@
     for d in range(groups):
         gains_sum[8 * d : 8 * d + 8, :] = total[:, d * part_width : (d + 1) * part_width]
     small.start()
-    ending = max(
-        up_task.steps(lag) - begun - past,
-        attn_task.steps(lag) + 2 - past,
-        back_task.steps(2),
-        small.steps(1),
-    )
 
     def close(i, c):
-        sums(begun + past + i)
-        attn_task.step(past + i - 2, lag)
-        small.step(i, 1)
-        back_task.step(i, 2)
+        back_task.step(i, late)
+        small.step(i, 2)
+        up_task.step(late + i, late)
+        attn_task.step(late + i, late)
+        give.step(late + i, late)
         return c
 
-    lax.fori_loop(0, ending, close, 0)
+    lax.fori_loop(0, max(chunks, spare_chunks, small.steps(2)), close, 0)
+    run_steps(late, late + spare_chunks, (lambda i: back_task.step(i, late), 0))
 
     @pl.when(mine)
     def _():
@@ -2020,7 +2074,7 @@
         for item in scatters:
             item.finish()
 
-    for item in (up_task, attn_task, back_task, small):
+    for item in (up_task, attn_task, back_task, give, small):
         item.finish()
 
 
@@ -2028,8 +2082,8 @@
     norm_one, wqkv, wout, norm_two, wgate, wup, wdown = weights
     x, q, kv, lse, mixed, dqkv, other_dresid = known
     count, width = dresid.shape
-    keys = kv.shape[0]
-    spare = holder.shape[0] // groups
+    keys = groups * count
+    spare = holder.shape[0] // (2 * groups)
     pieces, chunks, spare_chunks = 5, 8, spare // 32
     vmem = pl.BlockSpec(memory_space=pltpu.VMEM)
     far = pl.BlockSpec(memory_space=pl.ANY)
@@ -2037,13 +2091,19 @@
     sources = [wout, wqkv, x, q, kv, lse, mixed, dqkv, other_dresid, *grads]
     attn_width = sum(item.shape[0] for item in spreads)
     block = width // groups
-    scratch = [pltpu.VMEM(item.shape, item.dtype) for item in sources]
+    first_only = {3: count, 4: keys, 5: q_heads * count}
+    scratch = [
+        pltpu.VMEM((first_only.get(k, item.shape[0]),) + item.shape[1:], item.dtype) for k, item in enumerate(sources)
+    ]
     scratch += [
+        pltpu.VMEM((2 * count, attn_width - spreads[3].shape[0]), BF16),
+        pltpu.VMEM((2 * count, spreads[3].shape[0]), BF16),
         pltpu.VMEM((count, width), BF16),
-        pltpu.VMEM(q.shape, BF16),
+        pltpu.VMEM((count, q.shape[1]), BF16),
         pltpu.VMEM((kv.shape[1], keys), F32),
         pltpu.VMEM((2 * count, width), BF16),
         pltpu.VMEM((width, attn_width), BF16),
+        pltpu.VMEM((groups * spare, width), BF16),
         pltpu.VMEM((groups * spare, width), BF16),
         pltpu.VMEM((1, width), F32),
         pltpu.VMEM(gains.shape, F32),
@@ -2058,7 +2118,7 @@
         scratch += OwnScatter.scratch(groups, count, 2 * LANES, 5, BF16)
     for columns in (grads[0].shape[1], attn_width):
         scratch += OwnScatter.scratch(groups, block, columns, chunks, BF16)
-    scratch += OwnScatter.scratch(groups, spare, width, spare_chunks, BF16)
+    scratch += OwnScatter.scratch(groups, spare, width, spare_chunks, BF16) * 2
     scratch += OwnScatter.scratch(groups, 8, block, 1, F32)
     scratch += Line.scratch(count // 4, pieces, width, False) * 2
     return pl.pallas_call(
@@ -2066,18 +2126,136 @@
         out_shape=[
             jax.ShapeDtypeStruct((count, width), BF16),
             jax.ShapeDtypeStruct((spare, width), BF16),
+            jax.ShapeDtypeStruct((spare, width), BF16),
             jax.ShapeDtypeStruct((8, block), F32),
             jax.ShapeDtypeStruct((block, grads[0].shape[1]), F32),
             jax.ShapeDtypeStruct((block, attn_width), F32),
         ],
         in_specs=[vmem] * 13 + [far] * 11,
-        out_specs=[vmem] * 5,
+        out_specs=[vmem] * 6,
         scratch_shapes=scratch,
         compiler_params=pltpu.CompilerParams(
             collective_id=cid, has_side_effects=True, vmem_limit_bytes=VMEM_LIMIT
         ),
         name="last_attn",
     )(*spots, norm_one[None], dresid, holder, gains, *spreads, *sources, dx)
+
+
+def finish_kernel(groups, parts, *refs):
+    refs = list(refs)
+
+    def take(count):
+        taken = refs[:count]
+        del refs[:count]
+        return taken
+
+    (live,) = take(1)
+    through, y, y_back, cot, dx_first, dx_second, back_first, back_second = take(8)
+    gate, up, down, attn = take(4)
+    acts, backs = take(2)
+    outs = take(7)
+    tiles = take(4)
+    rows = take(4)
+    backs_near = take(4)
+    down_near, down_turned, attn_near, *attn_parts = take(7)
+    plain_near = take(2)
+    sems, out_sems = take(2)
+    count, spare = rows[0].shape[0], backs_near[0].shape[0]
+    seq = count + spare
+    whole = [
+        (through.at[0, 0], y.at[:count], y_back.at[:spare], acts.at[0, 0, 0]),
+        (through.at[1, 0], y.at[count:], y_back.at[spare:], acts.at[0, 1, 0]),
+        (cot.at[0, 0], dx_first, back_first, backs.at[0, 0, 0]),
+        (cot.at[1, 0], dx_second.at[count:], back_second, backs.at[0, 1, 0]),
+    ]
+    query_out, key_out, value_out, out_out, gate_out, up_out, down_out = outs
+    plain_in = [pltpu.make_async_copy(a, b, sems.at[14 + k]) for k, (a, b) in enumerate(zip((gate, up), plain_near))]
+    plain = [pltpu.make_async_copy(a, b, out_sems.at[k]) for k, (a, b) in enumerate(zip(plain_near, (gate_out.at[0], up_out.at[0])))]
+    load_down = pltpu.make_async_copy(down, down_near, sems.at[12])
+    load_attn = pltpu.make_async_copy(attn, attn_near, sems.at[13])
+    loads = []
+    for k, (a, b, c, _) in enumerate(whole):
+        loads.append(
+            [
+                pltpu.make_async_copy(src, dst, sems.at[3 * k + n])
+                for n, (src, dst) in enumerate(((a, tiles[k]), (b, rows[k]), (c, backs_near[k])))
+            ]
+        )
+    load_attn.start()
+    load_down.start()
+    for item in plain_in:
+        item.start()
+    for group in loads:
+        for item in group:
+            item.start()
+    stores = []
+    load_attn.wait()
+    at = 0
+    for k, (size, near, there) in enumerate(zip(parts, attn_parts, (query_out, key_out, value_out, out_out))):
+        value = attn_near[:, at : at + size]
+        near[...] = value if k == 0 else jnp.transpose(value)
+        at += size
+        stores.append(pltpu.make_async_copy(near, there.at[0], out_sems.at[2 + k]))
+        stores[-1].start()
+    for before, item in zip(plain_in, plain):
+        before.wait()
+        item.start()
+    load_down.wait()
+    down_turned[...] = jnp.transpose(down_near[...])
+    stores.append(pltpu.make_async_copy(down_turned, down_out.at[0], out_sems.at[6]))
+    stores[-1].start()
+    for k, group in enumerate(loads):
+        for item in group:
+            item.wait()
+        first = (k % 2) * seq
+
+        def one(i, c):
+            here = pl.ds(pl.multiple_of(i * 64, 64), 64)
+            alive = live[pl.ds(pl.multiple_of(first + i * 64, 64), 64)] > 0
+            tiles[k][here] = jnp.where(alive, rows[k][here], tiles[k][here])
+            return c
+
+        lax.fori_loop(0, count // 64, one, 0)
+
+        def two(i, c):
+            near = pl.ds(pl.multiple_of(i * 64, 64), 64)
+            here = pl.ds(pl.multiple_of(count + i * 64, 64), 64)
+            alive = live[pl.ds(pl.multiple_of(first + count + i * 64, 64), 64)] > 0
+            tiles[k][here] = jnp.where(alive, backs_near[k][near], tiles[k][here])
+            return c
+
+        lax.fori_loop(0, spare // 64, two, 0)
+        stores.append(pltpu.make_async_copy(tiles[k], whole[k][3], out_sems.at[7 + k]))
+        stores[-1].start()
+    for item in stores + plain:
+        item.wait()
+
+
+def finish(live, through, y, y_back, cot, dx_first, dx_second, back_first, back_second, grads, parts, groups):
+    count, width = dx_first.shape
+    spare = back_first.shape[0]
+    gate, up, down, attn = grads
+    block, hidden = down.shape
+    vmem = pl.BlockSpec(memory_space=pltpu.VMEM)
+    far = pl.BlockSpec(memory_space=pl.ANY)
+    shapes = [(block, parts[0])] + [(size, block) for size in parts[1:]]
+    outs = [jax.ShapeDtypeStruct((1, 2, 1, count + spare, width), BF16)] * 2
+    outs += [jax.ShapeDtypeStruct((1,) + item, F32) for item in shapes + [gate.shape, up.shape, (hidden, block)]]
+    scratch = [pltpu.VMEM((count + spare, width), BF16)] * 4
+    scratch += [pltpu.VMEM((count, width), BF16)] * 4 + [pltpu.VMEM((spare, width), BF16)] * 4
+    scratch += [pltpu.VMEM(down.shape, F32), pltpu.VMEM((hidden, block), F32), pltpu.VMEM(attn.shape, F32)]
+    scratch += [pltpu.VMEM(item, F32) for item in shapes]
+    scratch += [pltpu.VMEM(gate.shape, F32), pltpu.VMEM(up.shape, F32)]
+    scratch += [pltpu.SemaphoreType.DMA((16,)), pltpu.SemaphoreType.DMA((11,))]
+    return pl.pallas_call(
+        functools.partial(finish_kernel, groups, parts),
+        out_shape=outs,
+        in_specs=[vmem] + [far] * 12,
+        out_specs=[far] * 9,
+        scratch_shapes=scratch,
+        compiler_params=pltpu.CompilerParams(vmem_limit_bytes=VMEM_LIMIT),
+        name="finish",
+    )(live, through, y, y_back, cot, dx_first, dx_second, back_first, back_second, gate, up, down, attn)
 
 
 def rope_tables(pos):
@@ -2144,20 +2322,27 @@
     wout = rows_contract(spread_o, w_out[0]).astype(BF16)
     weights = (norm_attn[0], wqkv, wout, norm_ffn[0], w_gate[0], w_up[0], w_down[0])
 
+    all_in_one = micro == 2 and groups == 4
+
     source = jnp.where(first, inputs[:, 0], cotangent[:, 0])
-    length_rows = jnp.broadcast_to(lengths[:, 0].astype(F32)[:, None], (micro, 128))
-    length_rows = jnp.concatenate([length_rows, jnp.zeros((8 - micro, 128), F32)], axis=0)
-    first_extra, length_all = gather_rows([source[0, count:], length_rows], groups, 4)
-    lens = length_all.reshape(groups, 8, 128)[:, :micro, 0].T.astype(jnp.int32)
-    packed, slots = [], []
+    first_extra = lax.all_gather(source[0, count:], "dp", axis=0, tiled=True)
+    length_rows = jnp.broadcast_to(lengths[:, 0].astype(F32)[:, None], (micro, LANES))
+    length_rows = jnp.concatenate([length_rows, jnp.zeros((8 - micro, LANES), F32)], axis=0)
+    (length_all,) = gather_rows([length_rows], groups, 4)
+    lens = length_all.reshape(groups, 8, LANES)[:, :micro, 0].T.astype(jnp.int32)
+    packed, slots, chosen, kept_own = [], [], [], []
     for b in range(micro):
         seq, pos, own = slots_of(lens[b], count)
         slots.append((seq, pos))
+        wanted = seq[me] * spare + pos[me] - count
+        chosen.append(
+            jnp.logical_and(jnp.arange(groups * spare)[None, :] == wanted[:, None], ~own[me][:, None]).astype(BF16)
+        )
+        kept_own.append(jnp.where(own[me][:, None], source[b, :count], jnp.zeros((), BF16)))
+    for b in range(1 if all_in_one else micro):
         extra = first_extra if b == 0 else lax.all_gather(source[b, count:], "dp", axis=0, tiled=True)
-        wanted = seq[me] * spare + pos[me] - count
-        chosen = jnp.logical_and(jnp.arange(groups * spare)[None, :] == wanted[:, None], ~own[me][:, None])
-        brought = jnp.dot(chosen.astype(BF16), extra, preferred_element_type=F32).astype(BF16)
-        packed.append(jnp.where(own[me][:, None], source[b, :count], brought))
+        brought = times(chosen[b], extra)
+        packed.append((kept_own[b].astype(F32) + brought).astype(BF16))
 
     def spots_of(b):
         seq, pos = slots[b]
@@ -2182,7 +2367,6 @@
         return lax.psum_scatter(spread(rows, b), "dp", scatter_dimension=0, tiled=True)
 
     norm_one, norm_two = weights[0], weights[3]
-    all_in_one = micro == 2 and groups * count <= 2048
     empty = jnp.zeros((count, width), BF16)
 
     def spots_at(tick):
@@ -2195,20 +2379,27 @@
         joined[4] = joined[4][:, None]
         held = jnp.concatenate([holder(b) for b in range(micro)], axis=0).astype(BF16)
         y, dx, y_back, x, q, kv, lse, mixed, resid, gate, up, act, dy, d_resid, d_gate, d_up, d_qkv, gain_one, gain_two = main_ticks(
-            jnp.concatenate(packed, axis=0), joined, held, weights, groups, q_heads, k_heads, 0
+            packed[0],
+            (kept_own[1], source[1, count:], chosen[1]),
+            joined,
+            held,
+            weights,
+            groups,
+            q_heads,
+            k_heads,
+            0,
         )
-        results = [y[:count], y[count:]]
-        first_dresid, gain_last, grad_up, grad_down, grad_gate, back_last = last_ffn(
-            (dy, act, gate, up, d_gate, d_up, resid, d_resid, dx), held[groups * spare :], weights, groups, 1
+        first_dresid, gain_last, grad_up, grad_down, grad_gate = last_ffn(
+            (dy, act, gate, up, d_gate, d_up, resid, d_resid), weights, groups, 1
         )
         gain_last = jnp.where(first, gain_last, jnp.zeros_like(gain_last))
         gains = jnp.concatenate([gain_one, gain_two + gain_last, jnp.zeros((6, width), F32)], axis=0)
-        last_dx, back_first, gains, grad_up, grad_attn = last_attn(
-            (x, q[:count], kv[: groups * count], lse[: q_heads * count], mixed, d_qkv, d_resid),
+        last_dx, back_first, back_second, gains, grad_up, grad_attn = last_attn(
+            (x, q, kv, lse, mixed, d_qkv, d_resid),
             spots[0],
             first_dresid,
             dx,
-            held[: groups * spare],
+            held,
             gains,
             (spread_q, spread_k, spread_v, spread_o),
             (grad_up,),
@@ -2218,7 +2409,23 @@
             k_heads,
             2,
         )
-        grads_at = [last_dx, dx[count:]]
+        live = (jnp.arange(seq_len)[None, :] < lens[:, me][:, None]).astype(jnp.int32).reshape(-1, 1)
+        acts, backs, *grads = finish(
+            live,
+            inputs,
+            y,
+            y_back,
+            cotangent,
+            last_dx,
+            dx,
+            back_first,
+            back_second,
+            (grad_gate, grad_up, grad_down, grad_attn),
+            [w_query.shape[2], w_key.shape[2], w_value.shape[2], w_query.shape[2]],
+            groups,
+        )
+        grads[1:3] = [jnp.swapaxes(item, 1, 2) for item in grads[1:3]]
+        return (acts, backs, gains[:1], *grads[:4], gains[1:2], *grads[4:])
 
     else:
         arriving = empty
@@ -2280,14 +2487,11 @@
     acts = []
     for b in range(micro):
         rows = results[b]
-        back = y_back[b * spare : (b + 1) * spare] if all_in_one else come_back(rows, b)
-        acts.append(unpack(rows, back, b, inputs[b, 0]))
+        acts.append(unpack(rows, come_back(rows, b), b, inputs[b, 0]))
     backs = []
     for b in range(micro):
         rows = grads_at[b]
-        if all_in_one:
-            back = back_first if b == 0 else back_last
-        elif b == 0:
+        if b == 0:
             back, gains, grad_attn, *rest = return_rows(
                 spread(rows, b), gains, (grad_attn,) + ffn_grads[beside:], groups, 5, spare // 16
             )

time: 749 us -> 681 us (0.909)
  Pallas kernels: 652 us -> 621 us
  local copies, waits for them, and re-layouts: 39.1 us -> 11.3 us
  other arithmetic: 27.3 us -> 18.8 us
    pallas_call x1, Pallas kernels: 24.5 us -> 5.44 us  [gather_rows(): pl.pallas_call(functools.partial(gather_kernel, groups, count), out_shape...]
    unnamed x45 -> x23, local copies, waits for them, and re-layouts: 17.2 us -> 2.88 us
    pallas_call x1, Pallas kernels: 68.6 us -> 55.1 us  [last_ffn(): pl.pallas_call(functools.partial(last_ffn_kernel, groups, pieces, chunks)...]
    pallas_call x0 -> x1, Pallas kernels: none -> 13.1 us  [finish(): pl.pallas_call(functools.partial(finish_kernel, groups, parts), out_shape...]
    slice x6 -> x2, local copies, waits for them, and re-layouts: 8.92 us -> 1.36 us  [the longest x1 1.35 us: on_device(): return (acts, backs, gains[:1], *grads[:4], gains[1:2], *grads[4:])]
  transfers between devices with their start and end apart: 1 -> 1, of which waited for: 0 -> 0; matrix products, arithmetic and copies ran while one was open for 3% -> 4% of each run, Pallas kernels for 3% -> 1%
where the time goes in v4:
time: 681 us; the launch traced here: 674 us
  Pallas kernels  621 us (91%)
  other arithmetic  18.8 us (3%)
  between operations  14.6 us (2%)
  local copies, waits for them, and re-layouts  11.3 us (2%)
  matrix products  8.23 us (1%)
    pallas_call x1, Pallas kernels, main_ticks(): pl.pallas_call(functools.partial(main_kernel, groups, q_heads, k_heads, p...  450 us
    pallas_call x1, Pallas kernels, last_attn(): pl.pallas_call(functools.partial(last_attn_kernel, groups, q_heads, k_hea...  97.4 us
    pallas_call x1, Pallas kernels, last_ffn(): pl.pallas_call(functools.partial(last_ffn_kernel, groups, pieces, chunks)...  55.1 us
  transfers between devices with their start and end apart: 1, of which 0 were waited for; matrix products, arithmetic and copies ran while one was open for 4% of the time, Pallas kernels for 1%

profile of v4, /device:TPU:0, one launch (start us, length us, event | category | flops | bytes accessed | tf_op | source)
XLA Modules:
  0.0 673.5 jit_solution(11626531523371377820)
XLA Ops:
  7.2 3.2 fusion
  10.5 1.7 copy-done.2
  12.2 1.1 slice_bitcast_fusion.2
  13.4 5.4 gather_4.1
  22.1 1.2 fusion.36
  23.4 1.0 pad_maximum_fusion.9
  24.4 0.8 copy.65.refs_2_
  26.7 0.9 copy.62.refs_2_
  27.6 0.9 copy.63.refs_3_
  28.9 1.1 copy.73
  30.0 1.3 fusion.27
  32.6 1.0 fusion.13.refs_8_
  33.6 1.1 fusion.16
  35.7 1.3 add_convert_fusion.refs_7_
  37.0 1.1 fusion.1
  38.1 2.2 convolution_convert_fusion.refs_13_
  40.4 1.9 pad_maximum_fusion.refs_12_.refs_14_
  42.3 2.3 fusion.10.refs_10_
  44.6 3.9 fusion.2.refs_9_
  48.4 449.7 %main_ticks.1 = (bf16[640,1536]{1,0:T(8,128)(2,1)}, bf16[640,1536]{1,0:T(8,128)(2,1)}, bf16[384,1536]{1,0:T(8,128)(2,1)}, bf16[640,1536]{1,0:T(8,128)(2,1)}, bf1...) custom-call(f32[640,128]{1,0:T(8,128)} %get-tuple-element.98.refs_0_, ...), custom_call_target="tpu_custom_call" | custom-call | tf_op jit(solution)/shard_map/main_ticks/pallas_call | solution.py:1623
  498.1 55.1 %last_ffn.1 = (bf16[320,1536]{1,0:T(8,128)(2,1)}, f32[1,1536]{1,0:T(1,128)}, bf16[1536,1024]{1,0:T(8,128)(2,1)}, f32[384,1024]{1,0:T(8,128)}, f32[384,1024]{1,0:T(8,128)}) custom-call(f32[1,1536]{1,0:T(1,128)} %refs_0_.1, bf16[1024,1536]{1,0:T(8,128)(2,1)} %bitcast.100, bf16[1536,1024]{1,0:T(8,128)(2,1)} %bitcast.96, bf16[1536,1024]{1,0:T(8,128)(2,1)} %bitcast.98, ...), custom_call_target="tpu_custom_call" | custom-call | tf_op jit(solution)/shard_map/last_ffn/pallas_call | solution.py:1826
  554.7 97.4 %last_attn.1 = (bf16[320,1536]{1,0:T(8,128)(2,1)}, bf16[192,1536]{1,0:T(8,128)(2,1)}, bf16[192,1536]{1,0:T(8,128)(2,1)}, f32[8,384]{1,0:T(8,128)}, f32[384,1024]{1,0:T(8,128)}, /*index=5*/f32[384,1152]{1,0:T(8,128)}) custom-call(f32[320,128]{1,0:T(8,128)} %get-tuple-element.96.refs_0_, f32[320,128]{1,0:T(8,128)} %get-tuple-element.95.refs_1_, ...), custom_call_target="tpu_custom_call" | custom-call | tf_op jit(solution)/shard_map/last_attn/pallas_call | solution.py:2124
  652.0 1.4 fusion.49
  653.4 13.1 %finish.1 = (bf16[1,2,1,512,1536]{4,3,2,1,0:T(8,128)(2,1)}, bf16[1,2,1,512,1536]{4,3,2,1,0:T(8,128)(2,1)}, f32[1,384,384]{2,1,0:T(8,128)}, f32[1,192,384]{2,1,0:...) custom-call(s32[1024,1]{1,0:T(8,128)} %bitcast.101, ...), custom_call_target="tpu_custom_call" | custom-call | tf_op jit(solution)/shard_map/finish/pallas_call | solution.py:2250
  (93 shorter events, 9.1 us)
Async XLA Ops:
  7.2 29.9 %copy-start = (bf16[1,1536,384]{2,1,0:T(8,128)(2,1)S(1)}, bf16[1,1536,384]{2,1,0:T(8,128)(2,1)}, u32[]{:S(2)}) copy-start(bf16[1,1536,384]{2,1,0:T(8,128)(2,1)} %param.16) | copy-start | bytes 3538948
  7.2 37.4 %all-gather.3.cloned.1.call-start = ((), (), s32[]{:S(2)}) async-start(), calls=%async_computation | async-start | bytes 2949120 | tf_op jit(solution)/shard_map/all_gather | solution.py:2328
  10.5 1.7 copy-start.2
  12.2 1.1 copy-start.9
  22.1 9.2 %copy-start.5 = (s32[1,1280]{1,0:T(1,128)}, s32[1,1280]{1,0:T(1,128)S(1)}, u32[]{:S(2)}) copy-start(s32[1,1280]{1,0:T(1,128)S(1)} %get-tuple-element.105.refs_4_) | copy-start | bytes 15364
  29.9 4.7 copy-start.3
  31.3 3.9 copy-start.4
  35.7 2.4 copy-start.8
  498.1 55.1 %copy-start.6 = (f32[1,1536]{1,0:T(1,128)S(1)}, f32[1,1536]{1,0:T(1,128)}, u32[]{:S(2)}) copy-start(f32[1,1536]{1,0:T(1,128)} %get-tuple-element.62) | copy-start | bytes 18436
  498.1 55.8 %copy-start.7 = (f32[1,1536]{1,0:T(1,128)S(1)}, f32[1,1536]{1,0:T(1,128)}, u32[]{:S(2)}) copy-start(f32[1,1536]{1,0:T(1,128)} %get-tuple-element.61) | copy-start | bytes 18436
  653.4 13.1 %copy-start.1 = (bf16[1,1536,384]{2,1,0:T(8,128)(2,1)S(1)}, bf16[1,1536,384]{2,1,0:T(8,128)(2,1)}, u32[]{:S(2)}) copy-start(bf16[1,1536,384]{2,1,0:T(8,128)(2,1)} %param.16) | copy-start | bytes 3538948
Sparse Core Ops, SparseCore 0:
  13.4 26.7 all-gather.2

commit v5 on v4

--- a/solution.py
+++ b/solution.py
@@ -450,8 +450,8 @@
             total = self.part[self.rows(self.near, j)].astype(F32) + self.rin[self.local(self.near, j)].astype(F32)
             total = total + self.rmid[self.own(j)].astype(F32)
             if self.norm:
-                xrow, gain, gsum = self.norm
-                x = xrow[here].astype(F32)
+                xrow, gain, gsum, norm_at = self.norm
+                x = xrow[self.rows(self.near, j, norm_at)].astype(F32)
                 scale = lax.rsqrt(jnp.mean(x * x, axis=-1, keepdims=True) + epsilon)
                 unit = x * scale
                 gsum[...] += jnp.sum(total * unit, axis=0, keepdims=True)
@@ -765,7 +765,7 @@
     two_b.receive()
 
 
-VMEM_LIMIT = 58 * 2**20
+VMEM_LIMIT = 60 * 2**20
 
 
 def forward_tick(x, spots, weights, groups, q_heads, k_heads, cid):
@@ -820,7 +820,7 @@
     count, width = dy.shape
     quarter = count // 4
     a, b = [
-        Line(k * 2 * quarter, quarter, pieces, part, dy, dresid, refs[17 + 12 * k : 29 + 12 * k], norm=(resid, gain, gsum))
+        Line(k * 2 * quarter, quarter, pieces, part, dy, dresid, refs[17 + 12 * k : 29 + 12 * k], norm=(resid, gain, gsum, 0))
         for k in range(2)
     ]
     loads = load_all(list(zip(far_weights, near_weights)), w_sem)
@@ -940,7 +940,7 @@
             dresid,
             dx,
             take(14 if shift else 12),
-            norm=(x, gain, gsum),
+            norm=(x, gain, gsum, 0),
             moved=moved,
         )
         for k in range(2)
@@ -1109,7 +1109,7 @@
     cosine, sine, qcode, qstart, kcode, gain_one, gain_two, holder, chosen = take(9)
     packed, own_second, extra_second = take(3)
     far_weights = take(5)
-    y_out, dx_out, back_out = take(3)
+    y_out, dx_out, back_out, normed_one, normed_two = take(5)
     far_state = take(14)
     gsum_one, gsum_two = take(2)
     near_state = xs, q, kv, lse, mixed, resid, gate, up, act, dys, dresid, dgate, dup, dqkv = take(14)
@@ -1235,15 +1235,36 @@
 
         lax.fori_loop(begun, max(line.steps, begun + give.steps(give_lag) - give_lag), one, 0)
 
-    def given(slot, now):
+    def given(place, now):
         @pl.when(now)
         def _():
             give.finish()
-            pltpu.make_async_copy(returned, back_out.at[span(slot * spare, spare)], io_sem.at[1]).start()
-            pltpu.make_async_copy(returned, back_out.at[span(slot * spare, spare)], io_sem.at[1]).wait()
-
-    def forward(slot, carry):
+            pltpu.make_async_copy(returned, back_out.at[span(place * spare, spare)], io_sem.at[1]).start()
+            pltpu.make_async_copy(returned, back_out.at[span(place * spare, spare)], io_sem.at[1]).wait()
+
+    def back_lines(slot):
         base = slot * count
+        made = []
+        for k in range(4):
+            first = (k % 2) * half
+            scratch = list(line_scratch[k])
+            if k < 2:
+                norm = (resid, gain_two, gsum_two, base)
+                made.append(Line(first, quarter, pieces, part_one, dys, dresid, scratch, norm=norm, at=(base, base, 0)))
+            else:
+                scratch += [back_s.at[k - 2], back_r.at[2 * slot + k - 2]]
+                norm = (xs, gain_one, gsum_one, base)
+                made.append(
+                    Line(
+                        first, quarter, pieces, part_two, dresid, y, scratch, norm=norm, moved=(dys, -1), at=(base, 0, base)
+                    )
+                )
+        return made
+
+    def forward(slot):
+        base = slot * count
+        pending = jnp.logical_and(section == 1, slot == 1)
+        left_a, left_b = back_lines(0)[2:]
         whole = span(base, count)
         moved = (xs, 1)
         lines = []
@@ -1262,6 +1283,9 @@
         two_a.receive()
         two_b.receive()
         normalize_into(normed, xs, gain_one, 0, count, source_at=base)
+        keep_one = pltpu.make_async_copy(normed, normed_one.at[whole], io_sem.at[1])
+        keep_two = pltpu.make_async_copy(normed, normed_two.at[whole], io_sem.at[2])
+        keep_one.start()
 
         @pl.when(slot == 0)
         def _():
@@ -1283,10 +1307,15 @@
                 q[whole, here] = rolled(
                     value[:, h * LANES : (h + 1) * LANES], cosine[whole], sine[whole]
                 ).astype(BF16)
-        for level in range(levels - 1, -1, -1):
+        for level in range(levels - 1, 0, -1):
             gather.arrive(level)
-            if level:
-                gather.start(level - 1)
+            gather.start(level - 1)
+
+        @pl.when(pending)
+        def _():
+            run_steps(0, left_a.steps, (left_a.step, 0))
+
+        gather.arrive(0)
 
         @pl.when(slot == 0)
         def _():
@@ -1323,10 +1352,21 @@
 
         projected(part_one, mixed, wout, 0, base)
         one_a.start()
+
+        @pl.when(pending)
+        def _():
+            run_steps(0, left_b.steps, (left_b.step, 0))
+            left_out = pltpu.make_async_copy(y, dx_out.at[:count], io_sem.at[0])
+            left_out.start()
+            left_a.finish()
+            left_b.finish()
+            left_out.wait()
+
         attend(half)
         projected(part_one, mixed, wout, half, base)
         one_b.start()
-        give_back(0, slot == 1, one_a)
+        giving = jnp.logical_and(slot == 1, section == 0)
+        give_back(0, giving, one_a)
 
         @pl.when(slot == 0)
         def _():
@@ -1352,13 +1392,28 @@
 
             lax.fori_loop(0, tiles, one, 0)
 
+        keep_one.wait()
         hidden(0, one_b.step)
-        projected(part_two, act, wdown, 0, base)
-        two_a.start()
-        give_rest(slot == 1, one_b, tiles)
-        hidden(half, two_a.step)
-        projected(part_two, act, wdown, half, base)
-        two_b.start()
+
+        @pl.when(section == 0)
+        def _():
+            projected(part_two, act, wdown, 0, base)
+            two_a.start()
+
+        give_rest(giving, one_b, tiles)
+
+        def early(i):
+            @pl.when(section == 0)
+            def _():
+                two_a.step(i)
+
+        hidden(half, early)
+        keep_two.start()
+
+        @pl.when(section == 0)
+        def _():
+            projected(part_two, act, wdown, half, base)
+            two_b.start()
 
         @pl.when(slot == 0)
         def _():
@@ -1370,46 +1425,40 @@
                 def _():
                     target[count:] = (target[count:].astype(F32) + brought).astype(BF16)
 
-        run_steps(tiles, two_a.steps, (two_a.step, 0))
-        run_steps(0, two_b.steps, (two_b.step, 0))
         out = pltpu.make_async_copy(y, y_out.at[whole], io_sem.at[0])
-        out.start()
+
+        @pl.when(section == 0)
+        def _():
+            run_steps(tiles, two_a.steps, (two_a.step, 0))
+            run_steps(0, two_b.steps, (two_b.step, 0))
+            out.start()
+            two_a.finish()
+            two_b.finish()
+
         gather.finish()
-        for line in lines:
-            line.finish()
-        given(0, slot == 1)
+        one_a.finish()
+        one_b.finish()
+        keep_two.wait()
+        given(0, giving)
 
         @pl.when(slot == 0)
         def _():
             second.finish()
 
-        out.wait()
+        @pl.when(section == 0)
+        def _():
+            out.wait()
+
         for index in range(9):
             keep(index, slot).start()
         announce(meet_sem, neighbours)
-        return carry
-
-    lax.fori_loop(0, 2, forward, 0)
-
-    def backward(tick, carry):
-        slot = 1 - tick
+
+    def backward(slot):
+        giving = jnp.logical_or(section == 0, slot == 1)
+        later = jnp.logical_and(section == 1, slot == 0)
         base = slot * count
         whole = span(base, count)
-        lines = []
-        for k in range(4):
-            first = (k % 2) * half
-            scratch = list(line_scratch[k])
-            if k < 2:
-                norm = (resid, gain_two, gsum_two)
-                lines.append(Line(first, quarter, pieces, part_one, dys, dresid, scratch, norm=norm, at=(base, base, 0)))
-            else:
-                scratch += [back_s.at[k - 2], back_r.at[2 * slot + k - 2]]
-                norm = (xs, gain_one, gsum_one)
-                lines.append(
-                    Line(
-                        first, quarter, pieces, part_two, dresid, y, scratch, norm=norm, moved=(dys, -1), at=(base, 0, base)
-                    )
-                )
+        lines = back_lines(slot)
         one_a, one_b, two_a, two_b = lines
         two_a.receive()
         two_b.receive()
@@ -1450,7 +1499,7 @@
         hidden(half)
         back_hidden(half)
         one_b.start()
-        give_back(1, tick == 0, one_a)
+        give_back(1 - section, giving, one_a)
 
         def attend(first, g, each=None):
             def one(i, c):
@@ -1490,7 +1539,7 @@
         turns = repeat * blocks
         for g in range(k_heads):
             attend(0, g, lambda i: one_b.step(g * turns + i))
-        give_rest(tick == 0, one_b, k_heads * turns)
+        give_rest(giving, one_b, k_heads * turns)
         mix(half)
         for g in range(k_heads):
             attend(half, g)
@@ -1519,23 +1568,47 @@
         two_a.start()
         back(half)
         two_b.start()
-        run_steps(0, two_a.steps, (two_a.step, 0))
-        run_steps(0, two_b.steps, (two_b.step, 0))
-        out = pltpu.make_async_copy(y, dx_out.at[whole], io_sem.at[0])
-        out.start()
-        for line in lines:
-            line.finish()
+
+        @pl.when(jnp.logical_not(later))
+        def _():
+            run_steps(0, two_a.steps, (two_a.step, 0))
+            run_steps(0, two_b.steps, (two_b.step, 0))
+            out = pltpu.make_async_copy(y, dx_out.at[whole], io_sem.at[0])
+            out.start()
+            two_a.finish()
+            two_b.finish()
+            out.wait()
+
+        one_a.finish()
+        one_b.finish()
         for item in scatters:
             item.finish()
-        given(1, tick == 0)
-        out.wait()
+        given(1 + section, giving)
         for index in range(9, 14):
             keep(index, slot).start()
         announce(meet_sem, neighbours)
+
+    def turn(k, carry):
+        @pl.when(jnp.where(section == 0, k < 2, lax.rem(k, 2) == 0))
+        def _():
+            forward(jnp.where(section == 0, jnp.minimum(k, 1), k // 2))
+
+        @pl.when(jnp.where(section == 0, k == 2, lax.rem(k, 2) == 1))
+        def _():
+            backward(jnp.where(section == 0, 0, k // 2))
+
         return carry
 
-    lax.fori_loop(0, 1 + section, backward, 0)
+    lax.fori_loop(0, 3 + section, turn, 0)
     heard(meet_sem, neighbours)
+
+    @pl.when(section == 0)
+    def _():
+        spares[...] = times(holder[: groups * spare], y[...]).astype(BF16)
+        give.start()
+        run_steps(0, give.steps(give_lag), (lambda i: give.step(i, give_lag), 0))
+
+    given(2, section == 0)
     for k in range(2):
         Line(
             k * half,
@@ -1544,23 +1617,24 @@
             part_two,
             dresid,
             y,
-            list(line_scratch[2 + k]) + [back_s.at[k], back_r.at[k]],
+            list(line_scratch[2 + k]) + [back_s.at[k], back_r.at[2 + k]],
             moved=(dys, -1),
+            at=(0, 0, count),
         ).receive()
     for index in range(14):
-        keep(index, 1).wait()
+        keep(index, 0).wait()
         if index < 9:
-            keep(index, 0).wait()
+            keep(index, 1).wait()
 
     @pl.when(section > 0)
     def _():
         for index in range(9, 14):
-            keep(index, 0).wait()
+            keep(index, 1).wait()
 
     @pl.when(section == 0)
     def _():
-        keep(9, 0).start()
-        keep(9, 0).wait()
+        keep(9, 1).start()
+        keep(9, 1).wait()
 
 
 def main_ticks(packed, second, spots, holder, weights, groups, q_heads, k_heads, cid):
@@ -1581,7 +1655,9 @@
     outs = [
         shape(width),
         shape(width),
-        shape(width, 2 * spare),
+        shape(width, 3 * spare),
+        shape(width),
+        shape(width),
     ]
     state = [
         shape(width),
@@ -1650,41 +1726,63 @@
         del refs[:count]
         return taken
 
-    (gain,) = take(1)
-    sources = take(11)
-    first_dresid, gsum, g_up, down_sum, gate_sum = take(5)
+    gain, holder = take(2)
+    sources = take(14)
+    last_dresid, gsum, g_up, down_sum, gate_sum, y, returned = take(7)
     wdown, wgate, wup, dys, act, gate, up, dgate, dup, resid = kept = take(10)
-    n2, part, g_down, g_gate, w_sem = take(5)
-    (scratch,) = (take(12),)
-    count, width = part.shape
+    n2, part, g_down, g_gate, spares, w_sem = take(6)
+    line_scratch = [take(12) for _ in range(4)]
+    count, width = last_dresid.shape
     half = count // 2
     line_a, line_b = [
-        Line(k * half, half // 2, pieces, part, dys, first_dresid, item, norm=(resid, gain, gsum))
-        for k, item in enumerate((scratch, take(12)))
+        Line(
+            k * half,
+            half // 2,
+            pieces,
+            part,
+            dys,
+            last_dresid,
+            line_scratch[k],
+            norm=(resid, gain, gsum, count),
+            at=(count, 0, 0),
+        )
+        for k in range(2)
     ]
+    results = [Line(k * half, half // 2, pieces, part, resid, y, line_scratch[k]) for k in range(4)]
     down = OwnScatter(groups, width // groups, chunks, [g_down, down_sum] + take(OwnScatter.refs(groups)))
     gated = OwnScatter(groups, width // groups, chunks, [g_gate, gate_sum] + take(OwnScatter.refs(groups)))
+    spare = returned.shape[0]
+    give = OwnScatter(groups, spare, spare // 32, [spares, returned] + take(OwnScatter.refs(groups)))
     section = lax.axis_index("section")
     mine = section == 0
     tiles, wide, blocks = act.shape[1] // WIDE, width // WIDE, width // TILE
 
     def load(k):
         if k in (7, 8):
-            return pltpu.make_async_copy(sources[k].at[count:], kept[k].at[count:], w_sem.at[k])
+            return pltpu.make_async_copy(sources[k].at[:count], kept[k].at[:count], w_sem.at[k])
         return pltpu.make_async_copy(sources[k], kept[k], w_sem.at[k])
 
     lacks = [
-        pltpu.make_async_copy(sources[7].at[:count], kept[7].at[:count], w_sem.at[10]),
-        pltpu.make_async_copy(sources[8].at[:count], kept[8].at[:count], w_sem.at[11]),
-        pltpu.make_async_copy(sources[10].at[:count], first_dresid, w_sem.at[12]),
+        pltpu.make_async_copy(sources[7].at[count:], kept[7].at[count:], w_sem.at[10]),
+        pltpu.make_async_copy(sources[8].at[count:], kept[8].at[count:], w_sem.at[11]),
+        pltpu.make_async_copy(sources[10].at[count:], last_dresid, w_sem.at[12]),
     ]
-    loads = [load(k) for k in range(10)]
-    for k in (3, 0, 5, 6, 1, 2, 4, 9, 7, 8):
+    known = [
+        pltpu.make_async_copy(sources[11], y, w_sem.at[13]),
+        pltpu.make_async_copy(sources[12].at[:spare], returned, w_sem.at[14]),
+    ]
+    loads = [load(k) for k in range(10)] + [pltpu.make_async_copy(sources[13], n2, w_sem.at[15])]
+    for k in (3, 0, 5, 6, 1, 2, 4, 9, 10, 7, 8):
         loads[k].start()
 
     @pl.when(section > 0)
     def _():
         for item in lacks:
+            item.start()
+
+    @pl.when(mine)
+    def _():
+        for item in known:
             item.start()
 
     Line.greet()
@@ -1696,7 +1794,7 @@
         loads[k].wait()
 
     def hidden(first):
-        here = pl.ds(first, half)
+        here = pl.ds(count + first, half)
 
         def one(i, c):
             columns = lanes(i, WIDE)
@@ -1711,11 +1809,11 @@
         lax.fori_loop(0, tiles, one, 0)
 
     def back(first):
-        here = pl.ds(first, half)
+        here, there = pl.ds(first, half), pl.ds(count + first, half)
 
         def one(i, c):
             columns = lanes(i, WIDE)
-            total = with_transpose(dgate[here], wgate[columns, :]) + with_transpose(dup[here], wup[columns, :])
+            total = with_transpose(dgate[there], wgate[columns, :]) + with_transpose(dup[there], wup[columns, :])
             part[here, columns] = total.astype(BF16)
             return c
 
@@ -1734,6 +1832,20 @@
         line_a.start()
 
     loads[4].wait()
+
+    @pl.when(section > 0)
+    def _():
+        for k in range(4):
+            here = pl.ds(k * half, half)
+
+            def one(i, c):
+                part[here, lanes(i, WIDE)] = times(act[here], wdown[:, lanes(i, WIDE)]).astype(BF16)
+                return c
+
+            lax.fori_loop(0, wide, one, 0)
+            results[k].start()
+
+        loads[9].wait()
 
     def down_job(i, c):
         weight_job(g_down, dys, act, i)
@@ -1748,7 +1860,11 @@
         back(half)
         line_b.start()
 
-    for k in (9, 7, 8):
+    @pl.when(mine)
+    def _():
+        loads[9].wait()
+
+    for k in (10, 7, 8):
         loads[k].wait()
 
     @pl.when(section > 0)
@@ -1757,8 +1873,9 @@
         lacks[1].wait()
 
     late = 100
-    spans = 5
-    norm_rows = 2 * count // spans
+    spans = 0
+
+    first_done = line_a.steps + pieces
 
     def step(i, c):
         @pl.when(mine)
@@ -1766,11 +1883,22 @@
             line_a.step(i)
             line_b.step(i - line_a.steps)
 
-        down.step(i, late)
-
-        @pl.when(i < spans)
-        def _():
-            normalize_into(n2, resid, gain, i * norm_rows, norm_rows)
+        @pl.when(section > 0)
+        def _():
+            for k, item in enumerate(results):
+                item.step(i - k * pieces)
+
+            @pl.when(i == first_done)
+            def _():
+                spares[...] = times(holder[...], y[:count]).astype(BF16)
+                give.start()
+
+            give.step(i - first_done, late)
+
+        @pl.when(i < late)
+        def _():
+            down.step(i, late)
+            gated.step(i - spans - blocks, late)
 
         @pl.when(jnp.logical_and(i >= spans, i < spans + blocks))
         def _():
@@ -1780,15 +1908,14 @@
         def _():
             gated.start()
 
-        gated.step(i - spans - blocks, late)
-
         @pl.when(jnp.logical_and(i >= spans + blocks, i < spans + 2 * blocks))
         def _():
             weight_job(g_up, n2, dup, i - spans - blocks)
 
         return c
 
-    lax.fori_loop(0, max(line_a.steps + line_b.steps, spans + 2 * blocks, spans + blocks + chunks), step, 0)
+    enough = max(line_a.steps + line_b.steps, spans + 2 * blocks, spans + blocks + chunks)
+    lax.fori_loop(0, jnp.where(mine, enough, max(enough, line_a.steps + 3 * pieces, first_done + give.chunks)), step, 0)
     run_steps(late, late + chunks, (lambda i: down.step(i, late), 0), (lambda i: gated.step(i, late), 0))
 
     @pl.when(mine)
@@ -1796,17 +1923,25 @@
         line_a.finish()
         line_b.finish()
 
+        for item in known:
+            item.wait()
+
     @pl.when(section > 0)
     def _():
         lacks[2].wait()
+        run_steps(late, late + give.chunks, (lambda i: give.step(i, late), 0))
+        give.finish()
+        for item in results:
+            item.finish()
 
     down.finish()
     gated.finish()
 
 
-def last_ffn(known, weights, groups, cid):
+def last_ffn(known, holder, weights, groups, cid):
     norm_one, wqkv, wout, norm_two, wgate, wup, wdown = weights
-    dys, act, gate, up, dgate, dup, resid, dresid = known
+    dys, act, gate, up, dgate, dup, resid, dresid, y, y_back, normed_two = known
+    spare = holder.shape[0] // groups
     count, width = dys.shape[0] // 2, dys.shape[1]
     hidden = act.shape[1]
     pieces, chunks = 5, 8
@@ -1816,13 +1951,15 @@
     scratch = [pltpu.VMEM(item.shape, BF16) for item in sources]
     scratch += [
         pltpu.VMEM((2 * count, width), BF16),
-        pltpu.VMEM((count, width), BF16),
+        pltpu.VMEM((2 * count, width), BF16),
         pltpu.VMEM((width, hidden), BF16),
         pltpu.VMEM((width, hidden), BF16),
-        pltpu.SemaphoreType.DMA((13,)),
+        pltpu.VMEM((groups * spare, width), BF16),
+        pltpu.SemaphoreType.DMA((16,)),
     ]
-    scratch += Line.scratch(count // 4, pieces, width, False) * 2
+    scratch += Line.scratch(count // 4, pieces, width, False) * 4
     scratch += OwnScatter.scratch(groups, width // groups, hidden, chunks, BF16) * 2
+    scratch += OwnScatter.scratch(groups, spare, width, spare // 32, BF16)
     return pl.pallas_call(
         functools.partial(last_ffn_kernel, groups, pieces, chunks),
         out_shape=[
@@ -1831,15 +1968,17 @@
             jax.ShapeDtypeStruct((width, hidden), BF16),
             jax.ShapeDtypeStruct((width // groups, hidden), F32),
             jax.ShapeDtypeStruct((width // groups, hidden), F32),
+            jax.ShapeDtypeStruct((2 * count, width), BF16),
+            jax.ShapeDtypeStruct((spare, width), BF16),
         ],
-        in_specs=[vmem] + [far] * 11,
-        out_specs=[vmem] * 5,
+        in_specs=[vmem] * 2 + [far] * 14,
+        out_specs=[vmem] * 7,
         scratch_shapes=scratch,
         compiler_params=pltpu.CompilerParams(
             collective_id=cid, has_side_effects=True, vmem_limit_bytes=VMEM_LIMIT
         ),
         name="last_ffn",
-    )(norm_two[None], *sources, dresid)
+    )(norm_two[None], holder, *sources, dresid, y, y_back, normed_two)
 
 
 def last_attn_kernel(groups, q_heads, k_heads, pieces, chunks, spare_chunks, *refs):
@@ -1852,11 +1991,11 @@
 
     cosine, sine, qcode, qstart, kcode, gain, dresid, holder, gains, spread_q, spread_k, spread_v, spread_o = take(13)
     sources = take(10)
-    (dx_known,) = take(1)
-    dx, returned, returned_second, gains_out, up_sum, attn_sum = take(6)
+    dx_known, y, y_back, normed_one = take(4)
+    dx, returned, returned_y, gains_out, up_sum, attn_sum = take(6)
     wout, wqkv, x, q, kv, lse, mixed, dqkv, other_dresid, g_up = kept = take(10)
     plain, plain_mixed = take(2)
-    part, dmixed, dkv, n1, g_attn, spares, spares_second, gsum, gains_own, gains_all, gains_sum, w_sem, g_s, g_r = take(14)
+    part, dmixed, dkv, n1, g_attn, spares, spares_y, gsum, gains_own, gains_all, gains_sum, w_sem, g_s, g_r = take(14)
     levels = dp_bits(groups)
     count, width = part.shape
     half = count // 2
@@ -1874,20 +2013,26 @@
     ]
     spare = spares.shape[0] // groups
     back_task = OwnScatter(groups, spare, spare_chunks, [spares, returned] + take(OwnScatter.refs(groups)))
-    give = OwnScatter(groups, spare, spare_chunks, [spares_second, returned_second] + take(OwnScatter.refs(groups)))
+    give_y = OwnScatter(groups, spare, spare_chunks, [spares_y, returned_y] + take(OwnScatter.refs(groups)))
     small = OwnScatter(groups, 8, 1, [gains_sum, gains_out] + take(OwnScatter.refs(groups)))
     line_a, line_b = [
-        Line(k * half, half // 2, pieces, part, dresid, dx, take(12), norm=(x, gain, gsum)) for k in range(2)
+        Line(k * half, half // 2, pieces, part, dresid, dx, take(12), norm=(x, gain, gsum, count)) for k in range(2)
     ]
     section, t = lax.axis_index("section"), lax.axis_index("tensor")
     mine = section == 0
     order = [9, 0, 3, 4, 5, 1, 2, 6, 7, 8]
-    loads = [pltpu.make_async_copy(sources[k].at[: kept[k].shape[0]], kept[k], w_sem.at[k]) for k in range(10)]
+    loads = [pltpu.make_async_copy(sources[k].at[sources[k].shape[0] - kept[k].shape[0] :], kept[k], w_sem.at[k]) for k in range(10)]
     for k in order:
         loads[k].start()
-    known = pltpu.make_async_copy(dx_known.at[:count], dx, w_sem.at[11])
-    second = pltpu.make_async_copy(dx_known.at[count:], part, w_sem.at[10])
-    second.start()
+    known = pltpu.make_async_copy(dx_known.at[count:], dx, w_sem.at[11])
+    load_n1 = pltpu.make_async_copy(normed_one, n1, w_sem.at[10])
+    load_n1.start()
+    known_y = pltpu.make_async_copy(y_back.at[spare : 2 * spare], returned_y, w_sem.at[12])
+    load_y = pltpu.make_async_copy(y.at[count:], part, w_sem.at[12])
+
+    @pl.when(mine)
+    def _():
+        known_y.start()
 
     @pl.when(section > 0)
     def _():
@@ -1940,7 +2085,8 @@
             row_dot = jnp.sum(prob * d_prob, axis=-1, keepdims=True)
             d_scores = (prob * (d_prob - row_dot)).astype(BF16)
             d_query = times(d_scores, kv[:, lanes(g)]) * scale
-            dqkv[here, lanes(h)] = rolled(d_query, cosine[here], -sine[here]).astype(BF16)
+            there = pl.ds(pl.multiple_of(count + first + n * rows, rows), rows)
+            dqkv[there, lanes(h)] = rolled(d_query, cosine[here], -sine[here]).astype(BF16)
             dkv[lanes(g), :] += rows_contract(q[here, lanes(h)], d_scores) * scale
             dkv[lanes(k_heads + g), :] += rows_contract(dm, prob.astype(BF16))
             each(i)
@@ -1949,11 +2095,11 @@
         lax.fori_loop(0, turns, one, 0)
 
     def back(first):
-        here = pl.ds(first, half)
+        here, there = pl.ds(first, half), pl.ds(count + first, half)
 
         def one(i, c):
             columns = lanes(i, WIDE)
-            part[here, columns] = with_transpose(dqkv[here], wqkv[columns, :]).astype(BF16)
+            part[here, columns] = with_transpose(dqkv[there], wqkv[columns, :]).astype(BF16)
             return c
 
         lax.fori_loop(0, wide, one, 0)
@@ -1981,12 +2127,17 @@
     for item in (spread_q, spread_k, spread_v, spread_o):
         ends.append(ends[-1] + item.shape[0])
     starts = [0, q_heads, q_heads + k_heads, q_heads + 2 * k_heads]
-    second.wait()
-    spares_second[...] = times(holder[groups * spare :], part[...]).astype(BF16)
-    give.start()
-    normalize_into(n1, x, gain, 0, 2 * count)
+
+    @pl.when(section > 0)
+    def _():
+        load_y.start()
+        load_y.wait()
+        spares_y[...] = times(holder[...], part[...]).astype(BF16)
+        give_y.start()
+
+    load_n1.wait()
     plain_mixed[...] = with_transpose(mixed[...], spread_o[...]).astype(BF16)
-    other_dresid[:count] = dresid[...]
+    other_dresid[count:] = dresid[...]
 
     def out_job(i, c):
         here = lanes(i, TILE)
@@ -2000,8 +2151,8 @@
         ending = late + scatters[0].chunks
         run_steps(late, ending, *[(functools.partial(lambda s, i: s.step(i, late), s), 0) for s in scatters])
         for g in range(k_heads):
-            dqkv[:count, lanes(q_heads + g)] = rolled(owns[g][:, :LANES], cosine[...], -sine[...]).astype(BF16)
-            dqkv[:count, lanes(q_heads + k_heads + g)] = owns[g][:, LANES:].astype(BF16)
+            dqkv[count:, lanes(q_heads + g)] = rolled(owns[g][:, :LANES], cosine[...], -sine[...]).astype(BF16)
+            dqkv[count:, lanes(q_heads + k_heads + g)] = owns[g][:, LANES:].astype(BF16)
         back(0)
         line_a.start()
         back(half)
@@ -2036,18 +2187,22 @@
         def _():
             attn_task.start()
 
-        give.step(i - first_job, late)
         attn_task.step(i - jobs - 1, late)
+
+        @pl.when(section > 0)
+        def _():
+            give_y.step(i - first_job, late)
+
         return c
 
     lax.fori_loop(0, max(line_a.steps + line_b.steps, jobs + 1 + chunks), step, 0)
-    spares[...] = times(holder[: groups * spare], dx[...]).astype(BF16)
+    spares[...] = times(holder[...], dx[...]).astype(BF16)
     back_task.start()
-    section_one = jnp.where(mine, 1.0, 0.0)
     gains_own[...] = gains[...]
-    gains_own[:1] = gains[:1] + gsum[...] * section_one
+    gains_own[:1] = gains[:1] + gsum[...] * jnp.where(mine, 1.0, 0.0)
     for k in range(1, 4):
         spread(k).start()
+    run_steps(0, spare_chunks, (lambda i: back_task.step(i, late), 0))
     for k in range(1, 4):
         spread(k).wait()
     total = gains_own[...] + gains_all[0] + gains_all[1] + gains_all[2]
@@ -2057,14 +2212,17 @@
     small.start()
 
     def close(i, c):
-        back_task.step(i, late)
-        small.step(i, 2)
         up_task.step(late + i, late)
         attn_task.step(late + i, late)
-        give.step(late + i, late)
+
+        @pl.when(section > 0)
+        def _():
+            give_y.step(late + i, late)
+
+        small.step(i, 4)
         return c
 
-    lax.fori_loop(0, max(chunks, spare_chunks, small.steps(2)), close, 0)
+    lax.fori_loop(0, max(chunks, spare_chunks, small.steps(4)), close, 0)
     run_steps(late, late + spare_chunks, (lambda i: back_task.step(i, late), 0))
 
     @pl.when(mine)
@@ -2073,17 +2231,22 @@
         line_b.finish()
         for item in scatters:
             item.finish()
-
-    for item in (up_task, attn_task, back_task, give, small):
+        known_y.wait()
+
+    @pl.when(section > 0)
+    def _():
+        give_y.finish()
+
+    for item in (up_task, attn_task, back_task, small):
         item.finish()
 
 
-def last_attn(known, spots, dresid, dx, holder, gains, spreads, grads, weights, groups, q_heads, k_heads, cid):
+def last_attn(known, spots, dresid, dx, y, y_back, normed_one, holder, gains, spreads, grads, weights, groups, q_heads, k_heads, cid):
     norm_one, wqkv, wout, norm_two, wgate, wup, wdown = weights
     x, q, kv, lse, mixed, dqkv, other_dresid = known
     count, width = dresid.shape
     keys = groups * count
-    spare = holder.shape[0] // (2 * groups)
+    spare = holder.shape[0] // groups
     pieces, chunks, spare_chunks = 5, 8, spare // 32
     vmem = pl.BlockSpec(memory_space=pltpu.VMEM)
     far = pl.BlockSpec(memory_space=pl.ANY)
@@ -2109,7 +2272,7 @@
         pltpu.VMEM(gains.shape, F32),
         pltpu.VMEM((3,) + gains.shape, F32),
         pltpu.VMEM((groups * 8, block), F32),
-        dma((12,)),
+        dma((13,)),
         dma((3,)),
         dma((3,)),
     ]
@@ -2131,14 +2294,14 @@
             jax.ShapeDtypeStruct((block, grads[0].shape[1]), F32),
             jax.ShapeDtypeStruct((block, attn_width), F32),
         ],
-        in_specs=[vmem] * 13 + [far] * 11,
+        in_specs=[vmem] * 13 + [far] * 14,
         out_specs=[vmem] * 6,
         scratch_shapes=scratch,
         compiler_params=pltpu.CompilerParams(
             collective_id=cid, has_side_effects=True, vmem_limit_bytes=VMEM_LIMIT
         ),
         name="last_attn",
-    )(*spots, norm_one[None], dresid, holder, gains, *spreads, *sources, dx)
+    )(*spots, norm_one[None], dresid, holder, gains, *spreads, *sources, dx, y, y_back, normed_one)
 
 
 def finish_kernel(groups, parts, *refs):
@@ -2150,7 +2313,7 @@
         return taken
 
     (live,) = take(1)
-    through, y, y_back, cot, dx_first, dx_second, back_first, back_second = take(8)
+    through, y, y_first, y_second, cot, dx_first, dx_second, back_first, back_second = take(9)
     gate, up, down, attn = take(4)
     acts, backs = take(2)
     outs = take(7)
@@ -2163,10 +2326,10 @@
     count, spare = rows[0].shape[0], backs_near[0].shape[0]
     seq = count + spare
     whole = [
-        (through.at[0, 0], y.at[:count], y_back.at[:spare], acts.at[0, 0, 0]),
-        (through.at[1, 0], y.at[count:], y_back.at[spare:], acts.at[0, 1, 0]),
-        (cot.at[0, 0], dx_first, back_first, backs.at[0, 0, 0]),
-        (cot.at[1, 0], dx_second.at[count:], back_second, backs.at[0, 1, 0]),
+        (through.at[0, 0], y.at[:count], y_first, acts.at[0, 0, 0]),
+        (through.at[1, 0], y.at[count:], y_second, acts.at[0, 1, 0]),
+        (cot.at[0, 0], dx_first.at[:count], back_first.at[2 * spare :], backs.at[0, 0, 0]),
+        (cot.at[1, 0], dx_second, back_second, backs.at[0, 1, 0]),
     ]
     query_out, key_out, value_out, out_out, gate_out, up_out, down_out = outs
     plain_in = [pltpu.make_async_copy(a, b, sems.at[14 + k]) for k, (a, b) in enumerate(zip((gate, up), plain_near))]
@@ -2231,9 +2394,9 @@
         item.wait()
 
 
-def finish(live, through, y, y_back, cot, dx_first, dx_second, back_first, back_second, grads, parts, groups):
-    count, width = dx_first.shape
-    spare = back_first.shape[0]
+def finish(live, through, y, y_backs, cot, dx_first, dx_second, back_first, back_second, grads, parts, groups):
+    count, width = dx_second.shape
+    spare = back_second.shape[0]
     gate, up, down, attn = grads
     block, hidden = down.shape
     vmem = pl.BlockSpec(memory_space=pltpu.VMEM)
@@ -2250,12 +2413,12 @@
     return pl.pallas_call(
         functools.partial(finish_kernel, groups, parts),
         out_shape=outs,
-        in_specs=[vmem] + [far] * 12,
+        in_specs=[vmem] + [far] * 13,
         out_specs=[far] * 9,
         scratch_shapes=scratch,
         compiler_params=pltpu.CompilerParams(vmem_limit_bytes=VMEM_LIMIT),
         name="finish",
-    )(live, through, y, y_back, cot, dx_first, dx_second, back_first, back_second, gate, up, down, attn)
+    )(live, through, y, *y_backs, cot, dx_first, dx_second, back_first, back_second, gate, up, down, attn)
 
 
 def rope_tables(pos):
@@ -2378,7 +2541,7 @@
         joined = [jnp.concatenate(items, axis=0) for items in zip(*spots)]
         joined[4] = joined[4][:, None]
         held = jnp.concatenate([holder(b) for b in range(micro)], axis=0).astype(BF16)
-        y, dx, y_back, x, q, kv, lse, mixed, resid, gate, up, act, dy, d_resid, d_gate, d_up, d_qkv, gain_one, gain_two = main_ticks(
+        y, dx, y_back, normed_one, normed_two, x, q, kv, lse, mixed, resid, gate, up, act, dy, d_resid, d_gate, d_up, d_qkv, gain_one, gain_two = main_ticks(
             packed[0],
             (kept_own[1], source[1, count:], chosen[1]),
             joined,
@@ -2389,17 +2552,20 @@
             k_heads,
             0,
         )
-        first_dresid, gain_last, grad_up, grad_down, grad_gate = last_ffn(
-            (dy, act, gate, up, d_gate, d_up, resid, d_resid), weights, groups, 1
+        last_dresid, gain_last, grad_up, grad_down, grad_gate, y, y_first = last_ffn(
+            (dy, act, gate, up, d_gate, d_up, resid, d_resid, y, y_back, normed_two), held[: groups * spare], weights, groups, 1
         )
         gain_last = jnp.where(first, gain_last, jnp.zeros_like(gain_last))
         gains = jnp.concatenate([gain_one, gain_two + gain_last, jnp.zeros((6, width), F32)], axis=0)
-        last_dx, back_first, back_second, gains, grad_up, grad_attn = last_attn(
+        last_dx, back_second, y_second, gains, grad_up, grad_attn = last_attn(
             (x, q, kv, lse, mixed, d_qkv, d_resid),
-            spots[0],
-            first_dresid,
+            spots[1],
+            last_dresid,
             dx,
-            held,
+            y,
+            y_back,
+            normed_one,
+            held[groups * spare :],
             gains,
             (spread_q, spread_k, spread_v, spread_o),
             (grad_up,),
@@ -2414,11 +2580,11 @@
             live,
             inputs,
             y,
+            (y_first, y_second),
+            cotangent,
+            dx,
+            last_dx,
             y_back,
-            cotangent,
-            last_dx,
-            dx,
-            back_first,
             back_second,
             (grad_gate, grad_up, grad_down, grad_attn),
             [w_query.shape[2], w_key.shape[2], w_value.shape[2], w_query.shape[2]],

time: 681 us -> 610 us (0.90)
  Pallas kernels: 621 us -> 549 us
    pallas_call x1, Pallas kernels: 450 us -> 383 us  [main_ticks(): pl.pallas_call(functools.partial(main_kernel, groups, q_heads, k_heads, p...]
    pallas_call x1, Pallas kernels: 97.4 us -> 90.1 us  [last_attn(): pl.pallas_call(functools.partial(last_attn_kernel, groups, q_heads, k_hea...]
where the time goes in v5:
time: 610 us; the launch traced here: 603 us
  Pallas kernels  549 us (90%)
  other arithmetic  17.7 us (3%)
  between operations  14.6 us (2%)
  local copies, waits for them, and re-layouts  12.7 us (2%)
  matrix products  8.22 us (1%)
    pallas_call x1, Pallas kernels, main_ticks(): pl.pallas_call(functools.partial(main_kernel, groups, q_heads, k_heads, p...  383 us
    pallas_call x1, Pallas kernels, last_attn(): pl.pallas_call(functools.partial(last_attn_kernel, groups, q_heads, k_hea...  90.1 us
    pallas_call x1, Pallas kernels, last_ffn(): pl.pallas_call(functools.partial(last_ffn_kernel, groups, pieces, chunks)...  57.9 us
    pallas_call x1, Pallas kernels, finish(): pl.pallas_call(functools.partial(finish_kernel, groups, parts), out_shape...  13.1 us
  transfers between devices with their start and end apart: 1, of which 0 were waited for; matrix products, arithmetic and copies ran while one was open for 4% of the time, Pallas kernels for 1%

profile of v5, /device:TPU:0, one launch (start us, length us, event | category | flops | bytes accessed | tf_op | source)
XLA Modules:
  0.0 602.6 jit_solution(7859684528959759665)
XLA Ops:
  7.2 3.2 fusion
  10.5 1.7 copy-done.3
  12.2 1.1 slice_bitcast_fusion.2
  13.4 5.4 gather_4.1
  22.4 0.8 copy.65.refs_2_
  24.1 0.9 copy.62.refs_2_
  25.0 0.9 copy.63.refs_3_
  26.7 1.0 copy.73
  28.6 1.2 fusion.36
  29.9 1.2 fusion.27
  31.1 1.0 pad_maximum_fusion.9
  32.5 1.0 fusion.13.refs_8_
  33.6 1.1 fusion.16
  36.0 1.3 fusion.49
  37.3 1.1 fusion.1
  38.5 2.2 convolution_convert_fusion.refs_13_
  40.8 1.9 pad_maximum_fusion.refs_12_.refs_14_
  42.6 2.3 fusion.10.refs_10_
  44.9 3.9 fusion.2.refs_9_
  48.8 382.8 %main_ticks.1 = (bf16[640,1536]{1,0:T(8,128)(2,1)}, bf16[640,1536]{1,0:T(8,128)(2,1)}, bf16[576,1536]{1,0:T(8,128)(2,1)}, bf16[640,1536]{1,0:T(8,128)(2,1)}, bf1...) custom-call(f32[640,128]{1,0:T(8,128)} %get-tuple-element.108.refs_0, ...), custom_call_target="tpu_custom_call" | custom-call | tf_op jit(solution)/shard_map/main_ticks/pallas_call | solution.py:1699
  431.6 57.9 %last_ffn.1 = (bf16[320,1536]{1,0:T(8,128)(2,1)}, f32[1,1536]{1,0:T(1,128)}, bf16[1536,1024]{1,0:T(8,128)(2,1)}, f32[384,1024]{1,0:T(8,128)}, f32[384,1024]{1,0:...) custom-call(f32[1,1536]{1,0:T(1,128)} %refs_0_.1, bf16[768,320]{1,0:T(8,128)(2,1)} %get-tuple-element.104.refs_1_, ...), custom_call_target="tpu_custom_call" | custom-call | tf_op jit(solution)/shard_map/last_ffn/pallas_call | solution.py:1963
  491.0 90.1 %last_attn.1 = (bf16[320,1536]{1,0:T(8,128)(2,1)}, bf16[192,1536]{1,0:T(8,128)(2,1)}, bf16[192,1536]{1,0:T(8,128)(2,1)}, f32[8,384]{1,0:T(8,128)}, f32[384,1024]{1,0:T(8,128)}, /*index=5*/f32[384,1152]{1,0:T(8,128)}) custom-call(f32[320,128]{1,0:T(8,128)} %get-tuple-element.106.refs_0_, f32[320,128]{1,0:T(8,128)} %get-tuple-element.105.refs_1_, ...), custom_call_target="tpu_custom_call" | custom-call | tf_op jit(solution)/shard_map/last_attn/pallas_call | solution.py:2287
  581.1 1.4 fusion.50
  582.5 13.1 %finish.1 = (bf16[1,2,1,512,1536]{4,3,2,1,0:T(8,128)(2,1)}, bf16[1,2,1,512,1536]{4,3,2,1,0:T(8,128)(2,1)}, f32[1,384,384]{2,1,0:T(8,128)}, f32[1,192,384]{2,1,0:...) custom-call(s32[1024,1]{1,0:T(8,128)} %bitcast.101, ...), custom_call_target="tpu_custom_call" | custom-call | tf_op jit(solution)/shard_map/finish/pallas_call | solution.py:2413
  (96 shorter events, 9.5 us)
Async XLA Ops:
  7.2 30.1 %copy-start = (bf16[1,1536,384]{2,1,0:T(8,128)(2,1)S(1)}, bf16[1,1536,384]{2,1,0:T(8,128)(2,1)}, u32[]{:S(2)}) copy-start(bf16[1,1536,384]{2,1,0:T(8,128)(2,1)} %param.16) | copy-start | bytes 3538948
  7.2 37.7 %all-gather.3.cloned.1.call-start = ((), (), s32[]{:S(2)}) async-start(), calls=%async_computation | async-start | bytes 2949120 | tf_op jit(solution)/shard_map/all_gather | solution.py:2491
  10.5 1.7 copy-start.3
  12.2 1.1 copy-start.10
  21.8 9.4 %copy-start.6 = (s32[1,1280]{1,0:T(1,128)}, s32[1,1280]{1,0:T(1,128)S(1)}, u32[]{:S(2)}) copy-start(s32[1,1280]{1,0:T(1,128)S(1)} %get-tuple-element.116.refs_4_) | copy-start | bytes 15364
  29.9 4.8 copy-start.4
  31.1 4.1 copy-start.5
  36.0 2.4 copy-start.2
  37.3 1.3 copy-start.9
  431.6 58.0 %copy-start.7 = (f32[1,1536]{1,0:T(1,128)S(1)}, f32[1,1536]{1,0:T(1,128)}, u32[]{:S(2)}) copy-start(f32[1,1536]{1,0:T(1,128)} %get-tuple-element.69) | copy-start | bytes 18436
  431.6 58.7 %copy-start.8 = (f32[1,1536]{1,0:T(1,128)S(1)}, f32[1,1536]{1,0:T(1,128)}, u32[]{:S(2)}) copy-start(f32[1,1536]{1,0:T(1,128)} %get-tuple-element.68) | copy-start | bytes 18436
  582.5 13.1 %copy-start.1 = (bf16[1,1536,384]{2,1,0:T(8,128)(2,1)S(1)}, bf16[1,1536,384]{2,1,0:T(8,128)(2,1)}, u32[]{:S(2)}) copy-start(bf16[1,1536,384]{2,1,0:T(8,128)(2,1)} %param.16) | copy-start | bytes 3538948
Sparse Core Ops, SparseCore 0:
  13.4 26.8 all-gather.2

commit v6 on v5

--- a/solution.py
+++ b/solution.py
@@ -2,6 +2,7 @@
 
 import jax
 import jax.numpy as jnp
+import numpy as np
 from jax import lax
 from jax.experimental import pallas as pl
 from jax.experimental.pallas import tpu as pltpu
@@ -537,7 +538,8 @@
 
 
 class Gather:
-    def __init__(self, groups, rows, out, s_sem, r_sem):
+    def __init__(self, groups, rows, out, s_sem, r_sem, first=0, size=None):
+        self.first, self.size = first, size or rows
         self.groups, self.rows, self.out, self.s_sem, self.r_sem = groups, rows, out, s_sem, r_sem
         self.levels = dp_bits(groups)
         self.links = [dp_partner(k) for k in range(self.levels)]
@@ -553,7 +555,7 @@
         if not mine:
             low = low + (1 - 2 * bit) * (1 << level)
         block = i * (1 << (level + 1)) + low
-        place = self.out.at[pl.ds(pl.multiple_of(block * self.rows, self.rows), self.rows)]
+        place = self.out.at[pl.ds(pl.multiple_of(block * self.rows + self.first, self.size), self.size)]
         return remote(place, place, self.s_sem.at[level, i], self.r_sem.at[level, i], where)
 
     def start(self, level):
@@ -621,7 +623,7 @@
 def score_rows(q, kv, h, g, here, qcode, qstart, kcode):
     scores = with_transpose(q[here, lanes(h)], kv[:, lanes(g)]) * HD ** (-0.5)
     code = kcode[...]
-    return scores, jnp.logical_and(code <= qcode[here], code >= qstart[here])
+    return scores, jnp.logical_and(code <= qcode[here][:, :1], code >= qstart[here][:, :1])
 
 
 def load_all(pairs, sems):
@@ -1107,8 +1109,8 @@
         return taken
 
     cosine, sine, qcode, qstart, kcode, gain_one, gain_two, holder, chosen = take(9)
-    packed, own_second, extra_second = take(3)
-    far_weights = take(5)
+    own_rows, extra_first, extra_second = take(3)
+    far_weights = take(7)
     y_out, dx_out, back_out, normed_one, normed_two = take(5)
     far_state = take(14)
     gsum_one, gsum_two = take(2)
@@ -1117,7 +1119,7 @@
     wqkv, wout, wgate, wup, wdown = near_weights = take(5)
     part_one, part_two, normed, y, dmixed, dkv, w_sem, io_sem, meet_sem = take(9)
     levels = dp_bits(groups)
-    gather_sems = take(2)
+    gather_sems = [take(2) for _ in range(2)]
     line_scratch = [take(12) for _ in range(4)]
     forth_s, forth_r, back_s, back_r = take(4)
     spares, returned = take(2)
@@ -1158,35 +1160,37 @@
     Line.greet()
     greet({"section": 1 - section})
 
-    loads = load_all(list(zip(far_weights, near_weights)), w_sem)
-
-    def fetch(target):
-        return (
-            pltpu.make_async_copy(packed, target.at[:count], io_sem.at[0]),
-            pltpu.make_async_copy(own_second, target.at[count:], io_sem.at[1]),
-        )
+    ends = [0]
+    for item in far_weights[:3]:
+        ends.append(ends[-1] + item.shape[1])
+    parts = [wqkv.at[:, a:b] for a, b in zip(ends, ends[1:])]
+    copies = load_all(list(zip(far_weights, parts + list(near_weights[1:]))), w_sem)
+    loads = [copies[:3], *[[item] for item in copies[3:]]]
 
     place = span(lax.axis_index("dp") * spare, spare)
+    fetch_first = pltpu.make_async_copy(extra_first, spares, io_sem.at[2])
     fetch_extra = pltpu.make_async_copy(extra_second, spares.at[place], io_sem.at[2])
-    fetch_extra.start()
+    fetch_first.start()
     for which, target in enumerate((xs, dys)):
 
         @pl.when(section == which)
         def _():
-            for item in fetch(target):
-                item.start()
+            pltpu.make_async_copy(own_rows, target, io_sem.at[0]).start()
 
     pl.semaphore_wait(pltpu.get_barrier_semaphore(), jnp.where(jnp.logical_or(t == 1, t == 2), 2, 1) + levels + 1)
     announce(meet_sem, neighbours)
     gsum_one[...] = jnp.zeros_like(gsum_one)
     gsum_two[...] = jnp.zeros_like(gsum_two)
+    fetch_first.wait()
+    brought_first = times(chosen[:count], spares[...])
     for which, target in enumerate((xs, dys)):
 
         @pl.when(section == which)
         def _():
-            for item in fetch(target):
-                item.wait()
-
+            pltpu.make_async_copy(own_rows, target, io_sem.at[0]).wait()
+            target[:count] = (target[:count].astype(F32) + brought_first).astype(BF16)
+
+    fetch_extra.start()
     fetch_extra.wait()
 
     def keep(index, slot):
@@ -1241,6 +1245,33 @@
             give.finish()
             pltpu.make_async_copy(returned, back_out.at[span(place * spare, spare)], io_sem.at[1]).start()
             pltpu.make_async_copy(returned, back_out.at[span(place * spare, spare)], io_sem.at[1]).wait()
+
+    def ffn_back(slot, first, each=None):
+        here, there = span(first, half), span(slot * count + first, half)
+
+        def one(i, c):
+            columns = lanes(i, WIDE)
+            d_act = with_transpose(dys[there], wdown[columns, :])
+            gate_pre, up_pre = gate[there, columns].astype(F32), up[there, columns].astype(F32)
+            sigma = jax.nn.sigmoid(gate_pre)
+            d_silu = d_act * sigma
+            dup[there, columns] = (d_silu * gate_pre).astype(BF16)
+            dgate[there, columns] = (d_silu * up_pre * (1.0 + gate_pre * (1.0 - sigma))).astype(BF16)
+            if each:
+                each(i)
+            return c
+
+        lax.fori_loop(0, tiles, one, 0)
+
+        def two(i, c):
+            columns = lanes(i, WIDE)
+            total = with_transpose(dgate[there], wgate[columns, :]) + with_transpose(dup[there], wup[columns, :])
+            part_one[here, columns] = total.astype(BF16)
+            if each:
+                each(tiles + i)
+            return c
+
+        lax.fori_loop(0, wide, two, 0)
 
     def back_lines(slot):
         base = slot * count
@@ -1261,61 +1292,86 @@
                 )
         return made
 
-    def forward(slot):
+    def forward_lines(slot):
         base = slot * count
-        pending = jnp.logical_and(section == 1, slot == 1)
-        left_a, left_b = back_lines(0)[2:]
-        whole = span(base, count)
-        moved = (xs, 1)
-        lines = []
+        made = []
         for k in range(4):
             first = (k % 2) * half
             scratch = list(line_scratch[k])
             if k < 2:
-                lines.append(Line(first, quarter, pieces, part_one, xs, resid, scratch, at=(base, base, 0)))
+                made.append(Line(first, quarter, pieces, part_one, xs, resid, scratch, at=(base, base, 0)))
             else:
                 scratch += [forth_s.at[k - 2], forth_r.at[2 * slot + k - 2]]
-                lines.append(
-                    Line(first, quarter, pieces, part_two, resid, y, scratch, moved=moved, at=(base, 0, base))
+                made.append(
+                    Line(first, quarter, pieces, part_two, resid, y, scratch, moved=(xs, 1), at=(base, 0, base))
                 )
-        one_a, one_b, two_a, two_b = lines
-        gather = Gather(groups, count, kv.at[span(slot * keys, keys)], *gather_sems)
-        two_a.receive()
-        two_b.receive()
-        normalize_into(normed, xs, gain_one, 0, count, source_at=base)
-        keep_one = pltpu.make_async_copy(normed, normed_one.at[whole], io_sem.at[1])
-        keep_two = pltpu.make_async_copy(normed, normed_two.at[whole], io_sem.at[2])
-        keep_one.start()
-
-        @pl.when(slot == 0)
-        def _():
-            loads[0].wait()
-
-        mine = span(slot * keys + lax.axis_index("dp") * count, count)
+        return made
+
+    def gathers_of(slot):
+        place = kv.at[span(slot * keys, keys)]
+        return [Gather(groups, count, place, *gather_sems[h], h * half, half) for h in range(2)]
+
+    def keep_normed(slot):
+        return pltpu.make_async_copy(normed, normed_one.at[span(slot * count, count)], io_sem.at[1])
+
+    def begin(slot, sync):
+        base = slot * count
         middle = (q_heads + k_heads) * LANES
-        value = times(normed[...], wqkv[:, q_heads * LANES : middle])
-        for g in range(k_heads):
-            here = slice(g * LANES, (g + 1) * LANES)
-            kv[mine, here] = rolled(value[:, here], cosine[whole], sine[whole]).astype(BF16)
-        kv[mine, k_heads * LANES :] = times(normed[...], wqkv[:, middle:]).astype(BF16)
-        heard(meet_sem, neighbours)
-        gather.start(levels - 1)
+        for h, (line, gather) in enumerate(zip(forward_lines(slot)[2:], gathers_of(slot))):
+            line.receive()
+            normalize_into(normed, xs, gain_one, h * half, half, source_at=base)
+            if h == 0:
+
+                @pl.when(slot == 0)
+                def _():
+                    for item in loads[0]:
+                        item.wait()
+
+            here, there = span(h * half, half), span(base + h * half, half)
+            mine = span(slot * keys + lax.axis_index("dp") * count + h * half, half)
+            value = times(normed[here], wqkv[:, q_heads * LANES : middle])
+            for g in range(k_heads):
+                columns = slice(g * LANES, (g + 1) * LANES)
+                kv[mine, columns] = rolled(value[:, columns], cosine[there], sine[there]).astype(BF16)
+            kv[mine, k_heads * LANES :] = times(normed[here], wqkv[:, middle:]).astype(BF16)
+            if h == 0 and sync:
+                heard(meet_sem, neighbours)
+            gather.start(levels - 1)
+        keep_normed(slot).start()
+        whole = span(base, count)
         for first in range(0, q_heads, 2):
             value = times(normed[...], wqkv[:, first * LANES : (first + 2) * LANES])
             for h in range(2):
-                here = slice((first + h) * LANES, (first + h + 1) * LANES)
-                q[whole, here] = rolled(
+                columns = slice((first + h) * LANES, (first + h + 1) * LANES)
+                q[whole, columns] = rolled(
                     value[:, h * LANES : (h + 1) * LANES], cosine[whole], sine[whole]
                 ).astype(BF16)
+
+    def forward(slot):
+        base = slot * count
+        whole = span(base, count)
+        pending = jnp.logical_and(section == 1, slot == 1)
+        left_a, left_b = back_lines(0)[2:]
+        one_a, one_b, two_a, two_b = forward_lines(slot)
+        gathers = gathers_of(slot)
+        keep_one = keep_normed(slot)
+        keep_two = pltpu.make_async_copy(normed, normed_two.at[whole], io_sem.at[2])
+
+        @pl.when(jnp.logical_not(pending))
+        def _():
+            begin(slot, True)
+
         for level in range(levels - 1, 0, -1):
-            gather.arrive(level)
-            gather.start(level - 1)
+            for gather in gathers:
+                gather.arrive(level)
+                gather.start(level - 1)
 
         @pl.when(pending)
         def _():
             run_steps(0, left_a.steps, (left_a.step, 0))
 
-        gather.arrive(0)
+        for gather in gathers:
+            gather.arrive(0)
 
         @pl.when(slot == 0)
         def _():
@@ -1328,7 +1384,7 @@
                 here = span(base + first + b * rows, rows)
                 scores = with_transpose(q[here, lanes(h)], kv[span(slot * keys, keys), lanes(g)]) * scale
                 code = kcode[slot]
-                allowed = jnp.logical_and(code <= qcode[here], code >= qstart[here])
+                allowed = jnp.logical_and(code <= qcode[here][:, :1], code >= qstart[here][:, :1])
                 scores = jnp.where(allowed, scores, negative)
                 row_max = jnp.max(scores, axis=-1, keepdims=True)
                 expo = jnp.exp(scores - row_max)
@@ -1348,9 +1404,14 @@
 
         @pl.when(slot == 0)
         def _():
-            loads[1].wait()
+            loads[1][0].wait()
 
         projected(part_one, mixed, wout, 0, base)
+
+        @pl.when(pending)
+        def _():
+            heard(meet_sem, neighbours)
+
         one_a.start()
 
         @pl.when(pending)
@@ -1365,12 +1426,11 @@
         attend(half)
         projected(part_one, mixed, wout, half, base)
         one_b.start()
-        giving = jnp.logical_and(slot == 1, section == 0)
-        give_back(0, giving, one_a)
+        run_steps(0, one_a.steps, (one_a.step, 0))
 
         @pl.when(slot == 0)
         def _():
-            for item in loads[2:]:
+            for (item,) in loads[2:]:
                 item.wait()
             for level in range(levels - 1, 0, -1):
                 second.arrive(level)
@@ -1400,7 +1460,32 @@
             projected(part_two, act, wdown, 0, base)
             two_a.start()
 
-        give_rest(giving, one_b, tiles)
+        @pl.when(slot == 0)
+        def _():
+            second.arrive(0)
+            brought = times(chosen[count:], spares[...])
+            for which, target in enumerate((xs, dys)):
+
+                @pl.when(section == which)
+                def _():
+                    target[count:] = (target[count:].astype(F32) + brought).astype(BF16)
+
+        @pl.when(section == 1)
+        def _():
+            one_a.finish()
+            ffn_back(slot, 0, lambda i: one_b.step(tiles + i))
+            run_steps(2 * tiles + wide, one_b.steps, (one_b.step, 0))
+
+        @pl.when(section == 0)
+        def _():
+            run_steps(tiles, one_b.steps, (one_b.step, 0))
+
+        @pl.when(section == 1)
+        def _():
+            one_b.finish()
+            for gather in gathers:
+                gather.finish()
+            announce(meet_sem, neighbours)
 
         def early(i):
             @pl.when(section == 0)
@@ -1409,52 +1494,38 @@
 
         hidden(half, early)
         keep_two.start()
+        out = pltpu.make_async_copy(y, y_out.at[whole], io_sem.at[0])
 
         @pl.when(section == 0)
         def _():
             projected(part_two, act, wdown, half, base)
             two_b.start()
-
-        @pl.when(slot == 0)
-        def _():
-            second.arrive(0)
-            brought = times(chosen[...], spares[...])
-            for which, target in enumerate((xs, dys)):
-
-                @pl.when(section == which)
-                def _():
-                    target[count:] = (target[count:].astype(F32) + brought).astype(BF16)
-
-        out = pltpu.make_async_copy(y, y_out.at[whole], io_sem.at[0])
-
-        @pl.when(section == 0)
-        def _():
             run_steps(tiles, two_a.steps, (two_a.step, 0))
             run_steps(0, two_b.steps, (two_b.step, 0))
             out.start()
             two_a.finish()
             two_b.finish()
-
-        gather.finish()
-        one_a.finish()
-        one_b.finish()
+            for gather in gathers:
+                gather.finish()
+            one_a.finish()
+            one_b.finish()
+
         keep_two.wait()
-        given(0, giving)
 
         @pl.when(slot == 0)
         def _():
             second.finish()
-
-        @pl.when(section == 0)
-        def _():
-            out.wait()
 
         for index in range(9):
             keep(index, slot).start()
-        announce(meet_sem, neighbours)
+
+        @pl.when(section == 0)
+        def _():
+            out.wait()
+            announce(meet_sem, neighbours)
 
     def backward(slot):
-        giving = jnp.logical_or(section == 0, slot == 1)
+        giving = jnp.logical_and(section == 1, slot == 1)
         later = jnp.logical_and(section == 1, slot == 0)
         base = slot * count
         whole = span(base, count)
@@ -1465,41 +1536,14 @@
         dkv[...] = jnp.zeros_like(dkv)
         heard(meet_sem, neighbours)
 
-        def hidden(first, each=None):
-            here = span(base + first, half)
-
-            def one(i, c):
-                columns = lanes(i, WIDE)
-                d_act = with_transpose(dys[here], wdown[columns, :])
-                gate_pre, up_pre = gate[here, columns].astype(F32), up[here, columns].astype(F32)
-                sigma = jax.nn.sigmoid(gate_pre)
-                d_silu = d_act * sigma
-                dup[here, columns] = (d_silu * gate_pre).astype(BF16)
-                dgate[here, columns] = (d_silu * up_pre * (1.0 + gate_pre * (1.0 - sigma))).astype(BF16)
-                if each:
-                    each(i)
-                return c
-
-            lax.fori_loop(0, tiles, one, 0)
-
-        def back_hidden(first):
-            here, there = span(first, half), span(base + first, half)
-
-            def one(i, c):
-                columns = lanes(i, WIDE)
-                total = with_transpose(dgate[there], wgate[columns, :]) + with_transpose(dup[there], wup[columns, :])
-                part_one[here, columns] = total.astype(BF16)
-                return c
-
-            lax.fori_loop(0, wide, one, 0)
-
-        hidden(0)
-        back_hidden(0)
+        @pl.when(section == 0)
+        def _():
+            ffn_back(slot, 0)
+
         one_a.start()
-        hidden(half)
-        back_hidden(half)
+        ffn_back(slot, half)
         one_b.start()
-        give_back(1 - section, giving, one_a)
+        give_back(0, giving, one_a)
 
         def attend(first, g, each=None):
             def one(i, c):
@@ -1509,7 +1553,7 @@
                 k_rows = kv[span(slot * keys, keys), lanes(g)]
                 scores = with_transpose(q[here, lanes(h)], k_rows) * scale
                 code = kcode[slot]
-                allowed = jnp.logical_and(code <= qcode[here], code >= qstart[here])
+                allowed = jnp.logical_and(code <= qcode[here][:, :1], code >= qstart[here][:, :1])
                 known = lse[span((slot * q_heads + h) * count + first + n * rows, rows)][:, :1]
                 prob = jnp.where(allowed, jnp.exp(scores - known), 0.0)
                 dm = dmixed[near, lanes(h)]
@@ -1547,7 +1591,15 @@
             shares[g][:, :LANES] = jnp.transpose(dkv[lanes(g), :]).astype(BF16)
             shares[g][:, LANES:] = jnp.transpose(dkv[lanes(k_heads + g), :]).astype(BF16)
             scatters[g].start()
-        run_steps(0, scatters[0].steps(1), *[(functools.partial(lambda s, i: s.step(i, 1), s), 0) for s in scatters])
+        far = give_lag
+        everyone = [(functools.partial(lambda s, i: s.step(i, far), s), 0) for s in scatters]
+        run_steps(0, scatters[0].chunks, *everyone)
+
+        @pl.when(later)
+        def _():
+            begin(1, False)
+
+        run_steps(far, far + scatters[0].chunks, *everyone)
         for g in range(k_heads):
             dqkv[whole, lanes(q_heads + g)] = rolled(owns[g][:, :LANES], cosine[whole], -sine[whole]).astype(BF16)
             dqkv[whole, lanes(q_heads + k_heads + g)] = owns[g][:, LANES:].astype(BF16)
@@ -1583,16 +1635,32 @@
         one_b.finish()
         for item in scatters:
             item.finish()
-        given(1 + section, giving)
+        given(2, giving)
         for index in range(9, 14):
             keep(index, slot).start()
         announce(meet_sem, neighbours)
 
+    def give_alone(slot, place):
+        heard(meet_sem, neighbours)
+        spares[...] = times(holder[slot * groups * spare : (slot + 1) * groups * spare], y[...]).astype(BF16)
+        give.start()
+        run_steps(0, give.steps(give_lag), (lambda i: give.step(i, give_lag), 0))
+        given(place, section == 0)
+        announce(meet_sem, neighbours)
+
     def turn(k, carry):
         @pl.when(jnp.where(section == 0, k < 2, lax.rem(k, 2) == 0))
         def _():
             forward(jnp.where(section == 0, jnp.minimum(k, 1), k // 2))
 
+        @pl.when(jnp.logical_and(section == 0, k == 2))
+        def _():
+            give_alone(1, 1)
+            again = pltpu.make_async_copy(y_out.at[:count], y, io_sem.at[0])
+            again.start()
+            again.wait()
+            give_alone(0, 0)
+
         @pl.when(jnp.where(section == 0, k == 2, lax.rem(k, 2) == 1))
         def _():
             backward(jnp.where(section == 0, 0, k // 2))
@@ -1600,15 +1668,12 @@
         return carry
 
     lax.fori_loop(0, 3 + section, turn, 0)
-    heard(meet_sem, neighbours)
 
     @pl.when(section == 0)
     def _():
-        spares[...] = times(holder[: groups * spare], y[...]).astype(BF16)
-        give.start()
-        run_steps(0, give.steps(give_lag), (lambda i: give.step(i, give_lag), 0))
-
-    given(2, section == 0)
+        give_alone(0, 2)
+
+    heard(meet_sem, neighbours)
     for k in range(2):
         Line(
             k * half,
@@ -1637,10 +1702,10 @@
         keep(9, 1).wait()
 
 
-def main_ticks(packed, second, spots, holder, weights, groups, q_heads, k_heads, cid):
+def main_ticks(rows, spots, holder, weights, qkv, groups, q_heads, k_heads, cid):
     norm_one, wqkv, wout, norm_two, wgate, wup, wdown = weights
-    count, width = packed.shape
-    own_second, extra_second, chosen = second
+    own_rows, extra_first, extra_second, chosen = rows
+    count, width = own_rows.shape[0] // 2, own_rows.shape[1]
     hidden, keys = wgate.shape[1], groups * count
     pieces = 5
     vmem = pl.BlockSpec(memory_space=pltpu.VMEM)
@@ -1676,17 +1741,18 @@
         shape(both),
     ]
     outs += state + [shape(width, 1, F32)] * 2
-    far_weights = [wqkv, wout, wgate, wup, wdown]
+    near_weights = [wqkv, wout, wgate, wup, wdown]
+    far_weights = [*qkv, wout, wgate, wup, wdown]
     scratch = [pltpu.VMEM(item.shape, item.dtype) for item in state] + [dma((14, 2))]
-    scratch += [pltpu.VMEM(item.shape, BF16) for item in far_weights]
+    scratch += [pltpu.VMEM(item.shape, BF16) for item in near_weights]
     scratch += [pltpu.VMEM((count, width), BF16)] * 4 + [
         pltpu.VMEM((count, heads), BF16),
         pltpu.VMEM((2 * k_heads * LANES, keys), F32),
-        dma((5,)),
+        dma((7,)),
         dma((3,)),
         pltpu.SemaphoreType.REGULAR((2 + dp_bits(groups),)),
     ]
-    scratch += Gather.scratch(groups)
+    scratch += Gather.scratch(groups) * 2
     for k in range(4):
         scratch += Line.scratch(quarter_rows(count), pieces, width, False)
     scratch += [dma((2, 2, pieces)), dma((4, 2, pieces))] * 2
@@ -1699,14 +1765,14 @@
     return pl.pallas_call(
         functools.partial(main_kernel, groups, q_heads, k_heads, pieces),
         out_shape=outs,
-        in_specs=[vmem] * 9 + [far] * 8,
+        in_specs=[vmem] * 9 + [far] * 10,
         out_specs=[far] * (len(outs) - 2) + [vmem] * 2,
         scratch_shapes=scratch,
         compiler_params=pltpu.CompilerParams(
             collective_id=cid, has_side_effects=True, vmem_limit_bytes=VMEM_LIMIT
         ),
         name="main_ticks",
-    )(*spots, norm_one[None], norm_two[None], holder, chosen, packed, own_second, extra_second, *far_weights)
+    )(*spots, norm_one[None], norm_two[None], holder, chosen, own_rows, extra_first, extra_second, *far_weights)
 
 
 def quarter_rows(count):
@@ -2021,7 +2087,15 @@
     section, t = lax.axis_index("section"), lax.axis_index("tensor")
     mine = section == 0
     order = [9, 0, 3, 4, 5, 1, 2, 6, 7, 8]
-    loads = [pltpu.make_async_copy(sources[k].at[sources[k].shape[0] - kept[k].shape[0] :], kept[k], w_sem.at[k]) for k in range(10)]
+
+    def load(k):
+        here, there = sources[k].at[sources[k].shape[0] - kept[k].shape[0] :], kept[k]
+        if k in (7, 8):
+            here, there = sources[k].at[:count], kept[k].at[:count]
+        return pltpu.make_async_copy(here, there, w_sem.at[k])
+
+    lack = pltpu.make_async_copy(sources[7].at[count:], dqkv.at[count:], w_sem.at[13])
+    loads = [load(k) for k in range(10)]
     for k in order:
         loads[k].start()
     known = pltpu.make_async_copy(dx_known.at[count:], dx, w_sem.at[11])
@@ -2037,6 +2111,7 @@
     @pl.when(section > 0)
     def _():
         known.start()
+        lack.start()
 
     for k in range(1, 4):
         greet({"tensor": lax.rem(t + k, 4)})
@@ -2047,7 +2122,7 @@
     pl.semaphore_wait(pltpu.get_barrier_semaphore(), 3 + levels)
     loads[9].wait()
     up_task.start()
-    for k in order[1:]:
+    for k in (0, 3, 4, 5):
         loads[k].wait()
 
     wide, jobs = width // WIDE, width // TILE
@@ -2122,6 +2197,7 @@
     def _():
         run_steps(0, begun, (early, 0))
         known.wait()
+        lack.wait()
 
     ends = [0]
     for item in (spread_q, spread_k, spread_v, spread_o):
@@ -2135,6 +2211,8 @@
         spares_y[...] = times(holder[...], part[...]).astype(BF16)
         give_y.start()
 
+    for k in (1, 2, 6, 7, 8):
+        loads[k].wait()
     load_n1.wait()
     plain_mixed[...] = with_transpose(mixed[...], spread_o[...]).astype(BF16)
     other_dresid[count:] = dresid[...]
@@ -2272,7 +2350,7 @@
         pltpu.VMEM(gains.shape, F32),
         pltpu.VMEM((3,) + gains.shape, F32),
         pltpu.VMEM((groups * 8, block), F32),
-        dma((13,)),
+        dma((14,)),
         dma((3,)),
         dma((3,)),
     ]
@@ -2421,16 +2499,17 @@
     )(live, through, y, *y_backs, cot, dx_first, dx_second, back_first, back_second, gate, up, down, attn)
 
 
-def rope_tables(pos):
+def rope_tables(seq_len):
     half_width = HD // 2
-    inverse = rope_base ** (-(jnp.arange(half_width, dtype=F32) * 2.0 / HD))
-    angle = pos.astype(F32)[:, None] * inverse[None, :]
-    blank = jnp.zeros((pos.shape[0], LANES // 2 - half_width), F32)
-    cosine, sine = jnp.cos(angle), jnp.sin(angle)
-    return (
-        jnp.concatenate([cosine, blank, cosine, blank], axis=1),
-        jnp.concatenate([-sine, blank, sine, blank], axis=1),
-    )
+    inverse = np.float32(rope_base) ** (-(np.arange(half_width, dtype=np.float32) * np.float32(2.0) / np.float32(HD)))
+    angle = np.arange(seq_len, dtype=np.float32)[:, None] * inverse[None, :].astype(np.float32)
+    cosine, sine = np.cos(angle), np.sin(angle)
+    table = np.zeros((seq_len, 4, LANES // 2), np.float32)
+    table[:, 0, :half_width] = cosine
+    table[:, 1, :half_width] = cosine
+    table[:, 2, :half_width] = -sine
+    table[:, 3, :half_width] = sine
+    return table.reshape(seq_len, 2 * LANES)
 
 
 def spreader(heads, turned):
@@ -2479,40 +2558,38 @@
     q_heads, k_heads = w_query.shape[2] // HD, w_key.shape[2] // HD
     spread_q, spread_k = spreader(q_heads, True), spreader(k_heads, True)
     spread_v, spread_o = spreader(k_heads, False), spreader(q_heads, False)
-    wqkv = jnp.concatenate(
-        [times(w_query[0], spread_q), times(w_key[0], spread_k), times(w_value[0], spread_v)], axis=1
-    ).astype(BF16)
+    qkv = [
+        times(item[0], spread).astype(BF16)
+        for item, spread in ((w_query, spread_q), (w_key, spread_k), (w_value, spread_v))
+    ]
+    wqkv = jnp.concatenate(qkv, axis=1)
     wout = rows_contract(spread_o, w_out[0]).astype(BF16)
     weights = (norm_attn[0], wqkv, wout, norm_ffn[0], w_gate[0], w_up[0], w_down[0])
 
     all_in_one = micro == 2 and groups == 4
 
-    source = jnp.where(first, inputs[:, 0], cotangent[:, 0])
-    first_extra = lax.all_gather(source[0, count:], "dp", axis=0, tiled=True)
+    extras = [jnp.where(first, inputs[b, 0, count:], cotangent[b, 0, count:]) for b in range(micro)]
+    first_extra = lax.all_gather(extras[0], "dp", axis=0, tiled=True)
     length_rows = jnp.broadcast_to(lengths[:, 0].astype(F32)[:, None], (micro, LANES))
     length_rows = jnp.concatenate([length_rows, jnp.zeros((8 - micro, LANES), F32)], axis=0)
     (length_all,) = gather_rows([length_rows], groups, 4)
     lens = length_all.reshape(groups, 8, LANES)[:, :micro, 0].T.astype(jnp.int32)
-    packed, slots, chosen, kept_own = [], [], [], []
+    packed, slots, spots, chosen, kept_own = [], [], [], [], []
     for b in range(micro):
         seq, pos, own = slots_of(lens[b], count)
         slots.append((seq, pos))
-        wanted = seq[me] * spare + pos[me] - count
-        chosen.append(
-            jnp.logical_and(jnp.arange(groups * spare)[None, :] == wanted[:, None], ~own[me][:, None]).astype(BF16)
-        )
-        kept_own.append(jnp.where(own[me][:, None], source[b, :count], jnp.zeros((), BF16)))
-    for b in range(1 if all_in_one else micro):
-        extra = first_extra if b == 0 else lax.all_gather(source[b, count:], "dp", axis=0, tiled=True)
-        brought = times(chosen[b], extra)
-        packed.append((kept_own[b].astype(F32) + brought).astype(BF16))
-
-    def spots_of(b):
-        seq, pos = slots[b]
-        code = seq * seq_len + pos
-        return rope_tables(pos[me]) + (code[me][:, None], (seq[me] * seq_len)[:, None], code.reshape(1, -1))
-
-    spots = [spots_of(b) for b in range(micro)]
+        my_seq, my_pos, own = seq[me][:, None], pos[me][:, None], own[me][:, None]
+        here = (jnp.arange(seq_len)[None, :] == my_pos).astype(F32)
+        turned = jnp.dot(here, rope_tables(seq_len), precision=lax.Precision.HIGHEST)
+        code = (seq * seq_len + pos).reshape(1, -1)
+        spots.append((turned[:, :LANES], turned[:, LANES:], my_seq * seq_len + my_pos, my_seq * seq_len, code))
+        wanted = jnp.where(own, -1, my_seq * spare + my_pos - count)
+        chosen.append((jnp.arange(groups * spare)[None, :] == wanted).astype(BF16))
+        kept = jnp.where(first, inputs[b, 0, :count], cotangent[b, 0, :count])
+        kept_own.append(jnp.where(own, kept, jnp.zeros((), BF16)))
+    for b in range(0 if all_in_one else micro):
+        extra = first_extra if b == 0 else lax.all_gather(extras[b], "dp", axis=0, tiled=True)
+        packed.append((kept_own[b].astype(F32) + times(chosen[b], extra)).astype(BF16))
 
     def holder(b):
         seq, pos = slots[b]
@@ -2542,11 +2619,11 @@
         joined[4] = joined[4][:, None]
         held = jnp.concatenate([holder(b) for b in range(micro)], axis=0).astype(BF16)
         y, dx, y_back, normed_one, normed_two, x, q, kv, lse, mixed, resid, gate, up, act, dy, d_resid, d_gate, d_up, d_qkv, gain_one, gain_two = main_ticks(
-            packed[0],
-            (kept_own[1], source[1, count:], chosen[1]),
+            (jnp.concatenate(kept_own, axis=0), first_extra, extras[1], jnp.concatenate(chosen, axis=0)),
             joined,
             held,
             weights,
+            qkv,
             groups,
             q_heads,
             k_heads,

time: 610 us -> 590 us (0.967); the launches traced: 603 us -> 590 us
  no operation moved by 1% of the time
where the time goes in v6:
time: 590 us
  Pallas kernels  543 us (92%)
  other arithmetic  15.9 us (3%)
  between operations  14.7 us (2%)
  local copies, waits for them, and re-layouts  11.3 us (2%)
    pallas_call x1, Pallas kernels, main_ticks(): pl.pallas_call(functools.partial(main_kernel, groups, q_heads, k_heads, p...  379 us
    pallas_call x1, Pallas kernels, last_attn(): pl.pallas_call(functools.partial(last_attn_kernel, groups, q_heads, k_hea...  87.5 us
    pallas_call x1, Pallas kernels, last_ffn(): pl.pallas_call(functools.partial(last_ffn_kernel, groups, pieces, chunks)...  57.7 us
    pallas_call x1, Pallas kernels, finish(): pl.pallas_call(functools.partial(finish_kernel, groups, parts), out_shape...  13.1 us
  transfers between devices with their start and end apart: 1, of which 0 were waited for; matrix products, arithmetic and copies ran while one was open for 4% of the time, Pallas kernels for 1%

profile of v6, /device:TPU:0, one launch (start us, length us, event | category | flops | bytes accessed | tf_op | source)
XLA Modules:
  0.0 590.2 jit_solution(16049357621543997689)
XLA Ops:
  7.3 2.9 select_bitcast_fusion
  10.3 5.4 gather_4.1
  21.0 0.8 copy.76.refs_3_
  21.9 0.9 copy.73.refs_3_
  23.6 1.0 copy.83
  24.6 1.1 add_convert_fusion.1.refs_8_
  25.7 0.7 pad_maximum_fusion.2.refs_0_
  26.5 0.8 pad_maximum_fusion.3.refs_1_
  27.5 0.8 pad_add_fusion.refs_2_
  28.4 0.8 fusion.17
  29.4 1.1 fusion.7
  31.8 1.1 fusion.46
  33.1 1.8 copy-done.2
  35.2 1.4 pad_maximum_fusion.1.refs_9_
  36.6 2.2 convolution_convert_fusion.refs_15_.refs_13_
  38.8 1.1 fusion.refs_12_
  39.9 1.1 copy-done.7
  41.1 1.9 pad_maximum_fusion.refs_14_
  42.9 379.0 %main_ticks.1 = (bf16[640,1536]{1,0:T(8,128)(2,1)}, bf16[640,1536]{1,0:T(8,128)(2,1)}, bf16[576,1536]{1,0:T(8,128)(2,1)}, bf16[640,1536]{1,0:T(8,128)(2,1)}, bf1...) custom-call(f32[640,128]{1,0:T(8,128)} %pad_maximum_fusion.2.refs_0_, ...), custom_call_target="tpu_custom_call" | custom-call | tf_op jit(solution)/shard_map/main_ticks/pallas_call | solution.py:1765
  422.0 57.7 %last_ffn.1 = (bf16[320,1536]{1,0:T(8,128)(2,1)}, f32[1,1536]{1,0:T(1,128)}, bf16[1536,1024]{1,0:T(8,128)(2,1)}, f32[384,1024]{1,0:T(8,128)}, f32[384,1024]{1,0:...) custom-call(f32[1,1536]{1,0:T(1,128)} %refs_0_.1, bf16[768,320]{1,0:T(8,128)(2,1)} %get-tuple-element.120.refs_1_, ...), custom_call_target="tpu_custom_call" | custom-call | tf_op jit(solution)/shard_map/last_ffn/pallas_call | solution.py:2029
  479.8 0.7 fusion.25
  481.2 87.5 %last_attn.1 = (bf16[320,1536]{1,0:T(8,128)(2,1)}, bf16[192,1536]{1,0:T(8,128)(2,1)}, bf16[192,1536]{1,0:T(8,128)(2,1)}, f32[8,384]{1,0:T(8,128)}, f32[384,1024]{1,0:T(8,128)}, /*index=5*/f32[384,1152]{1,0:T(8,128)}) custom-call(f32[320,128]{1,0:T(8,128)} %copy-done.10, f32[320,128]{1,0:T(8,128)} %copy-done.9, s32[320,1]{1,0:T(8,128)} %copy-done.11, ...), custom_call_target="tpu_custom_call" | custom-call | tf_op jit(solution)/shard_map/last_attn/pallas_call | solution.py:2365
  568.7 1.4 fusion.49
  570.1 13.1 %finish.1 = (bf16[1,2,1,512,1536]{4,3,2,1,0:T(8,128)(2,1)}, bf16[1,2,1,512,1536]{4,3,2,1,0:T(8,128)(2,1)}, f32[1,384,384]{2,1,0:T(8,128)}, f32[1,192,384]{2,1,0:...) custom-call(s32[1024,1]{1,0:T(8,128)} %bitcast.92, ...), custom_call_target="tpu_custom_call" | custom-call | tf_op jit(solution)/shard_map/finish/pallas_call | solution.py:2491
  (116 shorter events, 9.1 us)
Async XLA Ops:
  7.2 29.4 %copy-start = (bf16[1,384,1536]{2,1,0:T(8,128)(2,1)S(1)}, bf16[1,384,1536]{2,1,0:T(8,128)(2,1)}, u32[]{:S(2)}) copy-start(bf16[1,384,1536]{2,1,0:T(8,128)(2,1)} %param.21) | copy-start | bytes 3538948
  7.2 35.8 %all-gather.3.cloned.1.call-start = ((), (), s32[]{:S(2)}) async-start(), calls=%async_computation | async-start | bytes 2949120 | tf_op jit(solution)/shard_map/all_gather | solution.py:2572
  7.2 2.9 copy-start.18
  7.3 10.6 %copy-start.8 = (f32[512,256]{1,0:T(8,128)S(1)}, f32[512,256]{1,0:T(8,128)}, u32[]{:S(2)}) copy-start(f32[512,256]{1,0:T(8,128)} %constant.57.clone) | copy-start | bytes 1572868
  20.0 5.7 copy-start.14
  20.7 6.6 %copy-start.9 = (f32[320,128]{1,0:T(8,128)}, f32[320,128]{1,0:T(8,128)S(1)}, u32[]{:S(2)}) copy-start(f32[320,128]{1,0:T(8,128)S(1)} %get-tuple-element.123.refs_1_) | copy-start | bytes 491524
  20.7 6.5 %copy-start.10 = (f32[320,128]{1,0:T(8,128)}, f32[320,128]{1,0:T(8,128)S(1)}, u32[]{:S(2)}) copy-start(f32[320,128]{1,0:T(8,128)S(1)} %get-tuple-element.124.refs_0_) | copy-start | bytes 491524
  20.9 6.6 %copy-start.11 = (s32[320,1]{1,0:T(8,128)}, s32[320,1]{1,0:T(8,128)S(1)}, u32[]{:S(2)}) copy-start(s32[320,1]{1,0:T(8,128)S(1)} %copy.69.refs_2_) | copy-start | bytes 3844
  25.7 4.7 copy-start.12
  27.3 3.7 copy-start.13
  30.5 2.6 copy-start.3
  31.0 8.9 %copy-start.5 = (bf16[1536,256]{1,0:T(8,128)(2,1)}, bf16[1536,256]{1,0:T(8,128)(2,1)S(1)}, u32[]{:S(2)}) copy-start(bf16[1536,256]{1,0:T(8,128)(2,1)S(1)} %fusion.1.refs_13_) | copy-start | bytes 2359300
  31.5 8.4 %copy-start.6 = (bf16[1536,256]{1,0:T(8,128)(2,1)}, bf16[1536,256]{1,0:T(8,128)(2,1)S(1)}, u32[]{:S(2)}) copy-start(bf16[1536,256]{1,0:T(8,128)(2,1)S(1)} %fusion.2.refs_14_) | copy-start | bytes 2359300
  31.5 3.3 copy-start.2
  31.8 3.3 copy-start.4
  36.6 2.2 copy-start.17
  39.9 1.1 copy-start.7
  422.0 57.8 %copy-start.15 = (f32[1,1536]{1,0:T(1,128)S(1)}, f32[1,1536]{1,0:T(1,128)}, u32[]{:S(2)}) copy-start(f32[1,1536]{1,0:T(1,128)} %get-tuple-element.69) | copy-start | bytes 18436
  422.0 58.5 %copy-start.16 = (f32[1,1536]{1,0:T(1,128)S(1)}, f32[1,1536]{1,0:T(1,128)}, u32[]{:S(2)}) copy-start(f32[1,1536]{1,0:T(1,128)} %get-tuple-element.68) | copy-start | bytes 18436
  570.1 13.1 %copy-start.1 = (bf16[1,384,1536]{2,1,0:T(8,128)(2,1)S(1)}, bf16[1,384,1536]{2,1,0:T(8,128)(2,1)}, u32[]{:S(2)}) copy-start(bf16[1,384,1536]{2,1,0:T(8,128)(2,1)} %param.21) | copy-start | bytes 3538948
Sparse Core Ops, SparseCore 0:
  10.3 26.7 all-gather.2

commit v7 on v6

--- a/solution.py
+++ b/solution.py
@@ -1793,10 +1793,10 @@
         return taken
 
     gain, holder = take(2)
-    sources = take(14)
-    last_dresid, gsum, g_up, down_sum, gate_sum, y, returned = take(7)
+    sources = take(15)
+    last_dresid, gsum, g_up, down_sum, gate_sum, y, returned, returned_dx = take(8)
     wdown, wgate, wup, dys, act, gate, up, dgate, dup, resid = kept = take(10)
-    n2, part, g_down, g_gate, spares, w_sem = take(6)
+    n2, part, g_down, g_gate, spares, spares_dx, dx, w_sem = take(8)
     line_scratch = [take(12) for _ in range(4)]
     count, width = last_dresid.shape
     half = count // 2
@@ -1819,6 +1819,8 @@
     gated = OwnScatter(groups, width // groups, chunks, [g_gate, gate_sum] + take(OwnScatter.refs(groups)))
     spare = returned.shape[0]
     give = OwnScatter(groups, spare, spare // 32, [spares, returned] + take(OwnScatter.refs(groups)))
+    give_dx = OwnScatter(groups, spare, spare // 32, [spares_dx, returned_dx] + take(OwnScatter.refs(groups)))
+    load_dx = pltpu.make_async_copy(sources[14].at[count:], dx, w_sem.at[16])
     section = lax.axis_index("section")
     mine = section == 0
     tiles, wide, blocks = act.shape[1] // WIDE, width // WIDE, width // TILE
@@ -1838,6 +1840,10 @@
         pltpu.make_async_copy(sources[12].at[:spare], returned, w_sem.at[14]),
     ]
     loads = [load(k) for k in range(10)] + [pltpu.make_async_copy(sources[13], n2, w_sem.at[15])]
+    @pl.when(section > 0)
+    def _():
+        load_dx.start()
+
     for k in (3, 0, 5, 6, 1, 2, 4, 9, 10, 7, 8):
         loads[k].start()
 
@@ -1899,9 +1905,10 @@
 
     loads[4].wait()
 
-    @pl.when(section > 0)
-    def _():
-        for k in range(4):
+    late = 100
+
+    def begin_results(which):
+        for k in which:
             here = pl.ds(k * half, half)
 
             def one(i, c):
@@ -1911,7 +1918,13 @@
             lax.fori_loop(0, wide, one, 0)
             results[k].start()
 
-        loads[9].wait()
+    @pl.when(section > 0)
+    def _():
+        load_dx.wait()
+        spares_dx[...] = times(holder[groups * spare :], dx[...]).astype(BF16)
+        give_dx.start()
+        begin_results((0, 1))
+        run_steps(0, give_dx.chunks, (lambda i: give_dx.step(i, late), 0))
 
     def down_job(i, c):
         weight_job(g_down, dys, act, i)
@@ -1919,6 +1932,11 @@
 
     lax.fori_loop(0, blocks, down_job, 0)
     down.start()
+
+    @pl.when(section > 0)
+    def _():
+        begin_results((2, 3))
+        loads[9].wait()
 
     @pl.when(mine)
     def _():
@@ -1938,7 +1956,6 @@
         lacks[0].wait()
         lacks[1].wait()
 
-    late = 100
     spans = 0
 
     first_done = line_a.steps + pieces
@@ -1956,7 +1973,7 @@
 
             @pl.when(i == first_done)
             def _():
-                spares[...] = times(holder[...], y[:count]).astype(BF16)
+                spares[...] = times(holder[: groups * spare], y[:count]).astype(BF16)
                 give.start()
 
             give.step(i - first_done, late)
@@ -1995,8 +2012,10 @@
     @pl.when(section > 0)
     def _():
         lacks[2].wait()
+        run_steps(late, late + give.chunks, (lambda i: give_dx.step(i, late), 0))
         run_steps(late, late + give.chunks, (lambda i: give.step(i, late), 0))
         give.finish()
+        give_dx.finish()
         for item in results:
             item.finish()
 
@@ -2006,8 +2025,8 @@
 
 def last_ffn(known, holder, weights, groups, cid):
     norm_one, wqkv, wout, norm_two, wgate, wup, wdown = weights
-    dys, act, gate, up, dgate, dup, resid, dresid, y, y_back, normed_two = known
-    spare = holder.shape[0] // groups
+    dys, act, gate, up, dgate, dup, resid, dresid, y, y_back, normed_two, dx = known
+    spare = holder.shape[0] // (2 * groups)
     count, width = dys.shape[0] // 2, dys.shape[1]
     hidden = act.shape[1]
     pieces, chunks = 5, 8
@@ -2021,30 +2040,33 @@
         pltpu.VMEM((width, hidden), BF16),
         pltpu.VMEM((width, hidden), BF16),
         pltpu.VMEM((groups * spare, width), BF16),
-        pltpu.SemaphoreType.DMA((16,)),
+        pltpu.VMEM((groups * spare, width), BF16),
+        pltpu.VMEM((count, width), BF16),
+        pltpu.SemaphoreType.DMA((17,)),
     ]
     scratch += Line.scratch(count // 4, pieces, width, False) * 4
     scratch += OwnScatter.scratch(groups, width // groups, hidden, chunks, BF16) * 2
-    scratch += OwnScatter.scratch(groups, spare, width, spare // 32, BF16)
+    scratch += OwnScatter.scratch(groups, spare, width, spare // 32, BF16) * 2
     return pl.pallas_call(
         functools.partial(last_ffn_kernel, groups, pieces, chunks),
         out_shape=[
             jax.ShapeDtypeStruct((count, width), BF16),
             jax.ShapeDtypeStruct((1, width), F32),
             jax.ShapeDtypeStruct((width, hidden), BF16),
-            jax.ShapeDtypeStruct((width // groups, hidden), F32),
-            jax.ShapeDtypeStruct((width // groups, hidden), F32),
+            jax.ShapeDtypeStruct((width // groups, hidden), BF16),
+            jax.ShapeDtypeStruct((width // groups, hidden), BF16),
             jax.ShapeDtypeStruct((2 * count, width), BF16),
             jax.ShapeDtypeStruct((spare, width), BF16),
+            jax.ShapeDtypeStruct((spare, width), BF16),
         ],
-        in_specs=[vmem] * 2 + [far] * 14,
-        out_specs=[vmem] * 7,
+        in_specs=[vmem] * 2 + [far] * 15,
+        out_specs=[vmem] * 8,
         scratch_shapes=scratch,
         compiler_params=pltpu.CompilerParams(
             collective_id=cid, has_side_effects=True, vmem_limit_bytes=VMEM_LIMIT
         ),
         name="last_ffn",
-    )(norm_two[None], holder, *sources, dresid, y, y_back, normed_two)
+    )(norm_two[None], holder, *sources, dresid, y, y_back, normed_two, dx)
 
 
 def last_attn_kernel(groups, q_heads, k_heads, pieces, chunks, spare_chunks, *refs):
@@ -2055,9 +2077,9 @@
         del refs[:count]
         return taken
 
-    cosine, sine, qcode, qstart, kcode, gain, dresid, holder, gains, spread_q, spread_k, spread_v, spread_o = take(13)
+    cosine, sine, qcode, qstart, kcode, gain, dresid, holder, gain_one, gain_two, gain_last, spread_q, spread_k, spread_v, spread_o = take(15)
     sources = take(10)
-    dx_known, y, y_back, normed_one = take(4)
+    dx_known, y, y_back, normed_one, back_known = take(5)
     dx, returned, returned_y, gains_out, up_sum, attn_sum = take(6)
     wout, wqkv, x, q, kv, lse, mixed, dqkv, other_dresid, g_up = kept = take(10)
     plain, plain_mixed = take(2)
@@ -2099,6 +2121,7 @@
     for k in order:
         loads[k].start()
     known = pltpu.make_async_copy(dx_known.at[count:], dx, w_sem.at[11])
+    known_back = pltpu.make_async_copy(back_known, returned, w_sem.at[14])
     load_n1 = pltpu.make_async_copy(normed_one, n1, w_sem.at[10])
     load_n1.start()
     known_y = pltpu.make_async_copy(y_back.at[spare : 2 * spare], returned_y, w_sem.at[12])
@@ -2112,6 +2135,7 @@
     def _():
         known.start()
         lack.start()
+        known_back.start()
 
     for k in range(1, 4):
         greet({"tensor": lax.rem(t + k, 4)})
@@ -2149,25 +2173,36 @@
         lax.fori_loop(0, q_heads, one, 0)
 
     def attend(first, g, each):
-        def one(i, c):
-            h, n = g * repeat + i // blocks, lax.rem(i, blocks)
+        heads = [g * repeat + r for r in range(repeat)]
+
+        def one(n, c):
             here = pl.ds(pl.multiple_of(first + n * rows, rows), rows)
-            scores, allowed = score_rows(q, kv, h, g, here, qcode, qstart, kcode)
-            there = pl.ds(pl.multiple_of(h * count + first + n * rows, rows), rows)
-            prob = jnp.where(allowed, jnp.exp(scores - lse[there][:, :1]), 0.0)
-            dm = dmixed[here, lanes(h)]
+            there = pl.ds(pl.multiple_of(count + first + n * rows, rows), rows)
+            stacked = jnp.concatenate([q[here, lanes(h)] for h in heads], axis=0)
+            scores = with_transpose(stacked, kv[:, lanes(g)]) * scale
+            code = kcode[...]
+            upper = jnp.concatenate([qcode[here][:, :1]] * repeat, axis=0)
+            lower = jnp.concatenate([qstart[here][:, :1]] * repeat, axis=0)
+            allowed = jnp.logical_and(code <= upper, code >= lower)
+            known = jnp.concatenate(
+                [lse[pl.ds(pl.multiple_of(h * count + first + n * rows, rows), rows)][:, :1] for h in heads], axis=0
+            )
+            prob = jnp.where(allowed, jnp.exp(scores - known), 0.0)
+            dm = jnp.concatenate([dmixed[here, lanes(h)] for h in heads], axis=0)
             d_prob = with_transpose(dm, kv[:, lanes(k_heads + g)])
             row_dot = jnp.sum(prob * d_prob, axis=-1, keepdims=True)
             d_scores = (prob * (d_prob - row_dot)).astype(BF16)
             d_query = times(d_scores, kv[:, lanes(g)]) * scale
-            there = pl.ds(pl.multiple_of(count + first + n * rows, rows), rows)
-            dqkv[there, lanes(h)] = rolled(d_query, cosine[here], -sine[here]).astype(BF16)
-            dkv[lanes(g), :] += rows_contract(q[here, lanes(h)], d_scores) * scale
+            for r, h in enumerate(heads):
+                turned = rolled(d_query[r * rows : (r + 1) * rows], cosine[here], -sine[here])
+                dqkv[there, lanes(h)] = turned.astype(BF16)
+            dkv[lanes(g), :] += rows_contract(stacked, d_scores) * scale
             dkv[lanes(k_heads + g), :] += rows_contract(dm, prob.astype(BF16))
-            each(i)
+            for r in range(repeat):
+                each(n * repeat + r)
             return c
 
-        lax.fori_loop(0, turns, one, 0)
+        lax.fori_loop(0, blocks, one, 0)
 
     def back(first):
         here, there = pl.ds(first, half), pl.ds(count + first, half)
@@ -2274,13 +2309,21 @@
         return c
 
     lax.fori_loop(0, max(line_a.steps + line_b.steps, jobs + 1 + chunks), step, 0)
-    spares[...] = times(holder[...], dx[...]).astype(BF16)
-    back_task.start()
-    gains_own[...] = gains[...]
-    gains_own[:1] = gains[:1] + gsum[...] * jnp.where(mine, 1.0, 0.0)
+    @pl.when(mine)
+    def _():
+        spares[...] = times(holder[...], dx[...]).astype(BF16)
+        back_task.start()
+
+    gains_own[...] = jnp.zeros_like(gains_own)
+    gains_own[:1] = gain_one[...] + jnp.where(mine, gsum[...], 0.0)
+    gains_own[1:2] = gain_two[...] + jnp.where(mine, gain_last[...], 0.0)
     for k in range(1, 4):
         spread(k).start()
-    run_steps(0, spare_chunks, (lambda i: back_task.step(i, late), 0))
+
+    @pl.when(mine)
+    def _():
+        run_steps(0, spare_chunks, (lambda i: back_task.step(i, late), 0))
+
     for k in range(1, 4):
         spread(k).wait()
     total = gains_own[...] + gains_all[0] + gains_all[1] + gains_all[2]
@@ -2301,7 +2344,16 @@
         return c
 
     lax.fori_loop(0, max(chunks, spare_chunks, small.steps(4)), close, 0)
-    run_steps(late, late + spare_chunks, (lambda i: back_task.step(i, late), 0))
+
+    @pl.when(mine)
+    def _():
+        run_steps(late, late + spare_chunks, (lambda i: back_task.step(i, late), 0))
+        back_task.finish()
+
+    @pl.when(section > 0)
+    def _():
+        known_back.wait()
+
 
     @pl.when(mine)
     def _():
@@ -2315,11 +2367,11 @@
     def _():
         give_y.finish()
 
-    for item in (up_task, attn_task, back_task, small):
+    for item in (up_task, attn_task, small):
         item.finish()
 
 
-def last_attn(known, spots, dresid, dx, y, y_back, normed_one, holder, gains, spreads, grads, weights, groups, q_heads, k_heads, cid):
+def last_attn(known, spots, dresid, dx, y, y_back, normed_one, back_known, holder, gains, spreads, grads, weights, groups, q_heads, k_heads, cid):
     norm_one, wqkv, wout, norm_two, wgate, wup, wdown = weights
     x, q, kv, lse, mixed, dqkv, other_dresid = known
     count, width = dresid.shape
@@ -2347,10 +2399,10 @@
         pltpu.VMEM((groups * spare, width), BF16),
         pltpu.VMEM((groups * spare, width), BF16),
         pltpu.VMEM((1, width), F32),
-        pltpu.VMEM(gains.shape, F32),
-        pltpu.VMEM((3,) + gains.shape, F32),
+        pltpu.VMEM((8, width), F32),
+        pltpu.VMEM((3, 8, width), F32),
         pltpu.VMEM((groups * 8, block), F32),
-        dma((14,)),
+        dma((15,)),
         dma((3,)),
         dma((3,)),
     ]
@@ -2369,17 +2421,17 @@
             jax.ShapeDtypeStruct((spare, width), BF16),
             jax.ShapeDtypeStruct((spare, width), BF16),
             jax.ShapeDtypeStruct((8, block), F32),
-            jax.ShapeDtypeStruct((block, grads[0].shape[1]), F32),
-            jax.ShapeDtypeStruct((block, attn_width), F32),
+            jax.ShapeDtypeStruct((block, grads[0].shape[1]), BF16),
+            jax.ShapeDtypeStruct((block, attn_width), BF16),
         ],
-        in_specs=[vmem] * 13 + [far] * 14,
+        in_specs=[vmem] * 15 + [far] * 15,
         out_specs=[vmem] * 6,
         scratch_shapes=scratch,
         compiler_params=pltpu.CompilerParams(
             collective_id=cid, has_side_effects=True, vmem_limit_bytes=VMEM_LIMIT
         ),
         name="last_attn",
-    )(*spots, norm_one[None], dresid, holder, gains, *spreads, *sources, dx, y, y_back, normed_one)
+    )(*spots, norm_one[None], dresid, holder, *gains, *spreads, *sources, dx, y, y_back, normed_one, back_known)
 
 
 def finish_kernel(groups, parts, *refs):
@@ -2390,16 +2442,17 @@
         del refs[:count]
         return taken
 
-    (live,) = take(1)
+    live, gains = take(2)
     through, y, y_first, y_second, cot, dx_first, dx_second, back_first, back_second = take(9)
     gate, up, down, attn = take(4)
     acts, backs = take(2)
     outs = take(7)
+    gain_one_out, gain_two_out = take(2)
     tiles = take(4)
     rows = take(4)
     backs_near = take(4)
     down_near, down_turned, attn_near, *attn_parts = take(7)
-    plain_near = take(2)
+    plain_near, plain_wide = take(2), take(2)
     sems, out_sems = take(2)
     count, spare = rows[0].shape[0], backs_near[0].shape[0]
     seq = count + spare
@@ -2411,7 +2464,7 @@
     ]
     query_out, key_out, value_out, out_out, gate_out, up_out, down_out = outs
     plain_in = [pltpu.make_async_copy(a, b, sems.at[14 + k]) for k, (a, b) in enumerate(zip((gate, up), plain_near))]
-    plain = [pltpu.make_async_copy(a, b, out_sems.at[k]) for k, (a, b) in enumerate(zip(plain_near, (gate_out.at[0], up_out.at[0])))]
+    plain = [pltpu.make_async_copy(a, b, out_sems.at[k]) for k, (a, b) in enumerate(zip(plain_wide, (gate_out.at[0], up_out.at[0])))]
     load_down = pltpu.make_async_copy(down, down_near, sems.at[12])
     load_attn = pltpu.make_async_copy(attn, attn_near, sems.at[13])
     loads = []
@@ -2433,16 +2486,19 @@
     load_attn.wait()
     at = 0
     for k, (size, near, there) in enumerate(zip(parts, attn_parts, (query_out, key_out, value_out, out_out))):
-        value = attn_near[:, at : at + size]
+        value = attn_near[:, at : at + size].astype(F32)
         near[...] = value if k == 0 else jnp.transpose(value)
         at += size
         stores.append(pltpu.make_async_copy(near, there.at[0], out_sems.at[2 + k]))
         stores[-1].start()
-    for before, item in zip(plain_in, plain):
+    gain_one_out[...] = gains[:1]
+    gain_two_out[...] = gains[1:2]
+    for before, near, wide, item in zip(plain_in, plain_near, plain_wide, plain):
         before.wait()
+        wide[...] = near[...].astype(F32)
         item.start()
     load_down.wait()
-    down_turned[...] = jnp.transpose(down_near[...])
+    down_turned[...] = jnp.transpose(down_near[...].astype(F32))
     stores.append(pltpu.make_async_copy(down_turned, down_out.at[0], out_sems.at[6]))
     stores[-1].start()
     for k, group in enumerate(loads):
@@ -2472,7 +2528,7 @@
         item.wait()
 
 
-def finish(live, through, y, y_backs, cot, dx_first, dx_second, back_first, back_second, grads, parts, groups):
+def finish(live, gains, through, y, y_backs, cot, dx_first, dx_second, back_first, back_second, grads, parts, groups):
     count, width = dx_second.shape
     spare = back_second.shape[0]
     gate, up, down, attn = grads
@@ -2482,21 +2538,22 @@
     shapes = [(block, parts[0])] + [(size, block) for size in parts[1:]]
     outs = [jax.ShapeDtypeStruct((1, 2, 1, count + spare, width), BF16)] * 2
     outs += [jax.ShapeDtypeStruct((1,) + item, F32) for item in shapes + [gate.shape, up.shape, (hidden, block)]]
+    outs += [jax.ShapeDtypeStruct((1, block), F32)] * 2
     scratch = [pltpu.VMEM((count + spare, width), BF16)] * 4
     scratch += [pltpu.VMEM((count, width), BF16)] * 4 + [pltpu.VMEM((spare, width), BF16)] * 4
-    scratch += [pltpu.VMEM(down.shape, F32), pltpu.VMEM((hidden, block), F32), pltpu.VMEM(attn.shape, F32)]
+    scratch += [pltpu.VMEM(down.shape, BF16), pltpu.VMEM((hidden, block), F32), pltpu.VMEM(attn.shape, BF16)]
     scratch += [pltpu.VMEM(item, F32) for item in shapes]
-    scratch += [pltpu.VMEM(gate.shape, F32), pltpu.VMEM(up.shape, F32)]
+    scratch += [pltpu.VMEM(gate.shape, BF16)] * 2 + [pltpu.VMEM(gate.shape, F32)] * 2
     scratch += [pltpu.SemaphoreType.DMA((16,)), pltpu.SemaphoreType.DMA((11,))]
     return pl.pallas_call(
         functools.partial(finish_kernel, groups, parts),
         out_shape=outs,
-        in_specs=[vmem] + [far] * 13,
-        out_specs=[far] * 9,
+        in_specs=[vmem] * 2 + [far] * 13,
+        out_specs=[far] * 9 + [vmem] * 2,
         scratch_shapes=scratch,
         compiler_params=pltpu.CompilerParams(vmem_limit_bytes=VMEM_LIMIT),
         name="finish",
-    )(live, through, y, *y_backs, cot, dx_first, dx_second, back_first, back_second, gate, up, down, attn)
+    )(live, gains, through, y, *y_backs, cot, dx_first, dx_second, back_first, back_second, gate, up, down, attn)
 
 
 def rope_tables(seq_len):
@@ -2629,11 +2686,9 @@
             k_heads,
             0,
         )
-        last_dresid, gain_last, grad_up, grad_down, grad_gate, y, y_first = last_ffn(
-            (dy, act, gate, up, d_gate, d_up, resid, d_resid, y, y_back, normed_two), held[: groups * spare], weights, groups, 1
+        last_dresid, gain_last, grad_up, grad_down, grad_gate, y, y_first, back_known = last_ffn(
+            (dy, act, gate, up, d_gate, d_up, resid, d_resid, y, y_back, normed_two, dx), held, weights, groups, 1
         )
-        gain_last = jnp.where(first, gain_last, jnp.zeros_like(gain_last))
-        gains = jnp.concatenate([gain_one, gain_two + gain_last, jnp.zeros((6, width), F32)], axis=0)
         last_dx, back_second, y_second, gains, grad_up, grad_attn = last_attn(
             (x, q, kv, lse, mixed, d_qkv, d_resid),
             spots[1],
@@ -2642,8 +2697,9 @@
             y,
             y_back,
             normed_one,
+            back_known,
             held[groups * spare :],
-            gains,
+            (gain_one, gain_two, gain_last),
             (spread_q, spread_k, spread_v, spread_o),
             (grad_up,),
             weights,
@@ -2655,6 +2711,7 @@
         live = (jnp.arange(seq_len)[None, :] < lens[:, me][:, None]).astype(jnp.int32).reshape(-1, 1)
         acts, backs, *grads = finish(
             live,
+            gains,
             inputs,
             y,
             (y_first, y_second),
@@ -2668,7 +2725,7 @@
             groups,
         )
         grads[1:3] = [jnp.swapaxes(item, 1, 2) for item in grads[1:3]]
-        return (acts, backs, gains[:1], *grads[:4], gains[1:2], *grads[4:])
+        return (acts, backs, grads[7], *grads[:4], grads[8], *grads[4:7])
 
     else:
         arriving = empty

time: 590 us -> 586 us (level)
  no operation moved by 1% of the time
where the time goes in v7:
time: 586 us
  Pallas kernels  542 us (92%)
  between operations  14.7 us (3%)
  other arithmetic  14.6 us (2%)
  local copies, waits for them, and re-layouts  7.69 us (1%)
  matrix products  6.76 us (1%)
    pallas_call x1, Pallas kernels, main_ticks(): pl.pallas_call(functools.partial(main_kernel, groups, q_heads, k_heads, p...  379 us
    pallas_call x1, Pallas kernels, last_attn(): pl.pallas_call(functools.partial(last_attn_kernel, groups, q_heads, k_hea...  87.5 us
    pallas_call x1, Pallas kernels, last_ffn(): pl.pallas_call(functools.partial(last_ffn_kernel, groups, pieces, chunks)...  57.4 us
    pallas_call x1, Pallas kernels, finish(): pl.pallas_call(functools.partial(finish_kernel, groups, parts), out_shape...  12.6 us
  transfers between devices with their start and end apart: 1, of which 0 were waited for; matrix products, arithmetic and copies ran while one was open for 4% of the time, Pallas kernels for 1%

profile of v7, /device:TPU:0, one launch (start us, length us, event | category | flops | bytes accessed | tf_op | source)
XLA Modules:
  0.0 586.0 jit_solution(9356568269899504857)
XLA Ops:
  7.3 2.8 select_bitcast_fusion
  10.2 5.4 gather_4.1
  18.5 0.5 fusion.10
  20.9 0.9 pad_maximum_fusion.2.refs_0_
  21.7 0.8 pad_maximum_fusion.3.refs_1_
  22.5 0.8 copy.76.refs_3_
  23.3 0.6 copy.74.refs_4_
  24.2 0.9 copy.73.refs_3_
  25.5 0.9 slice.69.refs_7_
  26.4 1.1 copy.83
  27.4 0.8 pad_add_fusion.refs_2_
  28.6 1.1 add_convert_fusion.1.refs_8_
  29.8 0.8 fusion.17
  30.5 1.1 fusion.7
  32.1 1.9 fusion.2.refs_14_
  34.3 1.4 pad_maximum_fusion.1.refs_9_
  35.7 2.2 convolution_convert_fusion.refs_15_
  38.0 1.1 fusion.refs_12_
  39.1 1.1 copy-done.7
  40.2 1.9 pad_maximum_fusion.refs_16_
  42.1 379.3 %main_ticks.1 = (bf16[640,1536]{1,0:T(8,128)(2,1)}, bf16[640,1536]{1,0:T(8,128)(2,1)}, bf16[576,1536]{1,0:T(8,128)(2,1)}, bf16[640,1536]{1,0:T(8,128)(2,1)}, bf1...) custom-call(f32[640,128]{1,0:T(8,128)} %pad_maximum_fusion.2.refs_0_, ...), custom_call_target="tpu_custom_call" | custom-call | tf_op jit(solution)/shard_map/main_ticks/pallas_call | solution.py:1765
  421.4 57.4 %last_ffn.1 = (bf16[320,1536]{1,0:T(8,128)(2,1)}, f32[1,1536]{1,0:T(1,128)}, bf16[1536,1024]{1,0:T(8,128)(2,1)}, bf16[384,1024]{1,0:T(8,128)(2,1)}, bf16[384,102...) custom-call(f32[1,1536]{1,0:T(1,128)} %refs_0_.1, ...), custom_call_target="tpu_custom_call" | custom-call | tf_op jit(solution)/shard_map/last_ffn/pallas_call | solution.py:2050
  478.8 87.5 %last_attn.1 = (bf16[320,1536]{1,0:T(8,128)(2,1)}, bf16[192,1536]{1,0:T(8,128)(2,1)}, bf16[192,1536]{1,0:T(8,128)(2,1)}, f32[8,384]{1,0:T(8,128)}, bf16[384,1024]{1,0:T(8,128)(2,1)}, /*index=5*/bf16[384,1152]{1,0:T(8,128)(2,1)}) custom-call(f32[320,128]{1,0:T(8,128)} %copy-done.10, f32[320,128]{1,0:T(8,128)} %copy-done.9, s32[320,1]{1,0:T(8,128)} %copy-done.11, ...), custom_call_target="tpu_custom_call" | custom-call | tf_op jit(solution)/shard_map/last_attn/pallas_call | solution.py:2417
  566.3 12.6 %finish.1 = (bf16[1,2,1,512,1536]{4,3,2,1,0:T(8,128)(2,1)}, bf16[1,2,1,512,1536]{4,3,2,1,0:T(8,128)(2,1)}, f32[1,384,384]{2,1,0:T(8,128)}, f32[1,192,384]{2,1,0:...) custom-call(s32[1024,1]{1,0:T(8,128)} %bitcast.92, ...), custom_call_target="tpu_custom_call" | custom-call | tf_op jit(solution)/shard_map/finish/pallas_call | solution.py:2548
  (105 shorter events, 6.5 us)
Async XLA Ops:
  7.2 28.5 %copy-start = (bf16[1,384,1536]{2,1,0:T(8,128)(2,1)S(1)}, bf16[1,384,1536]{2,1,0:T(8,128)(2,1)}, u32[]{:S(2)}) copy-start(bf16[1,384,1536]{2,1,0:T(8,128)(2,1)} %param.21) | copy-start | bytes 3538948
  7.2 34.9 %all-gather.3.cloned.1.call-start = ((), (), s32[]{:S(2)}) async-start(), calls=%async_computation | async-start | bytes 2949120 | tf_op jit(solution)/shard_map/all_gather | solution.py:2629
  7.2 2.9 copy-start.15
  7.3 11.2 %copy-start.8 = (f32[512,256]{1,0:T(8,128)S(1)}, f32[512,256]{1,0:T(8,128)}, u32[]{:S(2)}) copy-start(f32[512,256]{1,0:T(8,128)} %constant.55.clone) | copy-start | bytes 1572868
  19.6 3.8 copy-start.9
  19.6 3.8 copy-start.10
  20.8 6.7 %copy-start.2 = (bf16[1536,320]{1,0:T(8,128)(2,1)}, bf16[1536,320]{1,0:T(8,128)(2,1)S(1)}, u32[]{:S(2)}) copy-start(bf16[1536,320]{1,0:T(8,128)(2,1)S(1)} %add_convert_fusion.refs_7_.refs_1_) | copy-start | bytes 2949124
  20.8 6.6 %copy-start.13 = (s32[1,1280]{1,0:T(1,128)}, s32[1,1280]{1,0:T(1,128)S(1)}, u32[]{:S(2)}) copy-start(s32[1,1280]{1,0:T(1,128)S(1)} %get-tuple-element.130.refs_4_) | copy-start | bytes 15364
  24.1 5.7 copy-start.11
  26.4 5.2 copy-start.12
  27.4 6.6 %copy-start.4 = (bf16[2,1,512,1536]{3,2,1,0:T(8,128)(2,1)S(1)}, bf16[2,1,512,1536]{3,2,1,0:T(8,128)(2,1)}, u32[]{:S(2)}) copy-start(bf16[2,1,512,1536]{3,2,1,0:T(8,128)(2,1)} %refs_2_.1) | copy-start | bytes 9437188
  29.8 4.3 copy-start.3
  32.1 6.9 %copy-start.5 = (bf16[1536,256]{1,0:T(8,128)(2,1)}, bf16[1536,256]{1,0:T(8,128)(2,1)S(1)}, u32[]{:S(2)}) copy-start(bf16[1536,256]{1,0:T(8,128)(2,1)S(1)} %fusion.1.refs_13_) | copy-start | bytes 2359300
  34.0 5.0 copy-start.6
  35.7 2.2 copy-start.14
  39.1 1.1 copy-start.7
  566.3 12.6 %copy-start.1 = (bf16[1,384,1536]{2,1,0:T(8,128)(2,1)S(1)}, bf16[1,384,1536]{2,1,0:T(8,128)(2,1)}, u32[]{:S(2)}) copy-start(bf16[1,384,1536]{2,1,0:T(8,128)(2,1)} %param.21) | copy-start | bytes 3538948
Sparse Core Ops, SparseCore 0:
  10.3 26.8 all-gather.2

commit v8 on v7

--- a/solution.py
+++ b/solution.py
@@ -927,7 +927,7 @@
         share, own = take(2)
         shares.append(share)
         owns.append(own)
-        scatters.append(Scatter(groups, count, 5, [share, own] + take(4 * levels - 1)))
+        scatters.append(Scatter(groups, count, 2, [share, own] + take(4 * levels - 1)))
     tasks = [
         Scatter(groups, rows, chunks, [value, total] + take(4 * levels - 1))
         for (rows, chunks), value, total in zip(plans, values, totals)
@@ -1060,7 +1060,7 @@
     ]
     for _ in range(k_heads):
         scratch += [pltpu.VMEM((keys, 2 * LANES), BF16), pltpu.VMEM((count, 2 * LANES), F32)]
-        scratch += Scatter.scratch(groups, count, 2 * LANES, 5, BF16)
+        scratch += Scatter.scratch(groups, count, 2 * LANES, 2, BF16)
     plans = []
     for value in sums:
         rows = value.shape[0] // groups
@@ -1136,7 +1136,7 @@
         share, own = take(2)
         shares.append(share)
         owns.append(own)
-        scatters.append(Scatter(groups, count, 5, [share, own] + take(4 * levels - 1)))
+        scatters.append(Scatter(groups, count, 2, [share, own] + take(4 * levels - 1)))
     section = lax.axis_index("section")
     t = lax.axis_index("tensor")
     tiles, wide = gate.shape[1] // WIDE, width // WIDE
@@ -1761,7 +1761,7 @@
     scratch += Gather.scratch(groups)
     for _ in range(k_heads):
         scratch += [pltpu.VMEM((keys, 2 * LANES), BF16), pltpu.VMEM((count, 2 * LANES), F32)]
-        scratch += Scatter.scratch(groups, count, 2 * LANES, 5, BF16)
+        scratch += Scatter.scratch(groups, count, 2 * LANES, 2, BF16)
     return pl.pallas_call(
         functools.partial(main_kernel, groups, q_heads, k_heads, pieces),
         out_shape=outs,

time: 586 us -> 582 us (level)
  no operation moved by 1% of the time
where the time goes in v8:
time: 582 us
  Pallas kernels  538 us (92%)
  between operations  14.7 us (3%)
  other arithmetic  14.6 us (3%)
  local copies, waits for them, and re-layouts  7.69 us (1%)
  matrix products  6.76 us (1%)
    pallas_call x1, Pallas kernels, main_ticks(): pl.pallas_call(functools.partial(main_kernel, groups, q_heads, k_heads, p...  377 us
    pallas_call x1, Pallas kernels, last_attn(): pl.pallas_call(functools.partial(last_attn_kernel, groups, q_heads, k_hea...  86.1 us
    pallas_call x1, Pallas kernels, last_ffn(): pl.pallas_call(functools.partial(last_ffn_kernel, groups, pieces, chunks)...  56.7 us
    pallas_call x1, Pallas kernels, finish(): pl.pallas_call(functools.partial(finish_kernel, groups, parts), out_shape...  12.6 us
  transfers between devices with their start and end apart: 1, of which 0 were waited for; matrix products, arithmetic and copies ran while one was open for 4% of the time, Pallas kernels for 1%

profile of v8, /device:TPU:0, one launch (start us, length us, event | category | flops | bytes accessed | tf_op | source)
XLA Modules:
  0.0 581.7 jit_solution(5355664027368650096)
XLA Ops:
  7.3 2.8 select_bitcast_fusion
  10.2 5.4 gather_4.1
  18.5 0.5 fusion.10
  20.9 0.9 pad_maximum_fusion.2.refs_0_
  21.7 0.8 pad_maximum_fusion.3.refs_1_
  22.5 0.8 copy.76.refs_3_
  23.3 0.6 copy.74.refs_4_
  24.2 0.9 copy.73.refs_3_
  25.5 0.9 slice.69.refs_7_
  26.4 1.1 copy.83
  27.4 0.8 pad_add_fusion.refs_2_
  28.6 1.1 add_convert_fusion.1.refs_8_
  29.8 0.8 fusion.17
  30.5 1.1 fusion.7
  32.1 1.9 fusion.2.refs_14_
  34.3 1.4 pad_maximum_fusion.1.refs_9_
  35.7 2.2 convolution_convert_fusion.refs_15_
  38.0 1.1 fusion.refs_12_
  39.1 1.1 copy-done.7
  40.2 1.9 pad_maximum_fusion.refs_16_
  42.1 377.1 %main_ticks.1 = (bf16[640,1536]{1,0:T(8,128)(2,1)}, bf16[640,1536]{1,0:T(8,128)(2,1)}, bf16[576,1536]{1,0:T(8,128)(2,1)}, bf16[640,1536]{1,0:T(8,128)(2,1)}, bf1...) custom-call(f32[640,128]{1,0:T(8,128)} %pad_maximum_fusion.2.refs_0_, ...), custom_call_target="tpu_custom_call" | custom-call | tf_op jit(solution)/shard_map/main_ticks/pallas_call | solution.py:1765
  419.2 56.7 %last_ffn.1 = (bf16[320,1536]{1,0:T(8,128)(2,1)}, f32[1,1536]{1,0:T(1,128)}, bf16[1536,1024]{1,0:T(8,128)(2,1)}, bf16[384,1024]{1,0:T(8,128)(2,1)}, bf16[384,102...) custom-call(f32[1,1536]{1,0:T(1,128)} %refs_0_.1, ...), custom_call_target="tpu_custom_call" | custom-call | tf_op jit(solution)/shard_map/last_ffn/pallas_call | solution.py:2050
  475.9 86.1 %last_attn.1 = (bf16[320,1536]{1,0:T(8,128)(2,1)}, bf16[192,1536]{1,0:T(8,128)(2,1)}, bf16[192,1536]{1,0:T(8,128)(2,1)}, f32[8,384]{1,0:T(8,128)}, bf16[384,1024]{1,0:T(8,128)(2,1)}, /*index=5*/bf16[384,1152]{1,0:T(8,128)(2,1)}) custom-call(f32[320,128]{1,0:T(8,128)} %copy-done.10, f32[320,128]{1,0:T(8,128)} %copy-done.9, s32[320,1]{1,0:T(8,128)} %copy-done.11, ...), custom_call_target="tpu_custom_call" | custom-call | tf_op jit(solution)/shard_map/last_attn/pallas_call | solution.py:2417
  562.1 12.6 %finish.1 = (bf16[1,2,1,512,1536]{4,3,2,1,0:T(8,128)(2,1)}, bf16[1,2,1,512,1536]{4,3,2,1,0:T(8,128)(2,1)}, f32[1,384,384]{2,1,0:T(8,128)}, f32[1,192,384]{2,1,0:...) custom-call(s32[1024,1]{1,0:T(8,128)} %bitcast.92, ...), custom_call_target="tpu_custom_call" | custom-call | tf_op jit(solution)/shard_map/finish/pallas_call | solution.py:2548
  (105 shorter events, 6.5 us)
Async XLA Ops:
  7.2 28.5 %copy-start = (bf16[1,384,1536]{2,1,0:T(8,128)(2,1)S(1)}, bf16[1,384,1536]{2,1,0:T(8,128)(2,1)}, u32[]{:S(2)}) copy-start(bf16[1,384,1536]{2,1,0:T(8,128)(2,1)} %param.21) | copy-start | bytes 3538948
  7.2 34.9 %all-gather.3.cloned.1.call-start = ((), (), s32[]{:S(2)}) async-start(), calls=%async_computation | async-start | bytes 2949120 | tf_op jit(solution)/shard_map/all_gather | solution.py:2629
  7.2 2.9 copy-start.15
  7.3 11.2 %copy-start.8 = (f32[512,256]{1,0:T(8,128)S(1)}, f32[512,256]{1,0:T(8,128)}, u32[]{:S(2)}) copy-start(f32[512,256]{1,0:T(8,128)} %constant.55.clone) | copy-start | bytes 1572868
  19.6 3.8 copy-start.9
  19.6 3.8 copy-start.10
  20.8 6.7 %copy-start.2 = (bf16[1536,320]{1,0:T(8,128)(2,1)}, bf16[1536,320]{1,0:T(8,128)(2,1)S(1)}, u32[]{:S(2)}) copy-start(bf16[1536,320]{1,0:T(8,128)(2,1)S(1)} %add_convert_fusion.refs_7_.refs_1_) | copy-start | bytes 2949124
  20.8 6.6 %copy-start.13 = (s32[1,1280]{1,0:T(1,128)}, s32[1,1280]{1,0:T(1,128)S(1)}, u32[]{:S(2)}) copy-start(s32[1,1280]{1,0:T(1,128)S(1)} %get-tuple-element.130.refs_4_) | copy-start | bytes 15364
  24.1 5.7 copy-start.11
  26.4 5.2 copy-start.12
  27.4 6.6 %copy-start.4 = (bf16[2,1,512,1536]{3,2,1,0:T(8,128)(2,1)S(1)}, bf16[2,1,512,1536]{3,2,1,0:T(8,128)(2,1)}, u32[]{:S(2)}) copy-start(bf16[2,1,512,1536]{3,2,1,0:T(8,128)(2,1)} %refs_2_.1) | copy-start | bytes 9437188
  29.8 4.3 copy-start.3
  32.1 6.9 %copy-start.5 = (bf16[1536,256]{1,0:T(8,128)(2,1)}, bf16[1536,256]{1,0:T(8,128)(2,1)S(1)}, u32[]{:S(2)}) copy-start(bf16[1536,256]{1,0:T(8,128)(2,1)S(1)} %fusion.1.refs_13_) | copy-start | bytes 2359300
  34.0 5.0 copy-start.6
  35.7 2.2 copy-start.14
  39.1 1.1 copy-start.7
  562.0 12.6 %copy-start.1 = (bf16[1,384,1536]{2,1,0:T(8,128)(2,1)S(1)}, bf16[1,384,1536]{2,1,0:T(8,128)(2,1)}, u32[]{:S(2)}) copy-start(bf16[1,384,1536]{2,1,0:T(8,128)(2,1)} %param.21) | copy-start | bytes 3538948
Sparse Core Ops, SparseCore 0:
  10.3 26.8 all-gather.2
